TPU v7x, 512 devices: a whole 4x8x8 slice. The times are simulated.
512 devices in a mesh: leaf: 128 (over y, z, core), gy: 4 (over x).
Axes of the slice: x: 4, y: 8, z: 8, core: 2. Of those that a mesh axis runs over, the one named last changes fastest.
Arguments:
- field_old: float32 [8, 64, 40960], P('gy', None, 'leaf'), may hold values from -1.2 to 1.2
- coef_old: float32 [64, 40960], P(None, 'leaf'), may hold values from 0.5 to 4
- owner: int32 [40960], P('leaf'), may hold values from 0 to 127, as said below
- counts: int32 [128], P('leaf'), may hold values from 192 to 320, as said below
- pattern: int32 [6, 32768], P(None, 'leaf'), may hold values from -1 to 543, as said below
Outputs:
- extension: float32 [8, 64, 32768], P('gy', None, 'leaf')
Inputs may be any that keep to these rules, and one draw needn't show every extreme that they name: `owner`: only live slots matter. The live slots of device d name, in slot order, first device d - 1, then d, then d + 1; at most 32 name d - 1 and at most 32 name d + 1, some device hands exactly 32 each way, and every device receives exactly 256 live bricks. Live slots are the first counts[d] slots of device d. `pattern`: -1 means no neighbour across that face; otherwise the index into the bricks of devices d - 1, d and d + 1 after the rebalance, laid end to end. A neighbour on device d - 1 is one of its last 32 bricks, one on device d + 1 one of its first 32 bricks.
All inputs are finite; a program needn't handle non-finite values.
Results may differ from a plain program's by a relative error of at most 0.00002.
Values sent between devices are 32-bit elements; how exact they have to be, the bound alone decides.
No kernel may reach another device: no remote copies, remote signals or barrier semaphores. Data moves between devices by JAX's collectives and lax.ppermute only.
A program may use at most 64 MiB of HBM per device.

v0:
```python
import jax
import jax.numpy as jnp
from jax import lax
from jax.sharding import PartitionSpec as P

BRICKS_DEV = 256
SPILL = 32
Y = 8
SWEEPS = 2
OLD_SLOTS = 320


EXPONENT = 0.5
HEIGHT = 8.0
OMEGA = 0.8


def from_behind(block, axis, distance):
    devices = range(lax.axis_size(axis))
    route = [(i - distance, i) for i in devices if i - distance in devices]
    return lax.ppermute(block, axis, route)


def padded(block, sides, width):
    for axis, dim in sides:
        count = lax.axis_size(axis)
        forward = [(i, i + 1) for i in range(count - 1)]
        backward = [(target, source) for source, target in forward]
        low = lax.ppermute(
            lax.slice_in_dim(block, block.shape[dim] - width, None, axis=dim), axis, forward
        )
        high = lax.ppermute(lax.slice_in_dim(block, 0, width, axis=dim), axis, backward)
        block = jnp.concatenate([low, block, high], axis=dim)
    return block


def layer_weights(levels):
    y_here = HEIGHT * (levels / float(Y)) ** 2
    y_next = HEIGHT * ((levels + 1.0) / float(Y)) ** 2
    y_prev = HEIGHT * ((levels - 1.0) / float(Y)) ** 2
    step_up = y_next - y_here
    step_down = y_here - y_prev
    up_weight = ((y_here + y_next) * 0.5) ** EXPONENT
    down_weight = ((y_here + y_prev) * 0.5) ** EXPONENT
    has_lower = (levels > 0.5).astype(levels.dtype)
    up_link = up_weight / step_up
    down_link = has_lower * down_weight / step_down
    planar = 0.5 * (up_weight * step_up + has_lower * down_weight * step_down)
    surface = (levels < 0.5).astype(levels.dtype)
    return (
        planar.reshape(-1, 1, 1),
        down_link.reshape(-1, 1, 1),
        up_link.reshape(-1, 1, 1),
        surface.reshape(-1, 1, 1),
    )


def far_faces(source, pattern_rows, valid_rows):
    picked = []
    for direction in range(6):
        axis_no = 1 + direction // 2
        layer_no = 3 if direction % 2 == 0 else 0
        face_cells = lax.index_in_dim(source, layer_no, axis_no, keepdims=False)
        gathered = jnp.take(face_cells, pattern_rows[direction], axis=3) * valid_rows[direction]
        picked.append(gathered)
    return picked


def shifted_sum(cube_now, face_list):
    running_sum = jnp.concatenate([face_list[0][:, None], cube_now[:, :3]], axis=1)
    running_sum = running_sum + jnp.concatenate([cube_now[:, 1:], face_list[1][:, None]], axis=1)
    running_sum = running_sum + jnp.concatenate(
        [face_list[2][:, :, None], cube_now[:, :, :3]], axis=2
    )
    running_sum = running_sum + jnp.concatenate(
        [cube_now[:, :, 1:], face_list[3][:, :, None]], axis=2
    )
    running_sum = running_sum + jnp.concatenate(
        [face_list[4][:, :, :, None], cube_now[:, :, :, :3]], axis=3
    )
    running_sum = running_sum + jnp.concatenate(
        [cube_now[:, :, :, 1:], face_list[5][:, :, :, None]], axis=3
    )
    return running_sum


def relax(current, beneath, overhead, neighbour_sum, coef_cells, source_term, weights):
    planar, down_link, up_link, surface = weights
    applied = (
        planar * coef_cells * (6.0 * current - neighbour_sum)
        + (down_link + up_link + surface) * current
        - down_link * beneath
        - up_link * overhead
    )
    diagonal = 6.0 * planar * coef_cells + down_link + up_link + surface
    return current + OMEGA * (source_term - applied) / diagonal


def local(field_old, coef_old, owner, counts, pattern):
    layers = field_old.shape[0]
    bricks = pattern.shape[1]
    device = lax.axis_index("leaf")
    live_count = counts[0]
    slot_ids = jnp.arange(OLD_SLOTS, dtype=jnp.int32)
    is_live = slot_ids < live_count
    send_prev = jnp.sum((is_live & (owner == device - 1)).astype(jnp.int32))
    send_next = jnp.sum((is_live & (owner == device + 1)).astype(jnp.int32))
    stay_count = live_count - send_prev - send_next
    own_stack = jnp.concatenate([field_old, coef_old[None]], axis=0)
    bucket_ids = jnp.arange(SPILL, dtype=jnp.int32)
    prev_mask = (bucket_ids < send_prev).astype(jnp.float32)
    next_mask = (bucket_ids >= SPILL - send_next).astype(jnp.float32)
    to_prev = own_stack[:, :, :SPILL] * prev_mask
    next_start = live_count - SPILL
    to_next = lax.dynamic_slice_in_dim(own_stack, next_start, SPILL, 2) * next_mask
    from_prev = from_behind(to_next, "leaf", 1)
    from_next = from_behind(to_prev, "leaf", -1)
    arrive_prev = jnp.sum((from_prev[layers, 0, :] > 0).astype(jnp.int32))
    arrive_next = jnp.sum((from_next[layers, 0, :] > 0).astype(jnp.int32))
    virtual = jnp.concatenate([from_prev, own_stack, from_next], axis=2)
    new_ids = jnp.arange(BRICKS_DEV, dtype=jnp.int32)
    source_ids = jnp.where(
        new_ids < arrive_prev,
        SPILL - arrive_prev + new_ids,
        jnp.where(
            new_ids < arrive_prev + stay_count,
            SPILL + send_prev + new_ids - arrive_prev,
            SPILL + OLD_SLOTS + new_ids - arrive_prev - stay_count,
        ),
    )
    source_ids = jnp.clip(source_ids, 0, OLD_SLOTS + 2 * SPILL - 1)
    is_filled = (new_ids < arrive_prev + stay_count + arrive_next).astype(jnp.float32)
    placed = jnp.take(virtual, source_ids, axis=2) * is_filled
    field_new = placed[:layers]
    coef_new = placed[layers]
    levels = (lax.axis_index("gy") * layers + jnp.arange(layers, dtype=jnp.int32)).astype(
        jnp.float32
    )
    weights = layer_weights(levels)
    is_valid = pattern >= 0
    valid_rows = is_valid.astype(jnp.float32)
    window_rows = jnp.clip(pattern, 0, 3 * bricks - 1)
    window_width = 3 * bricks
    phase_field = field_new[0:1]
    source_term = weights[3] * (2.0 * phase_field - phase_field * phase_field * phase_field)
    current = field_new
    for sweep_no in range(SWEEPS):
        extended = padded(current, (("leaf", 2),), bricks)
        stacked = padded(current, (("gy", 0),), 1)
        beneath = stacked[:-2]
        overhead = stacked[2:]
        cube_wide = extended.reshape(layers, 4, 4, 4, window_width)
        face_list = far_faces(cube_wide, window_rows, valid_rows)
        cube_now = current.reshape(layers, 4, 4, 4, bricks)
        neighbour_sum = shifted_sum(cube_now, face_list).reshape(layers, 64, bricks)
        current = relax(current, beneath, overhead, neighbour_sum, coef_new, source_term, weights)
    return current


def solution(mesh):
    return jax.shard_map(
        local,
        mesh=mesh,
        in_specs=(P("gy", None, "leaf"), P(None, "leaf"), P("leaf"), P("leaf"), P(None, "leaf")),
        out_specs=P("gy", None, "leaf"),
        check_vma=False,
    )
```

profile of v0, /device:TPU:38, one launch (start us, length us, event | category | flops | bytes accessed | tf_op | source)
XLA Modules:
  0.0 178.1 jit_solution(9492368146923004021)
XLA Ops:
  0.7 1.3 convert_reduce_fusion.1
  3.2 1.0 fusion.37
  4.3 1.9 %collective-permute-start = (f32[3,64,32]{2,1,0:T(8,128)S(1)}, f32[3,64,32]{2,1,0:T(8,128)S(1)}, u32[]{:S(2)}, u32[]{:S(2)}) collective-permute-start(f32[3,64,32]{2,1,0:T(8,128)S(1)} %get-tuple-element.20), channel_id=1, source_target_pairs={{0,4},{4,8},{8,12},{12,16},{16,20},{20,24},{24,28},{28,32},{32,36}... | collective-permute-start | bytes 73736 | tf_op jit(solution)/shard_map/ppermute | solution.py:21
  6.2 10.3 %collective-permute-start.1 = (f32[3,64,32]{2,1,0:T(8,128)S(1)}, f32[3,64,32]{2,1,0:T(8,128)S(1)}, u32[]{:S(2)}, u32[]{:S(2)}) collective-permute-start(f32[3,64,32]{2,1,0:T(8,128)S(1)} %get-tuple-element.21), channel_id=1, source_target_pairs={{4,0},{8,4},{12,8},{16,12},{20,16},{24,20},{28,24},{32,28},{36,32}... | collective-permute-start | bytes 73736 | tf_op jit(solution)/shard_map/ppermute | solution.py:21
  31.6 1.1 pad_maximum_fusion.2
  33.1 1.0 gather_fusion
  35.6 1.9 %collective-permute-start.2 = (f32[2,64,256]{2,1,0:T(8,128)S(1)}, f32[2,64,256]{2,1,0:T(8,128)S(1)}, u32[]{:S(2)}, u32[]{:S(2)}) collective-permute-start(f32[2,64,256]{2,1,0:T(8,128)S(1)} %slice.243), channel_id=1, source_target_pairs={{0,4},{4,8},{8,12},{12,16},{16,20},{20,24},{24,28},{28,32},{32,36}... | collective-permute-start | bytes 393224 | tf_op jit(solution)/shard_map/ppermute | solution.py:29
  37.5 7.0 %collective-permute-start.3 = (f32[2,64,256]{2,1,0:T(8,128)S(1)}, f32[2,64,256]{2,1,0:T(8,128)S(1)}, u32[]{:S(2)}, u32[]{:S(2)}) collective-permute-start(f32[2,64,256]{2,1,0:T(8,128)S(1)} %slice.243), channel_id=1, source_target_pairs={{4,0},{8,4},{12,8},{16,12},{20,16},{24,20},{28,24},{32,28},{36,32}... | collective-permute-start | bytes 393224 | tf_op jit(solution)/shard_map/ppermute | solution.py:32
  44.6 0.7 fusion.61
  45.4 0.7 fusion.62
  46.8 1.3 collective-permute-start.4
  48.0 5.2 %collective-permute-start.5 = (f32[1,64,256]{2,1,0:T(8,128)}, f32[1,64,256]{2,1,0:T(8,128)}, u32[]{:S(2)}, u32[]{:S(2)}) collective-permute-start(f32[1,64,256]{2,1,0:T(8,128)} %get-tuple-element.25), channel_id=1, source_target_pairs={{1,0},{2,1},{3,2},{5,4},{6,5},{7,6},{9,8},{10,9},{11,10},{13,12},{... | collective-permute-start | bytes 196616 | tf_op jit(solution)/shard_map/ppermute | solution.py:32
  56.4 2.3 %copy.153 = f32[2,1,4,4,768]{3,2,4,0,1:T(4,128)S(1)} copy(f32[2,1,4,4,768]{4,0,3,2,1:T(2,128)} %get-tuple-element.18) | data formatting | bytes 196608
  58.7 2.3 %gather_fusion.2 = f32[256,2,4,4]{3,2,1,0:T(4,128)} fusion(f32[2,4,4,768]{2,1,3,0:T(4,128)S(1)} %bitcast.127, s32[1024]{0:T(1024)S(1)} %pad_clamp_fusion.4), kind=kCustom, calls=%fused_computation.1.clone | custom fusion | bytes 66560 | tf_op jit(solution)/shard_map/jit(_take)/gather | solution.py:64
  61.0 2.6 %fusion.10 = f32[2,1,4,4,256]{3,2,0,4,1:T(4,128)S(1)} fusion(f32[256,2,4,4]{3,2,1,0:T(4,128)} %gather_fusion.2, f32[256]{0:T(256)S(1)} %bitcast.153, pred[256]{0:T(512)(128)(4,1)S(1)} %compare_and_fusion.4), kind=kLoop, calls=%fused_computation.34 | loop fusion | flops 16384 | bytes 66816 | tf_op jit(solution)/shard_map/broadcast_in_dim | solution.py:71
  64.1 2.4 %copy.154 = f32[2,4,1,4,768]{3,1,4,0,2:T(4,128)S(1)} copy(f32[2,4,1,4,768]{4,0,3,2,1:T(2,128)} %get-tuple-element.17) | data formatting | bytes 196608
  66.5 2.4 %gather_fusion.3 = f32[256,2,4,4]{3,2,1,0:T(4,128)} fusion(f32[2,4,4,768]{2,1,3,0:T(4,128)S(1)} %bitcast.128, s32[1024]{0:T(1024)} %pad_clamp_fusion.3), kind=kCustom, calls=%fused_computation.2.clone | custom fusion | bytes 66560 | tf_op jit(solution)/shard_map/jit(_take)/gather | solution.py:64
  68.9 2.4 %fusion.9 = f32[2,4,1,4,256]{3,1,0,4,2:T(4,128)S(1)} fusion(f32[256,2,4,4]{3,2,1,0:T(4,128)} %gather_fusion.3, f32[256]{0:T(256)} %bitcast.151, pred[256]{0:T(512)(128)(4,1)} %compare_and_fusion.3), kind=kLoop, calls=%fused_computation.32 | loop fusion | flops 16384 | bytes 66816 | tf_op jit(solution)/shard_map/broadcast_in_dim | solution.py:73
  71.3 1.1 copy.129
  72.5 2.3 %copy.155 = f32[2,4,1,4,768]{3,1,4,0,2:T(4,128)S(1)} copy(f32[2,4,1,4,768]{4,0,3,2,1:T(2,128)} %get-tuple-element.16) | data formatting | bytes 196608
  74.8 2.4 %gather_fusion.4 = f32[256,2,4,4]{3,2,1,0:T(4,128)} fusion(f32[2,4,4,768]{2,1,3,0:T(4,128)S(1)} %bitcast.129, s32[1024]{0:T(1024)} %pad_clamp_fusion.2), kind=kCustom, calls=%fused_computation.3.clone | custom fusion | bytes 66560 | tf_op jit(solution)/shard_map/jit(_take)/gather | solution.py:64
  77.3 2.5 %fusion.8 = f32[2,4,1,4,256]{3,1,0,4,2:T(4,128)S(1)} fusion(f32[256,2,4,4]{3,2,1,0:T(4,128)} %gather_fusion.4, f32[256]{0:T(256)S(1)} %bitcast.149, pred[256]{0:T(512)(128)(4,1)} %compare_and_fusion.2), kind=kLoop, calls=%fused_computation.30 | loop fusion | flops 16384 | bytes 66816 | tf_op jit(solution)/shard_map/broadcast_in_dim | solution.py:76
  79.8 1.1 copy.131
  80.9 2.3 %copy.156 = f32[2,4,4,1,768]{2,1,4,0,3:T(4,128)S(1)} copy(f32[2,4,4,1,768]{4,0,3,2,1:T(2,128)} %get-tuple-element.15) | data formatting | bytes 196608
  83.2 2.4 %gather_fusion.5 = f32[256,2,4,4]{3,2,1,0:T(4,128)} fusion(f32[2,4,4,768]{2,1,3,0:T(4,128)S(1)} %bitcast.130, s32[1024]{0:T(1024)} %pad_clamp_fusion.1), kind=kCustom, calls=%fused_computation.4.clone | custom fusion | bytes 66560 | tf_op jit(solution)/shard_map/jit(_take)/gather | solution.py:64
  85.7 2.5 %fusion.7 = f32[2,4,4,1,256]{2,1,0,4,3:T(4,128)S(1)} fusion(f32[256,2,4,4]{3,2,1,0:T(4,128)} %gather_fusion.5, f32[256]{0:T(256)S(1)} %bitcast.147, pred[256]{0:T(512)(128)(4,1)} %compare_and_fusion.1), kind=kLoop, calls=%fused_computation.28 | loop fusion | flops 16384 | bytes 66816 | tf_op jit(solution)/shard_map/broadcast_in_dim | solution.py:79
  88.2 1.1 copy.133
  89.3 2.3 %copy.157 = f32[2,4,4,1,768]{2,1,4,0,3:T(4,128)S(1)} copy(f32[2,4,4,1,768]{4,0,3,2,1:T(2,128)} %get-tuple-element.14) | data formatting | bytes 196608
  91.6 2.4 %gather_fusion.6 = f32[256,2,4,4]{3,2,1,0:T(4,128)} fusion(f32[2,4,4,768]{2,1,3,0:T(4,128)S(1)} %bitcast.131, s32[1024]{0:T(1024)} %pad_clamp_fusion), kind=kCustom, calls=%fused_computation.5.clone | custom fusion | bytes 66560 | tf_op jit(solution)/shard_map/jit(_take)/gather | solution.py:64
  94.1 2.5 %fusion.6 = f32[2,4,4,1,256]{2,1,0,4,3:T(4,128)S(1)} fusion(f32[256,2,4,4]{3,2,1,0:T(4,128)} %gather_fusion.6, f32[256]{0:T(256)S(1)} %bitcast.145, pred[256]{0:T(512)(128)(4,1)} %compare_and_fusion), kind=kLoop, calls=%fused_computation.26 | loop fusion | flops 16384 | bytes 66816 | tf_op jit(solution)/shard_map/broadcast_in_dim | solution.py:82
  96.6 1.1 copy.135
  97.7 1.5 copy.152
  99.2 2.6 %gather_fusion.1 = f32[256,2,4,4]{3,2,1,0:T(4,128)} fusion(f32[2,4,4,768]{2,1,3,0:T(4,128)S(1)} %bitcast.132, s32[1024]{0:T(1024)} %pad_clamp_fusion.5), kind=kCustom, calls=%fused_computation.clone | custom fusion | bytes 66560 | tf_op jit(solution)/shard_map/jit(_take)/gather | solution.py:64
  101.9 2.6 %fusion.11 = f32[2,1,4,4,256]{3,2,0,4,1:T(4,128)S(1)} fusion(f32[256,2,4,4]{3,2,1,0:T(4,128)} %gather_fusion.1, f32[256]{0:T(256)S(1)} %bitcast.143, pred[256]{0:T(512)(128)(4,1)} %compare_and_fusion.5), kind=kLoop, calls=%fused_computation.36 | loop fusion | flops 16384 | bytes 66816 | tf_op jit(solution)/shard_map/broadcast_in_dim | solution.py:70
  105.3 1.1 fusion.14
  106.4 1.9 %collective-permute-start.6 = (f32[2,64,256]{2,1,0:T(8,128)S(1)}, f32[2,64,256]{2,1,0:T(8,128)S(1)}, u32[]{:S(2)}, u32[]{:S(2)}) collective-permute-start(f32[2,64,256]{2,1,0:T(8,128)S(1)} %fusion.14), channel_id=1, source_target_pairs={{0,4},{4,8},{8,12},{12,16},{16,20},{20,24},{24,28},{28,32},{32,36}... | collective-permute-start | bytes 393224 | tf_op jit(solution)/shard_map/ppermute | solution.py:29
  108.3 7.0 %collective-permute-start.7 = (f32[2,64,256]{2,1,0:T(8,128)S(1)}, f32[2,64,256]{2,1,0:T(8,128)S(1)}, u32[]{:S(2)}, u32[]{:S(2)}) collective-permute-start(f32[2,64,256]{2,1,0:T(8,128)S(1)} %fusion.14), channel_id=1, source_target_pairs={{4,0},{8,4},{12,8},{16,12},{20,16},{24,20},{28,24},{32,28},{36,32}... | collective-permute-start | bytes 393224 | tf_op jit(solution)/shard_map/ppermute | solution.py:32
  115.4 0.7 fusion.57
  116.2 0.7 fusion.58
  117.5 1.3 collective-permute-start.8
  118.8 5.2 %collective-permute-start.9 = (f32[1,64,256]{2,1,0:T(8,128)}, f32[1,64,256]{2,1,0:T(8,128)}, u32[]{:S(2)}, u32[]{:S(2)}) collective-permute-start(f32[1,64,256]{2,1,0:T(8,128)} %get-tuple-element.33), channel_id=1, source_target_pairs={{1,0},{2,1},{3,2},{5,4},{6,5},{7,6},{9,8},{10,9},{11,10},{13,12},{... | collective-permute-start | bytes 196616 | tf_op jit(solution)/shard_map/ppermute | solution.py:32
  127.2 2.3 %copy.159 = f32[2,1,4,4,768]{3,2,4,0,1:T(4,128)S(1)} copy(f32[2,1,4,4,768]{4,0,3,2,1:T(2,128)} %get-tuple-element.12) | data formatting | bytes 196608
  129.5 2.4 %gather_fusion.8 = f32[256,2,4,4]{3,2,1,0:T(4,128)} fusion(f32[2,4,4,768]{2,1,3,0:T(4,128)S(1)} %bitcast.121, s32[1024]{0:T(1024)} %copy-done.22), kind=kCustom, calls=%fused_computation.7.clone | custom fusion | bytes 66560 | tf_op jit(solution)/shard_map/jit(_take)/gather | solution.py:64
  132.0 2.6 %fusion.4 = f32[2,1,4,4,256]{3,2,0,4,1:T(4,128)S(1)} fusion(f32[256,2,4,4]{3,2,1,0:T(4,128)} %gather_fusion.8, f32[256]{0:T(256)S(1)} %bitcast.154, pred[256]{0:T(512)(128)(4,1)S(1)} %copy-done.28), kind=kLoop, calls=%fused_computation.22 | loop fusion | flops 16384 | bytes 66816 | tf_op jit(solution)/shard_map/broadcast_in_dim | solution.py:71
  135.0 2.4 %copy.160 = f32[2,4,1,4,768]{3,1,4,0,2:T(4,128)S(1)} copy(f32[2,4,1,4,768]{4,0,3,2,1:T(2,128)} %get-tuple-element.11) | data formatting | bytes 196608
  137.4 2.4 %gather_fusion.9 = f32[256,2,4,4]{3,2,1,0:T(4,128)} fusion(f32[2,4,4,768]{2,1,3,0:T(4,128)S(1)} %bitcast.122, s32[1024]{0:T(1024)} %pad_clamp_fusion.3), kind=kCustom, calls=%fused_computation.8.clone | custom fusion | bytes 66560 | tf_op jit(solution)/shard_map/jit(_take)/gather | solution.py:64
  139.8 2.4 %fusion.3 = f32[2,4,1,4,256]{3,1,0,4,2:T(4,128)S(1)} fusion(f32[256,2,4,4]{3,2,1,0:T(4,128)} %gather_fusion.9, f32[256]{0:T(256)} %bitcast.152, pred[256]{0:T(512)(128)(4,1)} %compare_and_fusion.3), kind=kLoop, calls=%fused_computation.20 | loop fusion | flops 16384 | bytes 66816 | tf_op jit(solution)/shard_map/broadcast_in_dim | solution.py:73
  142.3 1.1 copy.144
  143.4 2.3 %copy.161 = f32[2,4,1,4,768]{3,1,4,0,2:T(4,128)S(1)} copy(f32[2,4,1,4,768]{4,0,3,2,1:T(2,128)} %get-tuple-element.10) | data formatting | bytes 196608
  145.7 2.4 %gather_fusion.10 = f32[256,2,4,4]{3,2,1,0:T(4,128)} fusion(f32[2,4,4,768]{2,1,3,0:T(4,128)S(1)} %bitcast.123, s32[1024]{0:T(1024)} %pad_clamp_fusion.2), kind=kCustom, calls=%fused_computation.9.clone | custom fusion | bytes 66560 | tf_op jit(solution)/shard_map/jit(_take)/gather | solution.py:64
  148.2 2.5 %fusion.2 = f32[2,4,1,4,256]{3,1,0,4,2:T(4,128)S(1)} fusion(f32[256,2,4,4]{3,2,1,0:T(4,128)} %gather_fusion.10, f32[256]{0:T(256)S(1)} %bitcast.150, pred[256]{0:T(512)(128)(4,1)} %compare_and_fusion.2), kind=kLoop, calls=%fused_computation.18 | loop fusion | flops 16384 | bytes 66816 | tf_op jit(solution)/shard_map/broadcast_in_dim | solution.py:76
  150.7 1.1 copy.146
  151.8 2.3 %copy.162 = f32[2,4,4,1,768]{2,1,4,0,3:T(4,128)S(1)} copy(f32[2,4,4,1,768]{4,0,3,2,1:T(2,128)} %get-tuple-element.9) | data formatting | bytes 196608
  154.1 2.4 %gather_fusion.11 = f32[256,2,4,4]{3,2,1,0:T(4,128)} fusion(f32[2,4,4,768]{2,1,3,0:T(4,128)S(1)} %bitcast.124, s32[1024]{0:T(1024)} %pad_clamp_fusion.1), kind=kCustom, calls=%fused_computation.10.clone | custom fusion | bytes 66560 | tf_op jit(solution)/shard_map/jit(_take)/gather | solution.py:64
  156.6 2.5 %fusion.1 = f32[2,4,4,1,256]{2,1,0,4,3:T(4,128)S(1)} fusion(f32[256,2,4,4]{3,2,1,0:T(4,128)} %gather_fusion.11, f32[256]{0:T(256)S(1)} %bitcast.148, pred[256]{0:T(512)(128)(4,1)} %compare_and_fusion.1), kind=kLoop, calls=%fused_computation.16 | loop fusion | flops 16384 | bytes 66816 | tf_op jit(solution)/shard_map/broadcast_in_dim | solution.py:79
  159.1 1.1 copy.148
  160.2 2.3 %copy.163 = f32[2,4,4,1,768]{2,1,4,0,3:T(4,128)S(1)} copy(f32[2,4,4,1,768]{4,0,3,2,1:T(2,128)} %get-tuple-element.8) | data formatting | bytes 196608
  162.6 2.4 %gather_fusion.12 = f32[256,2,4,4]{3,2,1,0:T(4,128)} fusion(f32[2,4,4,768]{2,1,3,0:T(4,128)S(1)} %bitcast.125, s32[1024]{0:T(1024)} %pad_clamp_fusion), kind=kCustom, calls=%fused_computation.11.clone | custom fusion | bytes 66560 | tf_op jit(solution)/shard_map/jit(_take)/gather | solution.py:64
  165.0 2.6 %fusion = f32[2,4,4,1,256]{2,1,0,4,3:T(4,128)S(1)} fusion(f32[256,2,4,4]{3,2,1,0:T(4,128)} %gather_fusion.12, f32[256]{0:T(256)S(1)} %bitcast.146, pred[256]{0:T(512)(128)(4,1)S(1)} %copy-done.26), kind=kLoop, calls=%fused_computation.14 | loop fusion | flops 16384 | bytes 66816 | tf_op jit(solution)/shard_map/broadcast_in_dim | solution.py:82
  167.6 1.1 copy.150
  168.7 1.6 copy.158
  170.3 2.6 %gather_fusion.7 = f32[256,2,4,4]{3,2,1,0:T(4,128)} fusion(f32[2,4,4,768]{2,1,3,0:T(4,128)S(1)} %bitcast.126, s32[1024]{0:T(1024)} %pad_clamp_fusion.5), kind=kCustom, calls=%fused_computation.6.clone | custom fusion | bytes 66560 | tf_op jit(solution)/shard_map/jit(_take)/gather | solution.py:64
  172.9 2.6 %fusion.5 = f32[2,1,4,4,256]{3,2,0,4,1:T(4,128)S(1)} fusion(f32[256,2,4,4]{3,2,1,0:T(4,128)} %gather_fusion.7, f32[256]{0:T(256)S(1)} %bitcast.144, pred[256]{0:T(512)(128)(4,1)} %compare_and_fusion.5), kind=kLoop, calls=%fused_computation.24 | loop fusion | flops 16384 | bytes 66816 | tf_op jit(solution)/shard_map/broadcast_in_dim | solution.py:70
  176.4 1.7 fusion.17
  (127 shorter events, 24.1 us)
Async XLA Ops:
  4.3 24.1 %collective-permute-start = (f32[3,64,32]{2,1,0:T(8,128)S(1)}, f32[3,64,32]{2,1,0:T(8,128)S(1)}, u32[]{:S(2)}, u32[]{:S(2)}) collective-permute-start(f32[3,64,32]{2,1,0:T(8,128)S(1)} %get-tuple-element.20), channel_id=1, source_target_pairs={{0,4},{4,8},{8,12},{12,16},{16,20},{20,24},{24,28},{28,32},{32,36}... | collective-permute-start | bytes 73736 | tf_op jit(solution)/shard_map/ppermute | solution.py:21
  6.2 25.4 %collective-permute-start.1 = (f32[3,64,32]{2,1,0:T(8,128)S(1)}, f32[3,64,32]{2,1,0:T(8,128)S(1)}, u32[]{:S(2)}, u32[]{:S(2)}) collective-permute-start(f32[3,64,32]{2,1,0:T(8,128)S(1)} %get-tuple-element.21), channel_id=1, source_target_pairs={{4,0},{8,4},{12,8},{16,12},{20,16},{24,20},{28,24},{32,28},{36,32}... | collective-permute-start | bytes 73736 | tf_op jit(solution)/shard_map/ppermute | solution.py:21
  17.2 43.8 %copy-start.27 = (pred[256]{0:T(512)(128)(4,1)}, pred[256]{0:T(512)(128)(4,1)S(1)}, u32[]{:S(2)}) copy-start(pred[256]{0:T(512)(128)(4,1)S(1)} %compare_and_fusion.4) | copy-start | bytes 772
  22.4 36.3 %copy-start.22 = (s32[1024]{0:T(1024)}, s32[1024]{0:T(1024)S(1)}, u32[]{:S(2)}) copy-start(s32[1024]{0:T(1024)S(1)} %pad_clamp_fusion.4) | copy-start | bytes 12292
  23.0 38.0 %copy-start.20 = (f32[1,256]{1,0:T(1,128)}, f32[1,256]{1,0:T(1,128)S(1)}, u32[]{:S(2)}) copy-start(f32[1,256]{1,0:T(1,128)S(1)} %get-tuple-element.44) | copy-start | bytes 3076
  35.6 18.3 %collective-permute-start.2 = (f32[2,64,256]{2,1,0:T(8,128)S(1)}, f32[2,64,256]{2,1,0:T(8,128)S(1)}, u32[]{:S(2)}, u32[]{:S(2)}) collective-permute-start(f32[2,64,256]{2,1,0:T(8,128)S(1)} %slice.243), channel_id=1, source_target_pairs={{0,4},{4,8},{8,12},{12,16},{16,20},{20,24},{24,28},{28,32},{32,36}... | collective-permute-start | bytes 393224 | tf_op jit(solution)/shard_map/ppermute | solution.py:29
  37.5 16.4 %collective-permute-start.3 = (f32[2,64,256]{2,1,0:T(8,128)S(1)}, f32[2,64,256]{2,1,0:T(8,128)S(1)}, u32[]{:S(2)}, u32[]{:S(2)}) collective-permute-start(f32[2,64,256]{2,1,0:T(8,128)S(1)} %slice.243), channel_id=1, source_target_pairs={{4,0},{8,4},{12,8},{16,12},{20,16},{24,20},{28,24},{32,28},{36,32}... | collective-permute-start | bytes 393224 | tf_op jit(solution)/shard_map/ppermute | solution.py:32
  46.8 58.6 %collective-permute-start.4 = (f32[1,64,256]{2,1,0:T(8,128)}, f32[1,64,256]{2,1,0:T(8,128)}, u32[]{:S(2)}, u32[]{:S(2)}) collective-permute-start(f32[1,64,256]{2,1,0:T(8,128)} %get-tuple-element.23), channel_id=1, source_target_pairs={{0,1},{1,2},{2,3},{4,5},{5,6},{6,7},{8,9},{9,10},{10,11},{12,13},{... | collective-permute-start | bytes 196616 | tf_op jit(solution)/shard_map/ppermute | solution.py:29
  48.0 57.3 %collective-permute-start.5 = (f32[1,64,256]{2,1,0:T(8,128)}, f32[1,64,256]{2,1,0:T(8,128)}, u32[]{:S(2)}, u32[]{:S(2)}) collective-permute-start(f32[1,64,256]{2,1,0:T(8,128)} %get-tuple-element.25), channel_id=1, source_target_pairs={{1,0},{2,1},{3,2},{5,4},{6,5},{7,6},{9,8},{10,9},{11,10},{13,12},{... | collective-permute-start | bytes 196616 | tf_op jit(solution)/shard_map/ppermute | solution.py:32
  99.2 5.8 %copy-start.6 = (f32[2,4,4,3,256]{4,0,3,2,1:T(2,128)S(1)}, f32[2,4,4,3,256]{4,0,3,2,1:T(2,128)}, u32[]{:S(2)}) copy-start(f32[2,4,4,3,256]{4,0,3,2,1:T(2,128)} %get-tuple-element.34) | copy-start | bytes 294916
  101.8 3.2 %copy-start.7 = (f32[2,4,4,3,256]{4,0,3,2,1:T(2,128)S(1)}, f32[2,4,4,3,256]{4,0,3,2,1:T(2,128)}, u32[]{:S(2)}) copy-start(f32[2,4,4,3,256]{4,0,3,2,1:T(2,128)} %get-tuple-element.35) | copy-start | bytes 294916
  101.8 3.2 %copy-start.8 = (f32[2,4,3,4,256]{4,0,3,2,1:T(2,128)S(1)}, f32[2,4,3,4,256]{4,0,3,2,1:T(2,128)}, u32[]{:S(2)}) copy-start(f32[2,4,3,4,256]{4,0,3,2,1:T(2,128)} %get-tuple-element.36) | copy-start | bytes 294916
  101.8 3.2 %copy-start.9 = (f32[2,4,3,4,256]{4,0,3,2,1:T(2,128)S(1)}, f32[2,4,3,4,256]{4,0,3,2,1:T(2,128)}, u32[]{:S(2)}) copy-start(f32[2,4,3,4,256]{4,0,3,2,1:T(2,128)} %get-tuple-element.37) | copy-start | bytes 294916
  101.8 3.2 %copy-start.10 = (f32[2,3,4,4,256]{4,0,3,2,1:T(2,128)S(1)}, f32[2,3,4,4,256]{4,0,3,2,1:T(2,128)}, u32[]{:S(2)}) copy-start(f32[2,3,4,4,256]{4,0,3,2,1:T(2,128)} %get-tuple-element.38) | copy-start | bytes 294916
  101.8 3.2 %copy-start.11 = (f32[2,3,4,4,256]{4,0,3,2,1:T(2,128)S(1)}, f32[2,3,4,4,256]{4,0,3,2,1:T(2,128)}, u32[]{:S(2)}) copy-start(f32[2,3,4,4,256]{4,0,3,2,1:T(2,128)} %get-tuple-element.39) | copy-start | bytes 294916
  101.8 3.2 %copy-start.13 = (f32[2,4,1,4,256]{4,0,3,2,1:T(2,128)S(1)}, f32[2,4,1,4,256]{4,0,3,2,1:T(2,128)}, u32[]{:S(2)}) copy-start(f32[2,4,1,4,256]{4,0,3,2,1:T(2,128)} %copy.129) | copy-start | bytes 98308
  101.8 3.2 %copy-start.15 = (f32[2,4,1,4,256]{4,0,3,2,1:T(2,128)S(1)}, f32[2,4,1,4,256]{4,0,3,2,1:T(2,128)}, u32[]{:S(2)}) copy-start(f32[2,4,1,4,256]{4,0,3,2,1:T(2,128)} %copy.131) | copy-start | bytes 98308
  101.8 3.2 %copy-start.17 = (f32[2,4,4,1,256]{4,0,3,2,1:T(2,128)S(1)}, f32[2,4,4,1,256]{4,0,3,2,1:T(2,128)}, u32[]{:S(2)}) copy-start(f32[2,4,4,1,256]{4,0,3,2,1:T(2,128)} %copy.133) | copy-start | bytes 98308
  101.9 3.2 %copy-start.19 = (f32[2,4,4,1,256]{4,0,3,2,1:T(2,128)S(1)}, f32[2,4,4,1,256]{4,0,3,2,1:T(2,128)}, u32[]{:S(2)}) copy-start(f32[2,4,4,1,256]{4,0,3,2,1:T(2,128)} %copy.135) | copy-start | bytes 98308
  106.4 18.3 %collective-permute-start.6 = (f32[2,64,256]{2,1,0:T(8,128)S(1)}, f32[2,64,256]{2,1,0:T(8,128)S(1)}, u32[]{:S(2)}, u32[]{:S(2)}) collective-permute-start(f32[2,64,256]{2,1,0:T(8,128)S(1)} %fusion.14), channel_id=1, source_target_pairs={{0,4},{4,8},{8,12},{12,16},{16,20},{20,24},{24,28},{28,32},{32,36}... | collective-permute-start | bytes 393224 | tf_op jit(solution)/shard_map/ppermute | solution.py:29
  108.3 16.4 %collective-permute-start.7 = (f32[2,64,256]{2,1,0:T(8,128)S(1)}, f32[2,64,256]{2,1,0:T(8,128)S(1)}, u32[]{:S(2)}, u32[]{:S(2)}) collective-permute-start(f32[2,64,256]{2,1,0:T(8,128)S(1)} %fusion.14), channel_id=1, source_target_pairs={{4,0},{8,4},{12,8},{16,12},{20,16},{24,20},{28,24},{32,28},{36,32}... | collective-permute-start | bytes 393224 | tf_op jit(solution)/shard_map/ppermute | solution.py:32
  117.5 58.8 %collective-permute-start.8 = (f32[1,64,256]{2,1,0:T(8,128)}, f32[1,64,256]{2,1,0:T(8,128)}, u32[]{:S(2)}, u32[]{:S(2)}) collective-permute-start(f32[1,64,256]{2,1,0:T(8,128)} %get-tuple-element.32), channel_id=1, source_target_pairs={{0,1},{1,2},{2,3},{4,5},{5,6},{6,7},{8,9},{9,10},{10,11},{12,13},{... | collective-permute-start | bytes 196616 | tf_op jit(solution)/shard_map/ppermute | solution.py:29
  118.8 13.1 %copy-start.21 = (f32[1,256]{1,0:T(1,128)S(1)}, f32[1,256]{1,0:T(1,128)}, u32[]{:S(2)}) copy-start(f32[1,256]{1,0:T(1,128)} %copy-done.20) | copy-start | bytes 3076
  118.8 13.1 %copy-start.28 = (pred[256]{0:T(512)(128)(4,1)S(1)}, pred[256]{0:T(512)(128)(4,1)}, u32[]{:S(2)}) copy-start(pred[256]{0:T(512)(128)(4,1)} %copy-done.27) | copy-start | bytes 772
  118.8 57.5 %collective-permute-start.9 = (f32[1,64,256]{2,1,0:T(8,128)}, f32[1,64,256]{2,1,0:T(8,128)}, u32[]{:S(2)}, u32[]{:S(2)}) collective-permute-start(f32[1,64,256]{2,1,0:T(8,128)} %get-tuple-element.33), channel_id=1, source_target_pairs={{1,0},{2,1},{3,2},{5,4},{6,5},{7,6},{9,8},{10,9},{11,10},{13,12},{... | collective-permute-start | bytes 196616 | tf_op jit(solution)/shard_map/ppermute | solution.py:32
  156.6 8.4 %copy-start.26 = (pred[256]{0:T(512)(128)(4,1)S(1)}, pred[256]{0:T(512)(128)(4,1)}, u32[]{:S(2)}) copy-start(pred[256]{0:T(512)(128)(4,1)} %compare_and_fusion) | copy-start | bytes 772
  168.7 7.7 %copy-start.23 = (f32[2]{0:T(128)S(1)}, f32[2]{0:T(128)}, u32[]{:S(2)}) copy-start(f32[2]{0:T(128)} %get-tuple-element.54) | copy-start | bytes 28
  168.7 7.7 %copy-start.24 = (f32[2]{0:T(128)S(1)}, f32[2]{0:T(128)}, u32[]{:S(2)}) copy-start(f32[2]{0:T(128)} %get-tuple-element.55) | copy-start | bytes 28
  168.7 7.7 %copy-start.25 = (f32[2]{0:T(128)S(1)}, f32[2]{0:T(128)}, u32[]{:S(2)}) copy-start(f32[2]{0:T(128)} %get-tuple-element.56) | copy-start | bytes 28
  170.3 5.8 %copy-start = (f32[2,4,4,3,256]{4,0,3,2,1:T(2,128)S(1)}, f32[2,4,4,3,256]{4,0,3,2,1:T(2,128)}, u32[]{:S(2)}) copy-start(f32[2,4,4,3,256]{4,0,3,2,1:T(2,128)} %get-tuple-element.26) | copy-start | bytes 294916
  172.8 3.2 %copy-start.1 = (f32[2,4,4,3,256]{4,0,3,2,1:T(2,128)S(1)}, f32[2,4,4,3,256]{4,0,3,2,1:T(2,128)}, u32[]{:S(2)}) copy-start(f32[2,4,4,3,256]{4,0,3,2,1:T(2,128)} %get-tuple-element.27) | copy-start | bytes 294916
  172.8 3.2 %copy-start.2 = (f32[2,4,3,4,256]{4,0,3,2,1:T(2,128)S(1)}, f32[2,4,3,4,256]{4,0,3,2,1:T(2,128)}, u32[]{:S(2)}) copy-start(f32[2,4,3,4,256]{4,0,3,2,1:T(2,128)} %get-tuple-element.28) | copy-start | bytes 294916
  172.9 3.2 %copy-start.3 = (f32[2,4,3,4,256]{4,0,3,2,1:T(2,128)S(1)}, f32[2,4,3,4,256]{4,0,3,2,1:T(2,128)}, u32[]{:S(2)}) copy-start(f32[2,4,3,4,256]{4,0,3,2,1:T(2,128)} %get-tuple-element.29) | copy-start | bytes 294916
  172.9 3.2 %copy-start.4 = (f32[2,3,4,4,256]{4,0,3,2,1:T(2,128)S(1)}, f32[2,3,4,4,256]{4,0,3,2,1:T(2,128)}, u32[]{:S(2)}) copy-start(f32[2,3,4,4,256]{4,0,3,2,1:T(2,128)} %get-tuple-element.30) | copy-start | bytes 294916
  172.9 3.2 %copy-start.5 = (f32[2,3,4,4,256]{4,0,3,2,1:T(2,128)S(1)}, f32[2,3,4,4,256]{4,0,3,2,1:T(2,128)}, u32[]{:S(2)}) copy-start(f32[2,3,4,4,256]{4,0,3,2,1:T(2,128)} %get-tuple-element.31) | copy-start | bytes 294916
  172.9 3.2 %copy-start.12 = (f32[2,4,1,4,256]{4,0,3,2,1:T(2,128)S(1)}, f32[2,4,1,4,256]{4,0,3,2,1:T(2,128)}, u32[]{:S(2)}) copy-start(f32[2,4,1,4,256]{4,0,3,2,1:T(2,128)} %copy.144) | copy-start | bytes 98308
  172.9 3.2 %copy-start.14 = (f32[2,4,1,4,256]{4,0,3,2,1:T(2,128)S(1)}, f32[2,4,1,4,256]{4,0,3,2,1:T(2,128)}, u32[]{:S(2)}) copy-start(f32[2,4,1,4,256]{4,0,3,2,1:T(2,128)} %copy.146) | copy-start | bytes 98308
  172.9 3.2 %copy-start.16 = (f32[2,4,4,1,256]{4,0,3,2,1:T(2,128)S(1)}, f32[2,4,4,1,256]{4,0,3,2,1:T(2,128)}, u32[]{:S(2)}) copy-start(f32[2,4,4,1,256]{4,0,3,2,1:T(2,128)} %copy.148) | copy-start | bytes 98308
  172.9 3.2 %copy-start.18 = (f32[2,4,4,1,256]{4,0,3,2,1:T(2,128)S(1)}, f32[2,4,4,1,256]{4,0,3,2,1:T(2,128)}, u32[]{:S(2)}) copy-start(f32[2,4,4,1,256]{4,0,3,2,1:T(2,128)} %copy.150) | copy-start | bytes 98308
where the time goes:
time: 181 us; the launch traced here: 178 us
  local copies, waits for them, and re-layouts  79.1 us (44%)
  other arithmetic  50.4 us (28%)
  starting transfers between devices  42.9 us (24%)
  between operations  5.78 us (3%)
    gather x12, local copies, waits for them, and re-layouts, far_faces(): jnp.take(face_cells, pattern_rows[direction], axis=3)  29.4 us
    unnamed x70, local copies, waits for them, and re-layouts  26.7 us
    ppermute x4, starting transfers between devices, padded(): lax.ppermute(lax.slice_in_dim(block, 0, width, axis=dim), axis, backward)  24.3 us
    ppermute x2, starting transfers between devices, from_behind(): return lax.ppermute(block, axis, route)  12.2 us
    ppermute x4, starting transfers between devices, padded(): lax.ppermute(lax.slice_in_dim(block, block.shape[dim] - width, None, axis...  6.4 us
    broadcast_in_dim x2, other arithmetic, shifted_sum(): face_list[0][:, None]  5.22 us
    broadcast_in_dim x2, other arithmetic, shifted_sum(): face_list[1][:, None]  5.11 us
    broadcast_in_dim x2, other arithmetic, shifted_sum(): face_list[5][:, :, :, None]  5.06 us
  transfers between devices with their start and end apart: 10, of which 0 were waited for; matrix products, arithmetic and copies ran while one was open for 68% of the time, Pallas kernels for 0%

commit v1 on v0

v1 whole, which is shorter than its diff:
```python
import functools

import jax
import jax.numpy as jnp
import numpy as np
from jax import lax
from jax.experimental import pallas as pl
from jax.experimental.pallas import tpu as pltpu
from jax.sharding import PartitionSpec as P

BRICKS_DEV = 256
SPILL = 32
Y = 8
OLD_SLOTS = 320
EXPONENT = 0.5
HEIGHT = 8.0
OMEGA = 0.8

F32 = jnp.float32
LANES = 128
TILES = 8
GATHER = lax.GatherDimensionNumbers(
    offset_dims=(),
    collapsed_slice_dims=(1,),
    start_index_map=(1,),
    operand_batching_dims=(0,),
    start_indices_batching_dims=(0,),
)


def weight_table(layers):
    rows = []
    for level in range(-1, Y + 1):
        if not 0 <= level < Y:
            rows.append((0.0, 0.0, 0.0, 0.0, 1.0))
            continue
        y_here = HEIGHT * (level / Y) ** 2
        y_next = HEIGHT * ((level + 1) / Y) ** 2
        y_prev = HEIGHT * ((level - 1) / Y) ** 2
        step_up, step_down = y_next - y_here, y_here - y_prev
        up_weight = ((y_here + y_next) * 0.5) ** EXPONENT
        down_weight = ((y_here + y_prev) * 0.5) ** EXPONENT
        has_lower = float(level > 0)
        up_link = up_weight / step_up
        down_link = has_lower * down_weight / step_down
        planar = 0.5 * (up_weight * step_up + has_lower * down_weight * step_down)
        surface = float(level == 0)
        rows.append((planar, down_link, up_link, surface, down_link + up_link + surface))
    return np.asarray(rows, np.float32)


def weights_at(table, group, layers, offset):
    groups = Y // layers
    out = []
    for column in range(5):
        value = F32(table[offset + 1, column])
        for g in range(1, groups):
            value = jnp.where(group == g, F32(table[g * layers + offset + 1, column]), value)
        out.append(value)
    return out


def lanes():
    return lax.broadcasted_iota(jnp.int32, (8, LANES), 1)


def rows():
    return lax.broadcasted_iota(jnp.int32, (8, LANES), 0)


def spin(tile, shift):
    if isinstance(shift, int):
        return pltpu.roll(tile, shift % LANES, 1) if shift % LANES else tile
    return pltpu.roll(tile, jnp.bitwise_and(shift, LANES - 1), 1)


def pick(tile, index):
    return lax.gather(
        tile,
        index[:, :, None],
        GATHER,
        (1, 1),
        mode=lax.GatherScatterMode.PROMISE_IN_BOUNDS,
    )


def spill_counts(owner_ref, live_count, device):
    to_prev = jnp.int32(0)
    to_next = jnp.int32(0)
    for step in (32, 16, 8, 4, 2, 1):
        near = jnp.minimum(to_prev + step, SPILL)
        hit = (to_prev + step <= SPILL) & (owner_ref[near - 1] < device)
        to_prev = jnp.where(hit, to_prev + step, to_prev)
        near = jnp.minimum(to_next + step, SPILL)
        hit = (to_next + step <= SPILL) & (owner_ref[live_count - near] > device)
        to_next = jnp.where(hit, to_next + step, to_next)
    return to_prev, to_next


def old_tile(ref, lead, t, c):
    at = (lead, pl.ds(8 * t, 8)) if lead is not None else (pl.ds(8 * t, 8),)
    if c < 2:
        return ref[at + (pl.ds(LANES * c, LANES),)]
    half = ref[at + (pl.ds(2 * LANES, OLD_SLOTS - 2 * LANES),)]
    return jnp.concatenate([half, jnp.zeros((8, 3 * LANES - OLD_SLOTS), F32)], axis=1)


def face_indices(pattern_rows):
    sub = rows()
    kinds = (
        pattern_rows[0],
        pattern_rows[1],
        jnp.where(sub < 4, pattern_rows[3], pattern_rows[2]),
        jnp.where((sub & 3) == 3, pattern_rows[4], pattern_rows[5]),
    )
    out = []
    for w in kinds:
        source = w >> 7
        own = (source == 2) | (source == 3)
        beside = jnp.where(w >= 2 * BRICKS_DEV, w - (2 * BRICKS_DEV - SPILL), w - (BRICKS_DEV - SPILL))
        lane = jnp.where(own, w & (LANES - 1), jnp.where(w >= BRICKS_DEV - SPILL, beside, LANES - 1))
        out.append((lane, source == 2, source == 3))
    return out


def face(kind, tiles):
    lane, first, second = kind
    return jnp.where(first, pick(tiles[0], lane), jnp.where(second, pick(tiles[1], lane), pick(tiles[2], lane)))


class Sources:
    def __init__(self, read):
        sub = rows()
        self.tile = [[read(c, t) for t in range(TILES)] for c in range(3)]
        self.turned = [[pltpu.roll(v, 4, 0) for v in column] for column in self.tile]
        self.y_edge = [
            [jnp.where(sub < 4, column[2 * i], column[2 * i + 1]) for i in range(4)]
            for column in self.tile
        ]


def neighbour_sum(src, here, turned, kinds):
    sub = rows()
    low, k = sub < 4, sub & 3
    x_low, x_high, y_both, z_both = kinds
    total = []
    for t in range(TILES):
        if t < 2:
            below = face(x_low, [src.tile[c][6 + t] for c in range(3)])
        else:
            below = here[t - 2]
        if t >= 6:
            above = face(x_high, [src.tile[c][t - 6] for c in range(3)])
        else:
            above = here[t + 2]
        total.append(below + above)
    for i in range(4):
        edge = pltpu.roll(face(y_both, [src.y_edge[c][i] for c in range(3)]), 4, 0)
        first, second = turned[2 * i], turned[2 * i + 1]
        middle = jnp.where(low, first, second)
        total[2 * i] += jnp.where(low, edge, first) + middle
        total[2 * i + 1] += jnp.where(low, second, edge) + middle
    for t in range(TILES):
        edge = face(z_both, [src.turned[c][t] for c in range(3)])
        total[t] += pltpu.roll(jnp.where(k == 3, edge, here[t]), 1, 0)
        total[t] += pltpu.roll(jnp.where(k == 0, edge, here[t]), 7, 0)
    return total


def is_even(axis):
    return (lax.axis_index(axis) & 1) == 0


def send_kernel(
    field_hbm, coef_hbm, owner_hbm, counts_ref,
    near_ref, far_ref, field_ref, coef_ref,
    owner_ref, sems,
):
    pairs = ((owner_hbm, owner_ref), (field_hbm, field_ref), (coef_hbm, coef_ref))
    copies = [pltpu.make_async_copy(a, b, sems.at[i]) for i, (a, b) in enumerate(pairs)]
    for copy in copies:
        copy.start()
    lane, sub = lanes(), rows()
    even = is_even("leaf")
    copies[0].wait()
    live = counts_ref[0]
    to_prev, to_next = spill_counts(owner_ref, live, lax.axis_index("leaf"))
    kept = jnp.where(sub == 1, live, jnp.where(sub == 2, to_prev, to_next)).astype(F32)
    prev_count = jnp.where(sub == 0, to_prev.astype(F32), kept)
    next_count = jnp.where(sub == 0, to_next.astype(F32), kept)
    near_ref[pl.ds(96, 8), :] = jnp.where(even, next_count, prev_count)
    far_ref[pl.ds(96, 8), :] = jnp.where(even, prev_count, next_count)
    for a in range(3):
        ref, lead = (field_ref, a) if a < 2 else (coef_ref, None)
        if a == 0:
            copies[1].wait()
        if a == 2:
            copies[2].wait()
        for r in range(4):
            at = pl.ds(32 * a + 8 * r, 8)
            front = old_tile(ref, lead, r, 0)
            back = old_tile(ref, lead, r + 4, 0)
            prev = jnp.where(lane < 64, front, pltpu.roll(back, 64, 1))
            early = lane >= live - 192
            front = jnp.where(early, old_tile(ref, lead, r, 1), old_tile(ref, lead, r, 2))
            back = jnp.where(early, old_tile(ref, lead, r + 4, 1), old_tile(ref, lead, r + 4, 2))
            next = jnp.where(lane < 64, spin(front, 64 - live), spin(back, 128 - live))
            near_ref[at, :] = jnp.where(even, next, prev)
            far_ref[at, :] = jnp.where(even, prev, next)


def place_kernel(
    field_ref, coef_ref, pattern_ref, kept_ref, near_ref, far_ref,
    pack_ref, coef_out, band_out, sum_near, sum_far,
):
    lane = lanes()
    even = is_even("leaf")
    live, to_prev, to_next = (kept_ref[96 + i, 0].astype(jnp.int32) for i in (1, 2, 3))
    from_near, from_far = near_ref[96, 0], far_ref[96, 0]
    from_prev = jnp.where(even, from_far, from_near).astype(jnp.int32)
    from_next = jnp.where(even, from_near, from_far).astype(jnp.int32)
    stay = live - to_prev - to_next
    drift = to_prev - from_prev
    tail = from_prev + stay - LANES
    for a in range(3):
        ref, lead = (field_ref, a) if a < 2 else (coef_ref, None)
        for t in range(TILES):
            h = 64 * (t // 4)
            at = pl.ds(32 * a + 8 * (t % 4), 8)
            near, far = near_ref[at, :], far_ref[at, :]
            before, after = jnp.where(even, far, near), jnp.where(even, near, far)
            x0, x1, x2 = (old_tile(ref, lead, t, c) for c in range(3))
            r0, r1, r2 = spin(x0, -drift), spin(x1, -drift), spin(x2, -drift)
            own0 = jnp.where(lane < LANES - drift, r0, r1)
            own1 = jnp.where(lane < -drift, r0, jnp.where(lane < LANES - drift, r1, r2))
            own0 = jnp.where(lane < from_prev, spin(before, from_prev - 64 - h), own0)
            own1 = jnp.where(lane >= tail, spin(after, tail - h), own1)
            low = jnp.where(
                lane < SPILL - to_prev,
                spin(before, from_prev - to_prev - SPILL - h),
                spin(x0, SPILL - to_prev),
            )
            end = jnp.where(lane >= live - to_next - LANES, x1, x2)
            high = jnp.where(
                lane < SPILL + to_next,
                spin(end, SPILL + to_next - live),
                spin(after, SPILL + to_next - from_next - h),
            )
            band = jnp.where(lane < SPILL, low, jnp.where(lane < 2 * SPILL, high, 0.0))
            if a < 2:
                pack_ref[pl.ds(128 * a + 8 * t, 8), :] = own0
                pack_ref[pl.ds(128 * a + 64 + 8 * t, 8), :] = own1
            else:
                coef_out[pl.ds(8 * t, 8), :] = own0
                coef_out[pl.ds(64 + 8 * t, 8), :] = own1
            band_out[pl.ds(64 * a + 8 * t, 8), :] = band
    edge_rows = []
    for direction in range(6):
        first = jnp.broadcast_to(pattern_ref[pl.ds(direction, 1), pl.ds(0, LANES)], (8, LANES))
        second = jnp.broadcast_to(pattern_ref[pl.ds(direction, 1), pl.ds(LANES, LANES)], (8, LANES))
        edge_rows.append(jnp.where(lane < 64, first, second))
    kinds = face_indices(edge_rows)
    for a in range(2):

        def read(c, t):
            if c < 2:
                return pack_ref[pl.ds(128 * a + 64 * c + 8 * t, 8), :]
            return band_out[pl.ds(64 * a + 8 * t, 8), :]

        src = Sources(read)
        for r in range(4):
            pack_ref[pl.ds(256 + 32 * a + 8 * r, 8), :] = jnp.where(
                lane < 64, src.tile[2][r], pltpu.roll(src.tile[2][r + 4], 64, 1)
            )
        here = [jnp.where(lane < 64, src.tile[0][t], src.tile[1][t]) for t in range(TILES)]
        turned = [jnp.where(lane < 64, src.turned[0][t], src.turned[1][t]) for t in range(TILES)]
        total = neighbour_sum(src, here, turned, kinds)
        for half in range(2):
            at = pl.ds(16 * a + 8 * half, 8)
            first = [spin(total[2 * q + half], 32 * q) for q in range(4)]
            last = [spin(total[2 * q + half], 32 * q + 32) for q in range(4)]
            first, last = (
                jnp.where(
                    lane < 64,
                    jnp.where(lane < 32, values[0], values[1]),
                    jnp.where(lane < 96, values[2], values[3]),
                )
                for values in (first, last)
            )
            sum_near[at, :] = jnp.where(even, last, first)
            sum_far[at, :] = jnp.where(even, first, last)


def own(ref, a, c, t):
    return ref[pl.ds(128 * a + 64 * c + 8 * t, 8), :]


def own_kinds(pattern_ref):
    return [
        face_indices(
            [
                jnp.broadcast_to(pattern_ref[pl.ds(d, 1), pl.ds(LANES * c, LANES)], (8, LANES))
                for d in range(6)
            ]
        )
        for c in range(2)
    ]


def gains(weights, coef):
    spread = weights[0] * coef
    return spread, OMEGA / (6.0 * spread + weights[4])


def bulge(weights, phase):
    return weights[3] * (2.0 * phase - phase * phase * phase)


def own_kernel(layers, table, pattern_ref, pack_ref, coef_ref, band_ref, half_ref):
    group = lax.axis_index("gy")
    kinds = own_kinds(pattern_ref)
    weights = [weights_at(table, group, layers, a) for a in range(2)]
    for a in range(2):
        src = Sources(
            lambda c, t: own(pack_ref, a, c, t) if c < 2 else band_ref[pl.ds(64 * a + 8 * t, 8), :]
        )
        for c in range(2):
            total = neighbour_sum(src, src.tile[c], src.turned[c], kinds[c])
            for t in range(TILES):
                now = src.tile[c][t]
                spread, gain = gains(weights[a], coef_ref[pl.ds(64 * c + 8 * t, 8), :])
                push = spread * total[t] + weights[a][2 - a] * own(pack_ref, 1 - a, c, t)
                if a == 0:
                    push = push + bulge(weights[0], now)
                half_ref[pl.ds(128 * a + 64 * c + 8 * t, 8), :] = (1.0 - OMEGA) * now + gain * push


def relax_kernel(
    layers, table,
    pattern_ref, pack_ref, coef_ref, band_ref, half_ref, side_near, side_far, sum_near, sum_far,
    out_ref, next_own, next_band, next_side,
):
    lane = lanes()
    group = lax.axis_index("gy")
    even = is_even("leaf")
    even_group = is_even("gy")
    kinds = own_kinds(pattern_ref)
    w_lower, w_first, w_second, w_upper = (weights_at(table, group, layers, o) for o in (-1, 0, 1, 2))

    def step(weights, now, total, below, above, coef, phase):
        spread, gain = gains(weights, coef)
        push = spread * total + weights[1] * below + weights[2] * above
        if phase is not None:
            push = push + bulge(weights, phase)
        return (1.0 - OMEGA) * now + gain * push

    def beside(upper, at):
        near, far = side_near[at, :], side_far[at, :]
        return jnp.where(even_group, near, far) if upper else jnp.where(even_group, far, near)

    def side(upper, a, c, t):
        return beside(upper, pl.ds(128 * a + 64 * c + 8 * t, 8))

    def side_band(upper, a, t):
        tile = beside(upper, pl.ds(256 + 32 * a + 8 * (t % 4), 8))
        tile = pltpu.roll(tile, 64, 1) if t >= 4 else tile
        return jnp.where(lane < 64, tile, 0.0)

    for a in range(2):
        weights = w_second if a else w_first
        for c in range(2):
            for t in range(TILES):
                _, gain = gains(weights, coef_ref[pl.ds(64 * c + 8 * t, 8), :])
                missing = weights[1 + a] * side(a, 1 - a, c, t)
                next_own[pl.ds(128 * a + 64 * c + 8 * t, 8), :] = own(half_ref, a, c, t) + gain * missing
        for t in range(TILES):
            now = band_ref[pl.ds(64 * a + 8 * t, 8), :]
            coef = band_ref[pl.ds(128 + 8 * t, 8), :]
            at = pl.ds(16 * a + 8 * (t % 2), 8)
            q = t // 2
            near, far = sum_near[at, :], sum_far[at, :]
            low, high = jnp.where(even, far, near), jnp.where(even, near, far)
            low, high = spin(low, -32 * q), spin(high, 32 - 32 * q)
            total_t = jnp.where(lane < 32, low, jnp.where(lane < 64, high, 0.0))
            if a == 0:
                below, above = side_band(0, 1, t), band_ref[pl.ds(64 + 8 * t, 8), :]
                new = step(w_first, now, total_t, below, above, coef, now)
            else:
                below, above = band_ref[pl.ds(8 * t, 8), :], side_band(1, 0, t)
                new = step(w_second, now, total_t, below, above, coef, None)
            next_band[pl.ds(64 * a + 8 * t, 8), :] = new

    for upper in range(2):
        a = 1 - upper
        src = Sources(lambda c, t: side(upper, a, c, t) if c < 2 else side_band(upper, a, t))
        for c in range(2):
            total = neighbour_sum(src, src.tile[c], src.turned[c], kinds[c])
            for t in range(TILES):
                coef = coef_ref[pl.ds(64 * c + 8 * t, 8), :]
                if upper:
                    below, above = own(pack_ref, 1, c, t), side(1, 1, c, t)
                    new = step(w_upper, src.tile[c][t], total[t], below, above, coef, None)
                else:
                    below, above = side(0, 0, c, t), own(pack_ref, 0, c, t)
                    new = step(w_lower, src.tile[c][t], total[t], below, above, coef, None)
                next_side[pl.ds(128 * upper + 64 * c + 8 * t, 8), :] = new

    for a in range(2):
        src = Sources(
            lambda c, t: own(next_own, a, c, t) if c < 2 else next_band[pl.ds(64 * a + 8 * t, 8), :]
        )
        for c in range(2):
            total = neighbour_sum(src, src.tile[c], src.turned[c], kinds[c])
            for t in range(TILES):
                coef = coef_ref[pl.ds(64 * c + 8 * t, 8), :]
                now = src.tile[c][t]
                if a == 0:
                    below, above = own(next_side, 0, c, t), own(next_own, 1, c, t)
                    new = step(w_first, now, total[t], below, above, coef, own(pack_ref, 0, c, t))
                else:
                    below, above = own(next_own, 0, c, t), own(next_side, 1, c, t)
                    new = step(w_second, now, total[t], below, above, coef, None)
                out_ref[a, pl.ds(8 * t, 8), pl.ds(LANES * c, LANES)] = new


def swap(block, axis, first):
    route = []
    for i in range(first, lax.axis_size(axis) - 1, 2):
        route += [(i, i + 1), (i + 1, i)]
    return lax.ppermute(block, axis, route)


def call(kernel, shapes, spaces, *operands, scratch=(), flops=0):
    vmem = pltpu.VMEM
    space = {"h": pltpu.HBM, "v": vmem, "s": pltpu.SMEM}
    moved = sum(4 * int(np.prod(o.shape)) for o in operands)
    return pl.pallas_call(
        kernel,
        out_shape=[jax.ShapeDtypeStruct(s, F32) for s in shapes],
        in_specs=[pl.BlockSpec(memory_space=space[s]) for s in spaces],
        out_specs=[pl.BlockSpec(memory_space=vmem) for _ in shapes],
        scratch_shapes=list(scratch),
        compiler_params=pltpu.CompilerParams(vmem_limit_bytes=16 * 2**20),
        cost_estimate=pl.CostEstimate(flops=flops, bytes_accessed=moved, transcendentals=0),
    )(*operands)


def local(table, field_old, coef_old, owner, counts, pattern):
    layers = field_old.shape[0]
    stored = [pltpu.with_memory_space_constraint(x, pltpu.HBM) for x in (field_old, coef_old, owner)]
    to_near, to_far, field, coef = call(
        send_kernel,
        [(104, LANES), (104, LANES), field_old.shape, coef_old.shape],
        "hhhs",
        *stored, counts,
        scratch=[
            pltpu.SMEM((OLD_SLOTS,), jnp.int32),
            pltpu.SemaphoreType.DMA((3,)),
        ],
    )
    from_far = swap(to_far, "leaf", 1)
    from_near = swap(to_near, "leaf", 0)
    pack, coef, band, sum_near, sum_far = call(
        place_kernel,
        [(320, LANES), (128, LANES), (192, LANES), (32, LANES), (32, LANES)],
        "vvvvvv",
        field, coef, pattern, to_near, from_near, from_far,
    )
    sum_near = swap(sum_near, "leaf", 0)
    sum_far = swap(sum_far, "leaf", 1)
    side_near = swap(pack, "gy", 0)
    side_far = swap(pack, "gy", 1)
    (half,) = call(
        functools.partial(own_kernel, layers, table),
        [(256, LANES)],
        "vvvv",
        pattern, pack, coef, band,
    )
    (out,) = call(
        functools.partial(relax_kernel, layers, table),
        [(layers, 64, BRICKS_DEV)],
        "vvvvvvvvv",
        pattern, pack, coef, band, half, side_near, side_far, sum_near, sum_far,
        scratch=[pltpu.VMEM((rows, LANES), F32) for rows in (256, 128, 256)],
    )
    return out


def solution(mesh):
    layers = Y // mesh.shape["gy"]
    return jax.shard_map(
        functools.partial(local, weight_table(layers)),
        mesh=mesh,
        in_specs=(P("gy", None, "leaf"), P(None, "leaf"), P("leaf"), P("leaf"), P(None, "leaf")),
        out_specs=P("gy", None, "leaf"),
        check_vma=False,
    )
```

time: 181 us -> 34.7 us (0.19)
  the two profiles are of different devices: /device:TPU:38 before, /device:TPU:32 now
where the time goes in v1:
time: 34.7 us; the launch traced here: 34.4 us
  starting transfers between devices  26 us (75%)
  waiting for transfers between devices  4.14 us (12%)
  Pallas kernels  3.53 us (10%)
  between operations  0.75 us (2%)
    ppermute x6, starting transfers between devices, swap(): return lax.ppermute(block, axis, route)  26 us
    ppermute x6, waiting for transfers between devices, swap(): return lax.ppermute(block, axis, route)  4.14 us
    pallas_call x4, Pallas kernels, call(): pl.pallas_call(kernel, out_shape=[jax.ShapeDtypeStruct(s, F32) for s in s...  3.53 us
  transfers between devices with their start and end apart: 6, of which 2 were waited for; matrix products, arithmetic and copies ran while one was open for 0% of the time, Pallas kernels for 1%

profile of v1, /device:TPU:32, one launch (start us, length us, event | category | flops | bytes accessed | tf_op | source)
XLA Modules:
  0.0 34.4 jit_solution(11151126131078201386)
XLA Ops:
  0.7 0.0 copy-start
  0.7 1.1 %shard_map.55 = (f32[104,128]{1,0:T(8,128)S(1)}, f32[104,128]{1,0:T(8,128)S(1)}, f32[2,64,320]{2,1,0:T(8,128)S(1)}, f32[64,320]{1,0:T(8,128)S(1)}) custom-call(f32[2,64,320]{2,1,0:T(8,128)} %field_hbm.1, f32[64,320]{1,0:T(8,128)} %coef_hbm.1, s32[320]{0:T(512)} %owner_hbm.1, s32[1]{0:T(128)S(6)} %copy.6.counts_ref), custom_call_target="tpu_custom_call" | custom-call | bytes 247044 | tf_op jit(solution)/shard_map/pallas_call | solution.py:437
  1.8 10.3 %collective-permute-start.1 = (f32[104,128]{1,0:T(8,128)S(1)}, f32[104,128]{1,0:T(8,128)S(1)}, u32[]{:S(2)}, u32[]{:S(2)}) collective-permute-start(f32[104,128]{1,0:T(8,128)S(1)} %get-tuple-element.17), channel_id=1, source_target_pairs={{4,8},{8,4},{12,16},{16,12},{20,24},{24,20},{28,32},{32,28},{36,40... | collective-permute-start | bytes 159752 | tf_op jit(solution)/shard_map/ppermute | solution.py:430
  12.1 1.9 %collective-permute-start = (f32[104,128]{1,0:T(8,128)S(1)}, f32[104,128]{1,0:T(8,128)S(1)}, u32[]{:S(2)}, u32[]{:S(2)}) collective-permute-start(f32[104,128]{1,0:T(8,128)S(1)} %get-tuple-element.16.kept_ref), channel_id=1, source_target_pairs={{0,4},{4,0},{8,12},{12,8},{16,20},{20,16},{24,28},{28,24},{32,36},... | collective-permute-start | bytes 159752 | tf_op jit(solution)/shard_map/ppermute | solution.py:430
  14.0 0.0 collective-permute-done.1.far_ref
  14.0 1.2 %collective-permute-done.near_ref = f32[104,128]{1,0:T(8,128)S(1)} collective-permute-done((f32[104,128]{1,0:T(8,128)S(1)}, f32[104,128]{1,0:T(8,128)S(1)}, u32[]{:S(2)}, u32[]{:S(2)}) %collective-permute-start) | collective-permute-done | bytes 53280 | tf_op jit(solution)/shard_map/ppermute | solution.py:430
  15.2 0.0 copy-done
  15.2 0.6 %shard_map.56 = (f32[320,128]{1,0:T(8,128)S(1)}, f32[128,128]{1,0:T(8,128)S(1)}, f32[192,128]{1,0:T(8,128)S(1)}, f32[32,128]{1,0:T(8,128)S(1)}, f32[32,128]{1,0:T(8,128)S(1)}) custom-call(f32[2,64,320]{2,1,0:T(8,128)S(1)} %get-tuple-element.14.field_ref, f32[64,320]{1,0:T(8,128)S(1)} %get-tuple-element.15.coef_ref, s32[6,256]{1,0:T(8,128)S(1)} %copy-done, ...), custom_call_target="tpu_custom_call" | custom-call | bytes 411648 | tf_op jit(solution)/shard_map/pallas_call | solution.py:437
  15.8 0.7 %collective-permute-start.3 = (f32[320,128]{1,0:T(8,128)S(1)}, f32[320,128]{1,0:T(8,128)S(1)}, u32[]{:S(2)}, u32[]{:S(2)}) collective-permute-start(f32[320,128]{1,0:T(8,128)S(1)} %get-tuple-element.18.pack_ref), channel_id=1, source_target_pairs={{1,2},{2,1},{5,6},{6,5},{9,10},{10,9},{13,14},{14,13},{17,18},{18,... | collective-permute-start | bytes 491528 | tf_op jit(solution)/shard_map/ppermute | solution.py:430
  16.5 6.1 %collective-permute-start.2 = (f32[320,128]{1,0:T(8,128)S(1)}, f32[320,128]{1,0:T(8,128)S(1)}, u32[]{:S(2)}, u32[]{:S(2)}) collective-permute-start(f32[320,128]{1,0:T(8,128)S(1)} %get-tuple-element.18.pack_ref), channel_id=1, source_target_pairs={{0,1},{1,0},{2,3},{3,2},{4,5},{5,4},{6,7},{7,6},{8,9},{9,8},{10,11... | collective-permute-start | bytes 491528 | tf_op jit(solution)/shard_map/ppermute | solution.py:430
  22.7 1.9 %collective-permute-start.4 = (f32[32,128]{1,0:T(8,128)S(1)}, f32[32,128]{1,0:T(8,128)S(1)}, u32[]{:S(2)}, u32[]{:S(2)}) collective-permute-start(f32[32,128]{1,0:T(8,128)S(1)} %get-tuple-element.21), channel_id=1, source_target_pairs={{0,4},{4,0},{8,12},{12,8},{16,20},{20,16},{24,28},{28,24},{32,36},... | collective-permute-start | bytes 49160 | tf_op jit(solution)/shard_map/ppermute | solution.py:430
  24.6 5.1 %collective-permute-start.5 = (f32[32,128]{1,0:T(8,128)S(1)}, f32[32,128]{1,0:T(8,128)S(1)}, u32[]{:S(2)}, u32[]{:S(2)}) collective-permute-start(f32[32,128]{1,0:T(8,128)S(1)} %get-tuple-element.22), channel_id=1, source_target_pairs={{4,8},{8,4},{12,16},{16,12},{20,24},{24,20},{28,32},{32,28},{36,40... | collective-permute-start | bytes 49160 | tf_op jit(solution)/shard_map/ppermute | solution.py:430
  29.7 0.3 shard_map.57.half_ref
  30.0 0.0 collective-permute-done.4.sum_near
  30.0 2.9 %collective-permute-done.5.sum_far = f32[32,128]{1,0:T(8,128)S(1)} collective-permute-done((f32[32,128]{1,0:T(8,128)S(1)}, f32[32,128]{1,0:T(8,128)S(1)}, u32[]{:S(2)}, u32[]{:S(2)}) %collective-permute-start.5) | collective-permute-done | bytes 16416 | tf_op jit(solution)/shard_map/ppermute | solution.py:430
  33.0 0.0 collective-permute-done.3.side_far
  33.0 0.0 collective-permute-done.2.side_near
  33.0 1.4 %shard_map.58 = f32[2,64,256]{2,1,0:T(8,128)} custom-call(s32[6,256]{1,0:T(8,128)S(1)} %copy-done, f32[320,128]{1,0:T(8,128)S(1)} %get-tuple-element.18.pack_ref, f32[128,128]{1,0:T(8,128)S(1)} %get-tuple-element.19.coef_ref, f32[192,128]{1,0:T(8,128)S(1)} %get-tuple-element.20.band_ref, f32[256,128]{1,0:T(8,128)S(1)} %shard_map.57.half_ref, ...), custom_call_target="tpu_custom_call" | custom-call | bytes 825344 | tf_op jit(solution)/shard_map/pallas_call | solution.py:437
Async XLA Ops:
  0.7 14.6 %copy-start = (s32[6,256]{1,0:T(8,128)S(1)}, s32[6,256]{1,0:T(8,128)}, u32[]{:S(2)}) copy-start(s32[6,256]{1,0:T(8,128)} %pattern_ref.5) | copy-start | bytes 18436
  1.8 12.2 %collective-permute-start.1 = (f32[104,128]{1,0:T(8,128)S(1)}, f32[104,128]{1,0:T(8,128)S(1)}, u32[]{:S(2)}, u32[]{:S(2)}) collective-permute-start(f32[104,128]{1,0:T(8,128)S(1)} %get-tuple-element.17), channel_id=1, source_target_pairs={{4,8},{8,4},{12,16},{16,12},{20,24},{24,20},{28,32},{32,28},{36,40... | collective-permute-start | bytes 159752 | tf_op jit(solution)/shard_map/ppermute | solution.py:430
  12.1 3.1 %collective-permute-start = (f32[104,128]{1,0:T(8,128)S(1)}, f32[104,128]{1,0:T(8,128)S(1)}, u32[]{:S(2)}, u32[]{:S(2)}) collective-permute-start(f32[104,128]{1,0:T(8,128)S(1)} %get-tuple-element.16.kept_ref), channel_id=1, source_target_pairs={{0,4},{4,0},{8,12},{12,8},{16,20},{20,16},{24,28},{28,24},{32,36},... | collective-permute-start | bytes 159752 | tf_op jit(solution)/shard_map/ppermute | solution.py:430
  15.8 17.1 %collective-permute-start.3 = (f32[320,128]{1,0:T(8,128)S(1)}, f32[320,128]{1,0:T(8,128)S(1)}, u32[]{:S(2)}, u32[]{:S(2)}) collective-permute-start(f32[320,128]{1,0:T(8,128)S(1)} %get-tuple-element.18.pack_ref), channel_id=1, source_target_pairs={{1,2},{2,1},{5,6},{6,5},{9,10},{10,9},{13,14},{14,13},{17,18},{18,... | collective-permute-start | bytes 491528 | tf_op jit(solution)/shard_map/ppermute | solution.py:430
  16.5 16.4 %collective-permute-start.2 = (f32[320,128]{1,0:T(8,128)S(1)}, f32[320,128]{1,0:T(8,128)S(1)}, u32[]{:S(2)}, u32[]{:S(2)}) collective-permute-start(f32[320,128]{1,0:T(8,128)S(1)} %get-tuple-element.18.pack_ref), channel_id=1, source_target_pairs={{0,1},{1,0},{2,3},{3,2},{4,5},{5,4},{6,7},{7,6},{8,9},{9,8},{10,11... | collective-permute-start | bytes 491528 | tf_op jit(solution)/shard_map/ppermute | solution.py:430
  22.7 7.4 %collective-permute-start.4 = (f32[32,128]{1,0:T(8,128)S(1)}, f32[32,128]{1,0:T(8,128)S(1)}, u32[]{:S(2)}, u32[]{:S(2)}) collective-permute-start(f32[32,128]{1,0:T(8,128)S(1)} %get-tuple-element.21), channel_id=1, source_target_pairs={{0,4},{4,0},{8,12},{12,8},{16,20},{20,16},{24,28},{28,24},{32,36},... | collective-permute-start | bytes 49160 | tf_op jit(solution)/shard_map/ppermute | solution.py:430
  24.6 8.4 %collective-permute-start.5 = (f32[32,128]{1,0:T(8,128)S(1)}, f32[32,128]{1,0:T(8,128)S(1)}, u32[]{:S(2)}, u32[]{:S(2)}) collective-permute-start(f32[32,128]{1,0:T(8,128)S(1)} %get-tuple-element.22), channel_id=1, source_target_pairs={{4,8},{8,4},{12,16},{16,12},{20,24},{24,20},{28,32},{32,28},{36,40... | collective-permute-start | bytes 49160 | tf_op jit(solution)/shard_map/ppermute | solution.py:430

commit v2 on v1

--- a/solution.py
+++ b/solution.py
@@ -337,7 +337,7 @@
 
 def relax_kernel(
     layers, table,
-    pattern_ref, pack_ref, coef_ref, band_ref, half_ref, side_near, side_far, sum_near, sum_far,
+    pattern_ref, pack_ref, coef_ref, band_ref, half_ref, side_far, side_near, sum_far, sum_near,
     out_ref, next_own, next_band, next_side,
 ):
     lane = lanes()
@@ -466,10 +466,10 @@
         "vvvvvv",
         field, coef, pattern, to_near, from_near, from_far,
     )
-    sum_near = swap(sum_near, "leaf", 0)
-    sum_far = swap(sum_far, "leaf", 1)
     side_near = swap(pack, "gy", 0)
     side_far = swap(pack, "gy", 1)
+    sum_far = swap(sum_far, "leaf", 1)
+    sum_near = swap(sum_near, "leaf", 0)
     (half,) = call(
         functools.partial(own_kernel, layers, table),
         [(256, LANES)],
@@ -480,7 +480,7 @@
         functools.partial(relax_kernel, layers, table),
         [(layers, 64, BRICKS_DEV)],
         "vvvvvvvvv",
-        pattern, pack, coef, band, half, side_near, side_far, sum_near, sum_far,
+        pattern, pack, coef, band, half, side_far, side_near, sum_far, sum_near,
         scratch=[pltpu.VMEM((rows, LANES), F32) for rows in (256, 128, 256)],
     )
     return out

time: 34.7 us -> 32.6 us (0.939)
  the two profiles are of different devices: /device:TPU:32 before, /device:TPU:35 now
where the time goes in v2:
time: 32.6 us; the launch traced here: 32.3 us
  starting transfers between devices  26.7 us (82%)
  Pallas kernels  3.53 us (11%)
  waiting for transfers between devices  1.33 us (4%)
  between operations  0.75 us (2%)
    ppermute x6, starting transfers between devices, swap(): return lax.ppermute(block, axis, route)  26.7 us
    pallas_call x4, Pallas kernels, call(): pl.pallas_call(kernel, out_shape=[jax.ShapeDtypeStruct(s, F32) for s in s...  3.53 us
    ppermute x6, waiting for transfers between devices, swap(): return lax.ppermute(block, axis, route)  1.33 us
  transfers between devices with their start and end apart: 6, of which 2 were waited for; matrix products, arithmetic and copies ran while one was open for 0% of the time, Pallas kernels for 1%

profile of v2, /device:TPU:35, one launch (start us, length us, event | category | flops | bytes accessed | tf_op | source)
XLA Modules:
  0.0 32.3 jit_solution(1374061782822727186)
XLA Ops:
  0.7 0.0 copy-start
  0.7 1.1 %shard_map.55 = (f32[104,128]{1,0:T(8,128)S(1)}, f32[104,128]{1,0:T(8,128)S(1)}, f32[2,64,320]{2,1,0:T(8,128)S(1)}, f32[64,320]{1,0:T(8,128)S(1)}) custom-call(f32[2,64,320]{2,1,0:T(8,128)} %field_hbm.1, f32[64,320]{1,0:T(8,128)} %coef_hbm.1, s32[320]{0:T(512)} %owner_hbm.1, s32[1]{0:T(128)S(6)} %copy.6.counts_ref), custom_call_target="tpu_custom_call" | custom-call | bytes 247044 | tf_op jit(solution)/shard_map/pallas_call | solution.py:437
  1.8 4.6 %collective-permute-start.1 = (f32[104,128]{1,0:T(8,128)S(1)}, f32[104,128]{1,0:T(8,128)S(1)}, u32[]{:S(2)}, u32[]{:S(2)}) collective-permute-start(f32[104,128]{1,0:T(8,128)S(1)} %get-tuple-element.17), channel_id=1, source_target_pairs={{4,8},{8,4},{12,16},{16,12},{20,24},{24,20},{28,32},{32,28},{36,40... | collective-permute-start | bytes 159752 | tf_op jit(solution)/shard_map/ppermute | solution.py:430
  6.4 8.3 %collective-permute-start = (f32[104,128]{1,0:T(8,128)S(1)}, f32[104,128]{1,0:T(8,128)S(1)}, u32[]{:S(2)}, u32[]{:S(2)}) collective-permute-start(f32[104,128]{1,0:T(8,128)S(1)} %get-tuple-element.16.kept_ref), channel_id=1, source_target_pairs={{0,4},{4,0},{8,12},{12,8},{16,20},{20,16},{24,28},{28,24},{32,36},... | collective-permute-start | bytes 159752 | tf_op jit(solution)/shard_map/ppermute | solution.py:430
  14.7 0.0 collective-permute-done.1.far_ref
  14.7 0.9 %collective-permute-done.near_ref = f32[104,128]{1,0:T(8,128)S(1)} collective-permute-done((f32[104,128]{1,0:T(8,128)S(1)}, f32[104,128]{1,0:T(8,128)S(1)}, u32[]{:S(2)}, u32[]{:S(2)}) %collective-permute-start) | collective-permute-done | bytes 53280 | tf_op jit(solution)/shard_map/ppermute | solution.py:430
  15.5 0.0 copy-done
  15.5 0.6 %shard_map.56 = (f32[320,128]{1,0:T(8,128)S(1)}, f32[128,128]{1,0:T(8,128)S(1)}, f32[192,128]{1,0:T(8,128)S(1)}, f32[32,128]{1,0:T(8,128)S(1)}, f32[32,128]{1,0:T(8,128)S(1)}) custom-call(f32[2,64,320]{2,1,0:T(8,128)S(1)} %get-tuple-element.14.field_ref, f32[64,320]{1,0:T(8,128)S(1)} %get-tuple-element.15.coef_ref, s32[6,256]{1,0:T(8,128)S(1)} %copy-done, ...), custom_call_target="tpu_custom_call" | custom-call | bytes 411648 | tf_op jit(solution)/shard_map/pallas_call | solution.py:437
  16.2 2.2 %collective-permute-start.3 = (f32[320,128]{1,0:T(8,128)S(1)}, f32[320,128]{1,0:T(8,128)S(1)}, u32[]{:S(2)}, u32[]{:S(2)}) collective-permute-start(f32[320,128]{1,0:T(8,128)S(1)} %get-tuple-element.18.pack_ref), channel_id=1, source_target_pairs={{0,1},{1,0},{2,3},{3,2},{4,5},{5,4},{6,7},{7,6},{8,9},{9,8},{10,11... | collective-permute-start | bytes 491528 | tf_op jit(solution)/shard_map/ppermute | solution.py:430
  18.3 3.8 %collective-permute-start.2 = (f32[320,128]{1,0:T(8,128)S(1)}, f32[320,128]{1,0:T(8,128)S(1)}, u32[]{:S(2)}, u32[]{:S(2)}) collective-permute-start(f32[320,128]{1,0:T(8,128)S(1)} %get-tuple-element.18.pack_ref), channel_id=1, source_target_pairs={{1,2},{2,1},{5,6},{6,5},{9,10},{10,9},{13,14},{14,13},{17,18},{18,... | collective-permute-start | bytes 491528 | tf_op jit(solution)/shard_map/ppermute | solution.py:430
  22.1 1.9 %collective-permute-start.4 = (f32[32,128]{1,0:T(8,128)S(1)}, f32[32,128]{1,0:T(8,128)S(1)}, u32[]{:S(2)}, u32[]{:S(2)}) collective-permute-start(f32[32,128]{1,0:T(8,128)S(1)} %get-tuple-element.21), channel_id=1, source_target_pairs={{4,8},{8,4},{12,16},{16,12},{20,24},{24,20},{28,32},{32,28},{36,40... | collective-permute-start | bytes 49160 | tf_op jit(solution)/shard_map/ppermute | solution.py:430
  24.1 6.0 %collective-permute-start.5 = (f32[32,128]{1,0:T(8,128)S(1)}, f32[32,128]{1,0:T(8,128)S(1)}, u32[]{:S(2)}, u32[]{:S(2)}) collective-permute-start(f32[32,128]{1,0:T(8,128)S(1)} %get-tuple-element.22), channel_id=1, source_target_pairs={{0,4},{4,0},{8,12},{12,8},{16,20},{20,16},{24,28},{28,24},{32,36},... | collective-permute-start | bytes 49160 | tf_op jit(solution)/shard_map/ppermute | solution.py:430
  30.0 0.3 %shard_map.57.half_ref = f32[256,128]{1,0:T(8,128)S(1)} custom-call(s32[6,256]{1,0:T(8,128)S(1)} %copy-done, f32[320,128]{1,0:T(8,128)S(1)} %get-tuple-element.18.pack_ref, f32[128,128]{1,0:T(8,128)S(1)} %get-tuple-element.19.coef_ref, f32[192,128]{1,0:T(8,128)S(1)} %get-tuple-element.20.band_ref), custom_call_target="tpu_custom_call" | custom-call | bytes 333824 | tf_op jit(solution)/shard_map/pallas_call | solution.py:437
  30.4 0.0 collective-permute-done.4.sum_far
  30.4 0.5 %collective-permute-done.5.sum_near = f32[32,128]{1,0:T(8,128)S(1)} collective-permute-done((f32[32,128]{1,0:T(8,128)S(1)}, f32[32,128]{1,0:T(8,128)S(1)}, u32[]{:S(2)}, u32[]{:S(2)}) %collective-permute-start.5) | collective-permute-done | bytes 16416 | tf_op jit(solution)/shard_map/ppermute | solution.py:430
  30.9 0.0 collective-permute-done.3.side_near
  30.9 0.0 collective-permute-done.2.side_far
  30.9 1.4 %shard_map.58 = f32[2,64,256]{2,1,0:T(8,128)} custom-call(s32[6,256]{1,0:T(8,128)S(1)} %copy-done, f32[320,128]{1,0:T(8,128)S(1)} %get-tuple-element.18.pack_ref, f32[128,128]{1,0:T(8,128)S(1)} %get-tuple-element.19.coef_ref, f32[192,128]{1,0:T(8,128)S(1)} %get-tuple-element.20.band_ref, f32[256,128]{1,0:T(8,128)S(1)} %shard_map.57.half_ref, ...), custom_call_target="tpu_custom_call" | custom-call | bytes 825344 | tf_op jit(solution)/shard_map/pallas_call | solution.py:437
Async XLA Ops:
  0.7 14.9 %copy-start = (s32[6,256]{1,0:T(8,128)S(1)}, s32[6,256]{1,0:T(8,128)}, u32[]{:S(2)}) copy-start(s32[6,256]{1,0:T(8,128)} %pattern_ref.5) | copy-start | bytes 18436
  1.8 12.9 %collective-permute-start.1 = (f32[104,128]{1,0:T(8,128)S(1)}, f32[104,128]{1,0:T(8,128)S(1)}, u32[]{:S(2)}, u32[]{:S(2)}) collective-permute-start(f32[104,128]{1,0:T(8,128)S(1)} %get-tuple-element.17), channel_id=1, source_target_pairs={{4,8},{8,4},{12,16},{16,12},{20,24},{24,20},{28,32},{32,28},{36,40... | collective-permute-start | bytes 159752 | tf_op jit(solution)/shard_map/ppermute | solution.py:430
  6.4 9.2 %collective-permute-start = (f32[104,128]{1,0:T(8,128)S(1)}, f32[104,128]{1,0:T(8,128)S(1)}, u32[]{:S(2)}, u32[]{:S(2)}) collective-permute-start(f32[104,128]{1,0:T(8,128)S(1)} %get-tuple-element.16.kept_ref), channel_id=1, source_target_pairs={{0,4},{4,0},{8,12},{12,8},{16,20},{20,16},{24,28},{28,24},{32,36},... | collective-permute-start | bytes 159752 | tf_op jit(solution)/shard_map/ppermute | solution.py:430
  16.2 14.7 %collective-permute-start.3 = (f32[320,128]{1,0:T(8,128)S(1)}, f32[320,128]{1,0:T(8,128)S(1)}, u32[]{:S(2)}, u32[]{:S(2)}) collective-permute-start(f32[320,128]{1,0:T(8,128)S(1)} %get-tuple-element.18.pack_ref), channel_id=1, source_target_pairs={{0,1},{1,0},{2,3},{3,2},{4,5},{5,4},{6,7},{7,6},{8,9},{9,8},{10,11... | collective-permute-start | bytes 491528 | tf_op jit(solution)/shard_map/ppermute | solution.py:430
  18.3 12.5 %collective-permute-start.2 = (f32[320,128]{1,0:T(8,128)S(1)}, f32[320,128]{1,0:T(8,128)S(1)}, u32[]{:S(2)}, u32[]{:S(2)}) collective-permute-start(f32[320,128]{1,0:T(8,128)S(1)} %get-tuple-element.18.pack_ref), channel_id=1, source_target_pairs={{1,2},{2,1},{5,6},{6,5},{9,10},{10,9},{13,14},{14,13},{17,18},{18,... | collective-permute-start | bytes 491528 | tf_op jit(solution)/shard_map/ppermute | solution.py:430
  22.1 8.3 %collective-permute-start.4 = (f32[32,128]{1,0:T(8,128)S(1)}, f32[32,128]{1,0:T(8,128)S(1)}, u32[]{:S(2)}, u32[]{:S(2)}) collective-permute-start(f32[32,128]{1,0:T(8,128)S(1)} %get-tuple-element.21), channel_id=1, source_target_pairs={{4,8},{8,4},{12,16},{16,12},{20,24},{24,20},{28,32},{32,28},{36,40... | collective-permute-start | bytes 49160 | tf_op jit(solution)/shard_map/ppermute | solution.py:430
  24.1 6.8 %collective-permute-start.5 = (f32[32,128]{1,0:T(8,128)S(1)}, f32[32,128]{1,0:T(8,128)S(1)}, u32[]{:S(2)}, u32[]{:S(2)}) collective-permute-start(f32[32,128]{1,0:T(8,128)S(1)} %get-tuple-element.22), channel_id=1, source_target_pairs={{0,4},{4,0},{8,12},{12,8},{16,20},{20,16},{24,28},{28,24},{32,36},... | collective-permute-start | bytes 49160 | tf_op jit(solution)/shard_map/ppermute | solution.py:430

commit v3 on v2

--- a/solution.py
+++ b/solution.py
@@ -337,13 +337,20 @@
 
 def relax_kernel(
     layers, table,
-    pattern_ref, pack_ref, coef_ref, band_ref, half_ref, side_far, side_near, sum_far, sum_near,
-    out_ref, next_own, next_band, next_side,
+    pattern_ref, pack_ref, coef_ref, band_ref, half_ref, column_ref, sum_far, sum_near,
+    out_ref, next_own, next_band, next_side, lower_ref, upper_ref, sems,
 ):
     lane = lanes()
     group = lax.axis_index("gy")
     even = is_even("leaf")
-    even_group = is_even("gy")
+    groups = Y // layers
+    lower_at, upper_at = jnp.maximum(group - 1, 0), jnp.minimum(group + 1, groups - 1)
+    copies = [
+        pltpu.make_async_copy(column_ref.at[lower_at], lower_ref, sems.at[0]),
+        pltpu.make_async_copy(column_ref.at[upper_at], upper_ref, sems.at[1]),
+    ]
+    for copy in copies:
+        copy.start()
     kinds = own_kinds(pattern_ref)
     w_lower, w_first, w_second, w_upper = (weights_at(table, group, layers, o) for o in (-1, 0, 1, 2))
 
@@ -355,8 +362,9 @@
         return (1.0 - OMEGA) * now + gain * push
 
     def beside(upper, at):
-        near, far = side_near[at, :], side_far[at, :]
-        return jnp.where(even_group, near, far) if upper else jnp.where(even_group, far, near)
+        if upper:
+            return jnp.where(group < groups - 1, upper_ref[at, :], 0.0)
+        return jnp.where(group > 0, lower_ref[at, :], 0.0)
 
     def side(upper, a, c, t):
         return beside(upper, pl.ds(128 * a + 64 * c + 8 * t, 8))
@@ -365,6 +373,9 @@
         tile = beside(upper, pl.ds(256 + 32 * a + 8 * (t % 4), 8))
         tile = pltpu.roll(tile, 64, 1) if t >= 4 else tile
         return jnp.where(lane < 64, tile, 0.0)
+
+    for copy in copies:
+        copy.wait()
 
     for a in range(2):
         weights = w_second if a else w_first
@@ -466,8 +477,7 @@
         "vvvvvv",
         field, coef, pattern, to_near, from_near, from_far,
     )
-    side_near = swap(pack, "gy", 0)
-    side_far = swap(pack, "gy", 1)
+    column = pltpu.with_memory_space_constraint(lax.all_gather(pack, "gy"), pltpu.HBM)
     sum_far = swap(sum_far, "leaf", 1)
     sum_near = swap(sum_near, "leaf", 0)
     (half,) = call(
@@ -479,9 +489,10 @@
     (out,) = call(
         functools.partial(relax_kernel, layers, table),
         [(layers, 64, BRICKS_DEV)],
-        "vvvvvvvvv",
-        pattern, pack, coef, band, half, side_far, side_near, sum_far, sum_near,
-        scratch=[pltpu.VMEM((rows, LANES), F32) for rows in (256, 128, 256)],
+        "vvvvvhvv",
+        pattern, pack, coef, band, half, column, sum_far, sum_near,
+        scratch=[pltpu.VMEM((rows, LANES), F32) for rows in (256, 128, 256, 320, 320)]
+        + [pltpu.SemaphoreType.DMA((2,))],
     )
     return out
 

time: 32.6 us -> 41.1 us (1.26)
  the two profiles are of different devices: /device:TPU:35 before, /device:TPU:34 now
where the time goes in v3:
time: 41.1 us; the launch traced here: 40.9 us
  starting transfers between devices  19.8 us (48%)
  blocking collectives  14.6 us (36%)
  Pallas kernels  4.54 us (11%)
  waiting for transfers between devices  1.2 us (3%)
  between operations  0.74 us (2%)
    ppermute x4, starting transfers between devices, swap(): return lax.ppermute(block, axis, route)  19.8 us
    all_gather x1, blocking collectives, local(): lax.all_gather(pack, 'gy')  14.6 us
    pallas_call x4, Pallas kernels, call(): pl.pallas_call(kernel, out_shape=[jax.ShapeDtypeStruct(s, F32) for s in s...  4.54 us
    ppermute x4, waiting for transfers between devices, swap(): return lax.ppermute(block, axis, route)  1.2 us
  transfers between devices with their start and end apart: 4, of which 1 were waited for; matrix products, arithmetic and copies ran while one was open for 0% of the time, Pallas kernels for 1%

profile of v3, /device:TPU:34, one launch (start us, length us, event | category | flops | bytes accessed | tf_op | source)
XLA Modules:
  0.0 40.9 jit_solution(1337470252533928459)
XLA Ops:
  0.7 0.0 copy-start
  0.7 1.1 %shard_map.55 = (f32[104,128]{1,0:T(8,128)S(1)}, f32[104,128]{1,0:T(8,128)S(1)}, f32[2,64,320]{2,1,0:T(8,128)S(1)}, f32[64,320]{1,0:T(8,128)S(1)}) custom-call(f32[2,64,320]{2,1,0:T(8,128)} %field_hbm.1, f32[64,320]{1,0:T(8,128)} %coef_hbm.1, s32[320]{0:T(512)} %owner_hbm.1, s32[1]{0:T(128)S(6)} %copy.6.counts_ref), custom_call_target="tpu_custom_call" | custom-call | bytes 247044 | tf_op jit(solution)/shard_map/pallas_call | solution.py:448
  1.8 10.3 %collective-permute-start.1 = (f32[104,128]{1,0:T(8,128)S(1)}, f32[104,128]{1,0:T(8,128)S(1)}, u32[]{:S(2)}, u32[]{:S(2)}) collective-permute-start(f32[104,128]{1,0:T(8,128)S(1)} %get-tuple-element.17), channel_id=1, source_target_pairs={{4,8},{8,4},{12,16},{16,12},{20,24},{24,20},{28,32},{32,28},{36,40... | collective-permute-start | bytes 159752 | tf_op jit(solution)/shard_map/ppermute | solution.py:441
  12.1 1.9 %collective-permute-start = (f32[104,128]{1,0:T(8,128)S(1)}, f32[104,128]{1,0:T(8,128)S(1)}, u32[]{:S(2)}, u32[]{:S(2)}) collective-permute-start(f32[104,128]{1,0:T(8,128)S(1)} %get-tuple-element.16.kept_ref), channel_id=1, source_target_pairs={{0,4},{4,0},{8,12},{12,8},{16,20},{20,16},{24,28},{28,24},{32,36},... | collective-permute-start | bytes 159752 | tf_op jit(solution)/shard_map/ppermute | solution.py:441
  14.0 0.0 collective-permute-done.1.far_ref
  14.0 1.2 %collective-permute-done.near_ref = f32[104,128]{1,0:T(8,128)S(1)} collective-permute-done((f32[104,128]{1,0:T(8,128)S(1)}, f32[104,128]{1,0:T(8,128)S(1)}, u32[]{:S(2)}, u32[]{:S(2)}) %collective-permute-start) | collective-permute-done | bytes 53280 | tf_op jit(solution)/shard_map/ppermute | solution.py:441
  15.2 0.0 copy-done
  15.2 0.6 %shard_map.56 = (f32[320,128]{1,0:T(8,128)S(1)}, f32[128,128]{1,0:T(8,128)S(1)}, f32[192,128]{1,0:T(8,128)S(1)}, f32[32,128]{1,0:T(8,128)S(1)}, f32[32,128]{1,0:T(8,128)S(1)}) custom-call(f32[2,64,320]{2,1,0:T(8,128)S(1)} %get-tuple-element.14.field_ref, f32[64,320]{1,0:T(8,128)S(1)} %get-tuple-element.15.coef_ref, s32[6,256]{1,0:T(8,128)S(1)} %copy-done, ...), custom_call_target="tpu_custom_call" | custom-call | bytes 411648 | tf_op jit(solution)/shard_map/pallas_call | solution.py:448
  15.8 5.6 %collective-permute-start.2 = (f32[32,128]{1,0:T(8,128)S(1)}, f32[32,128]{1,0:T(8,128)S(1)}, u32[]{:S(2)}, u32[]{:S(2)}) collective-permute-start(f32[32,128]{1,0:T(8,128)S(1)} %get-tuple-element.21), channel_id=1, source_target_pairs={{4,8},{8,4},{12,16},{16,12},{20,24},{24,20},{28,32},{32,28},{36,40... | collective-permute-start | bytes 49160 | tf_op jit(solution)/shard_map/ppermute | solution.py:441
  21.5 1.9 %collective-permute-start.3 = (f32[32,128]{1,0:T(8,128)S(1)}, f32[32,128]{1,0:T(8,128)S(1)}, u32[]{:S(2)}, u32[]{:S(2)}) collective-permute-start(f32[32,128]{1,0:T(8,128)S(1)} %get-tuple-element.22), channel_id=1, source_target_pairs={{0,4},{4,0},{8,12},{12,8},{16,20},{20,16},{24,28},{28,24},{32,36},... | collective-permute-start | bytes 49160 | tf_op jit(solution)/shard_map/ppermute | solution.py:441
  23.4 14.6 %all-gather = f32[1280,128]{1,0:T(8,128)} all-gather(f32[320,128]{1,0:T(8,128)S(1)} %get-tuple-element.18.pack_ref), channel_id=2, replica_groups=mesh['leaf'=128,'gy'=4] {'gy'}, dimensions={0}, use_global_device_ids=true | all-gather | bytes 819200 | tf_op jit(solution)/shard_map/all_gather | solution.py:480
  38.1 0.3 shard_map.57.half_ref
  38.4 0.0 collective-permute-done.2.sum_far
  38.4 0.0 collective-permute-done.3.sum_near
  38.4 2.4 %shard_map.58 = f32[2,64,256]{2,1,0:T(8,128)} custom-call(s32[6,256]{1,0:T(8,128)S(1)} %copy-done, f32[320,128]{1,0:T(8,128)S(1)} %get-tuple-element.18.pack_ref, f32[128,128]{1,0:T(8,128)S(1)} %get-tuple-element.19.coef_ref, f32[192,128]{1,0:T(8,128)S(1)} %get-tuple-element.20.band_ref, f32[256,128]{1,0:T(8,128)S(1)} %shard_map.57.half_ref, ...), custom_call_target="tpu_custom_call" | custom-call | bytes 1153024 | tf_op jit(solution)/shard_map/pallas_call | solution.py:448
Async XLA Ops:
  0.7 14.6 %copy-start = (s32[6,256]{1,0:T(8,128)S(1)}, s32[6,256]{1,0:T(8,128)}, u32[]{:S(2)}) copy-start(s32[6,256]{1,0:T(8,128)} %pattern_ref.5) | copy-start | bytes 18436
  1.8 12.2 %collective-permute-start.1 = (f32[104,128]{1,0:T(8,128)S(1)}, f32[104,128]{1,0:T(8,128)S(1)}, u32[]{:S(2)}, u32[]{:S(2)}) collective-permute-start(f32[104,128]{1,0:T(8,128)S(1)} %get-tuple-element.17), channel_id=1, source_target_pairs={{4,8},{8,4},{12,16},{16,12},{20,24},{24,20},{28,32},{32,28},{36,40... | collective-permute-start | bytes 159752 | tf_op jit(solution)/shard_map/ppermute | solution.py:441
  12.1 3.1 %collective-permute-start = (f32[104,128]{1,0:T(8,128)S(1)}, f32[104,128]{1,0:T(8,128)S(1)}, u32[]{:S(2)}, u32[]{:S(2)}) collective-permute-start(f32[104,128]{1,0:T(8,128)S(1)} %get-tuple-element.16.kept_ref), channel_id=1, source_target_pairs={{0,4},{4,0},{8,12},{12,8},{16,20},{20,16},{24,28},{28,24},{32,36},... | collective-permute-start | bytes 159752 | tf_op jit(solution)/shard_map/ppermute | solution.py:441
  15.8 22.6 %collective-permute-start.2 = (f32[32,128]{1,0:T(8,128)S(1)}, f32[32,128]{1,0:T(8,128)S(1)}, u32[]{:S(2)}, u32[]{:S(2)}) collective-permute-start(f32[32,128]{1,0:T(8,128)S(1)} %get-tuple-element.21), channel_id=1, source_target_pairs={{4,8},{8,4},{12,16},{16,12},{20,24},{24,20},{28,32},{32,28},{36,40... | collective-permute-start | bytes 49160 | tf_op jit(solution)/shard_map/ppermute | solution.py:441
  21.5 16.9 %collective-permute-start.3 = (f32[32,128]{1,0:T(8,128)S(1)}, f32[32,128]{1,0:T(8,128)S(1)}, u32[]{:S(2)}, u32[]{:S(2)}) collective-permute-start(f32[32,128]{1,0:T(8,128)S(1)} %get-tuple-element.22), channel_id=1, source_target_pairs={{0,4},{4,0},{8,12},{12,8},{16,20},{20,16},{24,28},{28,24},{32,36},... | collective-permute-start | bytes 49160 | tf_op jit(solution)/shard_map/ppermute | solution.py:441

commit v4 on v2

--- a/solution.py
+++ b/solution.py
@@ -105,16 +105,19 @@
     return jnp.concatenate([half, jnp.zeros((8, 3 * LANES - OLD_SLOTS), F32)], axis=1)
 
 
-def face_indices(pattern_rows):
+def face_rows(pattern_rows):
     sub = rows()
-    kinds = (
+    return (
         pattern_rows[0],
         pattern_rows[1],
         jnp.where(sub < 4, pattern_rows[3], pattern_rows[2]),
         jnp.where((sub & 3) == 3, pattern_rows[4], pattern_rows[5]),
     )
+
+
+def face_indices(pattern_rows):
     out = []
-    for w in kinds:
+    for w in face_rows(pattern_rows):
         source = w >> 7
         own = (source == 2) | (source == 3)
         beside = jnp.where(w >= 2 * BRICKS_DEV, w - (2 * BRICKS_DEV - SPILL), w - (BRICKS_DEV - SPILL))
@@ -124,14 +127,17 @@
 
 
 def face(kind, tiles):
+    if len(tiles) == 1:
+        return pick(tiles[0], kind[0])
     lane, first, second = kind
     return jnp.where(first, pick(tiles[0], lane), jnp.where(second, pick(tiles[1], lane), pick(tiles[2], lane)))
 
 
 class Sources:
-    def __init__(self, read):
+    def __init__(self, read, count=3):
         sub = rows()
-        self.tile = [[read(c, t) for t in range(TILES)] for c in range(3)]
+        self.columns = range(count)
+        self.tile = [[read(c, t) for t in range(TILES)] for c in self.columns]
         self.turned = [[pltpu.roll(v, 4, 0) for v in column] for column in self.tile]
         self.y_edge = [
             [jnp.where(sub < 4, column[2 * i], column[2 * i + 1]) for i in range(4)]
@@ -146,22 +152,22 @@
     total = []
     for t in range(TILES):
         if t < 2:
-            below = face(x_low, [src.tile[c][6 + t] for c in range(3)])
+            below = face(x_low, [src.tile[c][6 + t] for c in src.columns])
         else:
             below = here[t - 2]
         if t >= 6:
-            above = face(x_high, [src.tile[c][t - 6] for c in range(3)])
+            above = face(x_high, [src.tile[c][t - 6] for c in src.columns])
         else:
             above = here[t + 2]
         total.append(below + above)
     for i in range(4):
-        edge = pltpu.roll(face(y_both, [src.y_edge[c][i] for c in range(3)]), 4, 0)
+        edge = pltpu.roll(face(y_both, [src.y_edge[c][i] for c in src.columns]), 4, 0)
         first, second = turned[2 * i], turned[2 * i + 1]
         middle = jnp.where(low, first, second)
         total[2 * i] += jnp.where(low, edge, first) + middle
         total[2 * i + 1] += jnp.where(low, second, edge) + middle
     for t in range(TILES):
-        edge = face(z_both, [src.turned[c][t] for c in range(3)])
+        edge = face(z_both, [src.turned[c][t] for c in src.columns])
         total[t] += pltpu.roll(jnp.where(k == 3, edge, here[t]), 1, 0)
         total[t] += pltpu.roll(jnp.where(k == 0, edge, here[t]), 7, 0)
     return total
@@ -171,124 +177,205 @@
     return (lax.axis_index(axis) & 1) == 0
 
 
-def send_kernel(
-    field_hbm, coef_hbm, owner_hbm, counts_ref,
-    near_ref, far_ref, field_ref, coef_ref,
-    owner_ref, sems,
+def ends(ref, lead, r, live, next_side):
+    lane = lanes()
+    front, back = old_tile(ref, lead, r, 0), old_tile(ref, lead, r + 4, 0)
+    prev = jnp.where(lane < 64, front, pltpu.roll(back, 64, 1))
+    early = lane >= live - 192
+    front = jnp.where(early, old_tile(ref, lead, r, 1), old_tile(ref, lead, r, 2))
+    back = jnp.where(early, old_tile(ref, lead, r + 4, 1), old_tile(ref, lead, r + 4, 2))
+    next = jnp.where(lane < 64, spin(front, 64 - live), spin(back, 128 - live))
+    return jnp.where(next_side, next, prev)
+
+
+def near_kernel(
+    field_hbm, coef_hbm, owner_hbm, counts_ref, near_ref, field_ref, coef_ref, owner_ref, sems
 ):
     pairs = ((owner_hbm, owner_ref), (field_hbm, field_ref), (coef_hbm, coef_ref))
     copies = [pltpu.make_async_copy(a, b, sems.at[i]) for i, (a, b) in enumerate(pairs)]
     for copy in copies:
         copy.start()
+    sub = rows()
+    even = is_even("leaf")
+    live = counts_ref[0]
+    copies[0].wait()
+    to_prev, to_next = spill_counts(owner_ref, live, lax.axis_index("leaf"))
+    handed = jnp.where(even, to_next, to_prev)
+    kept = jnp.where(sub == 1, live, jnp.where(sub == 2, to_prev, to_next))
+    near_ref[pl.ds(96, 8), :] = jnp.where(sub == 0, handed, kept).astype(F32)
+    for a in range(3):
+        ref, lead = (field_ref, a) if a < 2 else (coef_ref, None)
+        if a != 1:
+            copies[1 + a // 2].wait()
+        for r in range(4):
+            near_ref[pl.ds(32 * a + 8 * r, 8), :] = ends(ref, lead, r, live, even)
+
+
+def pattern_row(pattern_ref, direction, c):
+    row = pattern_ref[pl.ds(direction, 1), pl.ds(LANES * c, LANES)]
+    return jnp.broadcast_to(row, (8, LANES))
+
+
+def pack_quarters(total, half, first):
+    lane = lanes()
+    base = jnp.where(first, 0, 32)
+    q = [spin(total[2 * i + half], base + 32 * i) for i in range(4)]
+    return jnp.where(
+        lane < 64, jnp.where(lane < 32, q[0], q[1]), jnp.where(lane < 96, q[2], q[3])
+    )
+
+
+def far_kernel(field_ref, coef_ref, pattern_ref, kept_ref, near_ref, far_ref, own_ref, band_ref):
     lane, sub = lanes(), rows()
     even = is_even("leaf")
-    copies[0].wait()
-    live = counts_ref[0]
-    to_prev, to_next = spill_counts(owner_ref, live, lax.axis_index("leaf"))
-    kept = jnp.where(sub == 1, live, jnp.where(sub == 2, to_prev, to_next)).astype(F32)
-    prev_count = jnp.where(sub == 0, to_prev.astype(F32), kept)
-    next_count = jnp.where(sub == 0, to_next.astype(F32), kept)
-    near_ref[pl.ds(96, 8), :] = jnp.where(even, next_count, prev_count)
-    far_ref[pl.ds(96, 8), :] = jnp.where(even, prev_count, next_count)
+    live, to_prev, to_next = (kept_ref[96 + i, 0].astype(jnp.int32) for i in (1, 2, 3))
+    from_near = near_ref[96, 0].astype(jnp.int32)
+    stay = live - to_prev - to_next
+    from_far = BRICKS_DEV - stay - from_near
+    from_prev, from_next = jnp.where(even, from_far, from_near), jnp.where(even, from_near, from_far)
+    drift = to_prev - from_prev
+    tail = from_prev + stay - LANES
+    handed = jnp.where(even, to_prev, to_next)
+    values = (handed, live, to_prev, to_next, from_prev, from_next, 0, 0)
+    counts = jnp.zeros((8, LANES), jnp.int32)
+    for i, value in enumerate(values):
+        counts = jnp.where(sub == i, value, counts)
+    far_ref[pl.ds(96, 8), :] = counts.astype(F32)
+    spill = (lane >= SPILL - to_prev) & (lane < SPILL + to_next)
+    near_low, near_high = jnp.where(even, SPILL, 0), jnp.where(even, 2 * SPILL, SPILL)
+    near_lanes = (lane >= near_low) & (lane < near_high)
+    arrive_by = jnp.where(even, tail, from_prev - 64)
+    band_by = jnp.where(even, SPILL + to_next - from_next, from_prev - to_prev - SPILL)
     for a in range(3):
         ref, lead = (field_ref, a) if a < 2 else (coef_ref, None)
-        if a == 0:
-            copies[1].wait()
-        if a == 2:
-            copies[2].wait()
         for r in range(4):
-            at = pl.ds(32 * a + 8 * r, 8)
-            front = old_tile(ref, lead, r, 0)
-            back = old_tile(ref, lead, r + 4, 0)
-            prev = jnp.where(lane < 64, front, pltpu.roll(back, 64, 1))
-            early = lane >= live - 192
-            front = jnp.where(early, old_tile(ref, lead, r, 1), old_tile(ref, lead, r, 2))
-            back = jnp.where(early, old_tile(ref, lead, r + 4, 1), old_tile(ref, lead, r + 4, 2))
-            next = jnp.where(lane < 64, spin(front, 64 - live), spin(back, 128 - live))
-            near_ref[at, :] = jnp.where(even, next, prev)
-            far_ref[at, :] = jnp.where(even, prev, next)
-
-
-def place_kernel(
-    field_ref, coef_ref, pattern_ref, kept_ref, near_ref, far_ref,
-    pack_ref, coef_out, band_out, sum_near, sum_far,
-):
-    lane = lanes()
-    even = is_even("leaf")
-    live, to_prev, to_next = (kept_ref[96 + i, 0].astype(jnp.int32) for i in (1, 2, 3))
-    from_near, from_far = near_ref[96, 0], far_ref[96, 0]
-    from_prev = jnp.where(even, from_far, from_near).astype(jnp.int32)
-    from_next = jnp.where(even, from_near, from_far).astype(jnp.int32)
-    stay = live - to_prev - to_next
-    drift = to_prev - from_prev
-    tail = from_prev + stay - LANES
-    for a in range(3):
-        ref, lead = (field_ref, a) if a < 2 else (coef_ref, None)
+            far_ref[pl.ds(32 * a + 8 * r, 8), :] = ends(ref, lead, r, live, jnp.logical_not(even))
         for t in range(TILES):
             h = 64 * (t // 4)
-            at = pl.ds(32 * a + 8 * (t % 4), 8)
-            near, far = near_ref[at, :], far_ref[at, :]
-            before, after = jnp.where(even, far, near), jnp.where(even, near, far)
+            near = near_ref[pl.ds(32 * a + 8 * (t % 4), 8), :]
             x0, x1, x2 = (old_tile(ref, lead, t, c) for c in range(3))
             r0, r1, r2 = spin(x0, -drift), spin(x1, -drift), spin(x2, -drift)
             own0 = jnp.where(lane < LANES - drift, r0, r1)
             own1 = jnp.where(lane < -drift, r0, jnp.where(lane < LANES - drift, r1, r2))
-            own0 = jnp.where(lane < from_prev, spin(before, from_prev - 64 - h), own0)
-            own1 = jnp.where(lane >= tail, spin(after, tail - h), own1)
-            low = jnp.where(
-                lane < SPILL - to_prev,
-                spin(before, from_prev - to_prev - SPILL - h),
-                spin(x0, SPILL - to_prev),
-            )
-            end = jnp.where(lane >= live - to_next - LANES, x1, x2)
-            high = jnp.where(
-                lane < SPILL + to_next,
-                spin(end, SPILL + to_next - live),
-                spin(after, SPILL + to_next - from_next - h),
-            )
-            band = jnp.where(lane < SPILL, low, jnp.where(lane < 2 * SPILL, high, 0.0))
+            arrived = spin(near, arrive_by - h)
+            own0 = jnp.where(lane < from_prev, jnp.where(even, 0.0, arrived), own0)
+            own1 = jnp.where(lane >= tail, jnp.where(even, arrived, 0.0), own1)
+            last = jnp.where(lane >= live - to_next - LANES, x1, x2)
+            gone = jnp.where(lane < SPILL, spin(x0, SPILL - to_prev), spin(last, SPILL + to_next - live))
+            band = jnp.where(spill, gone, jnp.where(near_lanes, spin(near, band_by - h), 0.0))
+            own_ref[pl.ds(128 * a + 8 * t, 8), :] = own0
+            own_ref[pl.ds(128 * a + 64 + 8 * t, 8), :] = own1
+            band_ref[pl.ds(64 * a + 8 * t, 8), :] = band
+    far_rows = [
+        jnp.where(even, pattern_row(pattern_ref, d, 0), pattern_row(pattern_ref, d, 1)) for d in range(6)
+    ]
+    sent = jnp.zeros((8, LANES), jnp.int32)
+    for d in range(6):
+        row = spin(far_rows[d], jnp.where(even, 0, 32))
+        sent = jnp.where(sub == d, row, sent)
+    sent = jnp.where(lane < 32, sent, pltpu.roll(sent, 32, 1))
+    far_ref[pl.ds(104, 8), :] = sent.astype(F32)
+    kinds = face_indices(far_rows)
+    for a in range(2):
+
+        def read(c, t):
+            if c < 2:
+                return own_ref[pl.ds(128 * a + 64 * c + 8 * t, 8), :]
+            return jnp.where(near_lanes, band_ref[pl.ds(64 * a + 8 * t, 8), :], 0.0)
+
+        src = Sources(read)
+        here = [jnp.where(even, src.tile[0][t], src.tile[1][t]) for t in range(TILES)]
+        turned = [jnp.where(even, src.turned[0][t], src.turned[1][t]) for t in range(TILES)]
+        total = neighbour_sum(src, here, turned, kinds)
+        for half in range(2):
+            far_ref[pl.ds(112 + 16 * a + 8 * half, 8), :] = pack_quarters(total, half, even)
+
+
+def place_kernel(
+    pattern_ref, kept_ref, own_ref, band_ref, far_ref,
+    pack_near, pack_far, coef_out, band_out, sum_near, sum_far,
+):
+    lane, sub = lanes(), rows()
+    even = is_even("leaf")
+    even_group = is_even("gy")
+    _, live, to_prev, to_next, from_prev, from_next = (
+        kept_ref[96 + i, 0].astype(jnp.int32) for i in range(6)
+    )
+    tail = from_prev + live - to_prev - to_next - LANES
+    first = jnp.where(even, from_prev, 0)
+    final = jnp.where(even, LANES, tail)
+    stays_low = jnp.where(even, 0, SPILL + to_next)
+    stays_high = jnp.where(even, SPILL - to_prev, 2 * SPILL)
+    stays = (lane >= stays_low) & (lane < stays_high)
+    arrive_by = jnp.where(even, from_prev - 64, tail)
+    band_by = jnp.where(even, from_prev - to_prev - SPILL, SPILL + to_next - from_next)
+    for a in range(3):
+        for t in range(TILES):
+            h = 64 * (t // 4)
+            far = far_ref[pl.ds(32 * a + 8 * (t % 4), 8), :]
+            arrived = spin(far, arrive_by - h)
+            own0 = jnp.where(lane < first, arrived, own_ref[pl.ds(128 * a + 8 * t, 8), :])
+            own1 = jnp.where(lane >= final, arrived, own_ref[pl.ds(128 * a + 64 + 8 * t, 8), :])
+            at = pl.ds(64 * a + 8 * t, 8)
+            band_out[at, :] = jnp.where(stays, spin(far, band_by - h), band_ref[at, :])
             if a < 2:
-                pack_ref[pl.ds(128 * a + 8 * t, 8), :] = own0
-                pack_ref[pl.ds(128 * a + 64 + 8 * t, 8), :] = own1
+                for pack in (pack_near, pack_far):
+                    pack[pl.ds(128 * a + 8 * t, 8), :] = own0
+                    pack[pl.ds(128 * a + 64 + 8 * t, 8), :] = own1
             else:
                 coef_out[pl.ds(8 * t, 8), :] = own0
                 coef_out[pl.ds(64 + 8 * t, 8), :] = own1
-            band_out[pl.ds(64 * a + 8 * t, 8), :] = band
-    edge_rows = []
-    for direction in range(6):
-        first = jnp.broadcast_to(pattern_ref[pl.ds(direction, 1), pl.ds(0, LANES)], (8, LANES))
-        second = jnp.broadcast_to(pattern_ref[pl.ds(direction, 1), pl.ds(LANES, LANES)], (8, LANES))
-        edge_rows.append(jnp.where(lane < 64, first, second))
-    kinds = face_indices(edge_rows)
+    for r in range(4):
+        packed = [
+            jnp.where(
+                lane < 64,
+                band_out[pl.ds(64 * a + 8 * r, 8), :],
+                pltpu.roll(band_out[pl.ds(64 * a + 8 * r + 32, 8), :], 64, 1),
+            )
+            for a in range(2)
+        ]
+        pack_near[pl.ds(256 + 8 * r, 8), :] = jnp.where(even_group, packed[1], packed[0])
+        pack_far[pl.ds(256 + 8 * r, 8), :] = jnp.where(even_group, packed[0], packed[1])
+
+    near_kinds = face_indices(
+        [jnp.where(even, pattern_row(pattern_ref, d, 1), pattern_row(pattern_ref, d, 0)) for d in range(6)]
+    )
+    shift = jnp.where(even, 480, 224)
+    window = [
+        jnp.broadcast_to(far_ref[pl.ds(104 + d, 1), :], (8, LANES)).astype(jnp.int32) - shift
+        for d in range(6)
+    ]
+    window = [jnp.where((w >= 0) & (w < 2 * SPILL), w, LANES - 1) for w in window]
+    far_kinds = [(w,) for w in face_rows(window)]
+    far_low, far_high = jnp.where(even, 0, SPILL), jnp.where(even, SPILL, 2 * SPILL)
+    far_lanes = (lane >= far_low) & (lane < far_high)
+    mine = (lane < 2 * SPILL) & jnp.logical_not(far_lanes)
+    given = far_lanes & (lane >= SPILL - to_prev) & (lane < SPILL + to_next)
+    unpack_by = jnp.where(even, 0, 32)
     for a in range(2):
 
         def read(c, t):
             if c < 2:
-                return pack_ref[pl.ds(128 * a + 64 * c + 8 * t, 8), :]
+                return pack_near[pl.ds(128 * a + 64 * c + 8 * t, 8), :]
             return band_out[pl.ds(64 * a + 8 * t, 8), :]
 
         src = Sources(read)
-        for r in range(4):
-            pack_ref[pl.ds(256 + 32 * a + 8 * r, 8), :] = jnp.where(
-                lane < 64, src.tile[2][r], pltpu.roll(src.tile[2][r + 4], 64, 1)
-            )
-        here = [jnp.where(lane < 64, src.tile[0][t], src.tile[1][t]) for t in range(TILES)]
-        turned = [jnp.where(lane < 64, src.turned[0][t], src.turned[1][t]) for t in range(TILES)]
-        total = neighbour_sum(src, here, turned, kinds)
+        here = [jnp.where(even, src.tile[1][t], src.tile[0][t]) for t in range(TILES)]
+        turned = [jnp.where(even, src.turned[1][t], src.turned[0][t]) for t in range(TILES)]
+        total = neighbour_sum(src, here, turned, near_kinds)
         for half in range(2):
-            at = pl.ds(16 * a + 8 * half, 8)
-            first = [spin(total[2 * q + half], 32 * q) for q in range(4)]
-            last = [spin(total[2 * q + half], 32 * q + 32) for q in range(4)]
-            first, last = (
-                jnp.where(
-                    lane < 64,
-                    jnp.where(lane < 32, values[0], values[1]),
-                    jnp.where(lane < 96, values[2], values[3]),
-                )
-                for values in (first, last)
-            )
-            sum_near[at, :] = jnp.where(even, last, first)
-            sum_far[at, :] = jnp.where(even, first, last)
+            sum_near[pl.ds(16 * a + 8 * half, 8), :] = pack_quarters(total, half, jnp.logical_not(even))
+
+        def meet(_, t):
+            facing = spin(jnp.where(even, src.tile[0][t], src.tile[1][t]), 32)
+            return jnp.where(given, src.tile[2][t], jnp.where(mine, facing, 0.0))
+
+        joint = Sources(meet, 1)
+        total = neighbour_sum(joint, joint.tile[0], joint.turned[0], far_kinds)
+        for t in range(TILES):
+            part = far_ref[pl.ds(112 + 16 * a + 8 * (t % 2), 8), :]
+            part = spin(part, unpack_by - 32 * (t // 2))
+            sum_far[pl.ds(64 * a + 8 * t, 8), :] = jnp.where(far_lanes, total[t] + part, 0.0)
 
 
 def own(ref, a, c, t):
@@ -344,6 +431,8 @@
     group = lax.axis_index("gy")
     even = is_even("leaf")
     even_group = is_even("gy")
+    unpack_by = jnp.where(even, SPILL, 0)
+    near_lanes = (lane >= unpack_by) & (lane < unpack_by + SPILL)
     kinds = own_kinds(pattern_ref)
     w_lower, w_first, w_second, w_upper = (weights_at(table, group, layers, o) for o in (-1, 0, 1, 2))
 
@@ -361,8 +450,8 @@
     def side(upper, a, c, t):
         return beside(upper, pl.ds(128 * a + 64 * c + 8 * t, 8))
 
-    def side_band(upper, a, t):
-        tile = beside(upper, pl.ds(256 + 32 * a + 8 * (t % 4), 8))
+    def side_band(upper, t):
+        tile = beside(upper, pl.ds(256 + 8 * (t % 4), 8))
         tile = pltpu.roll(tile, 64, 1) if t >= 4 else tile
         return jnp.where(lane < 64, tile, 0.0)
 
@@ -376,23 +465,20 @@
         for t in range(TILES):
             now = band_ref[pl.ds(64 * a + 8 * t, 8), :]
             coef = band_ref[pl.ds(128 + 8 * t, 8), :]
-            at = pl.ds(16 * a + 8 * (t % 2), 8)
-            q = t // 2
-            near, far = sum_near[at, :], sum_far[at, :]
-            low, high = jnp.where(even, far, near), jnp.where(even, near, far)
-            low, high = spin(low, -32 * q), spin(high, 32 - 32 * q)
-            total_t = jnp.where(lane < 32, low, jnp.where(lane < 64, high, 0.0))
+            near = sum_near[pl.ds(16 * a + 8 * (t % 2), 8), :]
+            near = spin(near, unpack_by - 32 * (t // 2))
+            total_t = jnp.where(near_lanes, near, sum_far[pl.ds(64 * a + 8 * t, 8), :])
             if a == 0:
-                below, above = side_band(0, 1, t), band_ref[pl.ds(64 + 8 * t, 8), :]
+                below, above = side_band(0, t), band_ref[pl.ds(64 + 8 * t, 8), :]
                 new = step(w_first, now, total_t, below, above, coef, now)
             else:
-                below, above = band_ref[pl.ds(8 * t, 8), :], side_band(1, 0, t)
+                below, above = band_ref[pl.ds(8 * t, 8), :], side_band(1, t)
                 new = step(w_second, now, total_t, below, above, coef, None)
             next_band[pl.ds(64 * a + 8 * t, 8), :] = new
 
     for upper in range(2):
         a = 1 - upper
-        src = Sources(lambda c, t: side(upper, a, c, t) if c < 2 else side_band(upper, a, t))
+        src = Sources(lambda c, t: side(upper, a, c, t) if c < 2 else side_band(upper, t))
         for c in range(2):
             total = neighbour_sum(src, src.tile[c], src.turned[c], kinds[c])
             for t in range(TILES):
@@ -448,27 +534,29 @@
 def local(table, field_old, coef_old, owner, counts, pattern):
     layers = field_old.shape[0]
     stored = [pltpu.with_memory_space_constraint(x, pltpu.HBM) for x in (field_old, coef_old, owner)]
-    to_near, to_far, field, coef = call(
-        send_kernel,
-        [(104, LANES), (104, LANES), field_old.shape, coef_old.shape],
+    to_near, field, coef = call(
+        near_kernel,
+        [(104, LANES), field_old.shape, coef_old.shape],
         "hhhs",
         *stored, counts,
-        scratch=[
-            pltpu.SMEM((OLD_SLOTS,), jnp.int32),
-            pltpu.SemaphoreType.DMA((3,)),
-        ],
+        scratch=[pltpu.SMEM((OLD_SLOTS,), jnp.int32), pltpu.SemaphoreType.DMA((3,))],
+    )
+    from_near = swap(to_near, "leaf", 0)
+    to_far, own_part, band_part = call(
+        far_kernel,
+        [(144, LANES), (384, LANES), (192, LANES)],
+        "vvvvv",
+        field, coef, pattern, to_near, from_near,
     )
     from_far = swap(to_far, "leaf", 1)
-    from_near = swap(to_near, "leaf", 0)
-    pack, coef, band, sum_near, sum_far = call(
+    pack, pack_far, coef, band, sum_near, sum_far = call(
         place_kernel,
-        [(320, LANES), (128, LANES), (192, LANES), (32, LANES), (32, LANES)],
-        "vvvvvv",
-        field, coef, pattern, to_near, from_near, from_far,
+        [(288, LANES), (288, LANES), (128, LANES), (192, LANES), (32, LANES), (128, LANES)],
+        "vvvvv",
+        pattern, to_far, own_part, band_part, from_far,
     )
     side_near = swap(pack, "gy", 0)
-    side_far = swap(pack, "gy", 1)
-    sum_far = swap(sum_far, "leaf", 1)
+    side_far = swap(pack_far, "gy", 1)
     sum_near = swap(sum_near, "leaf", 0)
     (half,) = call(
         functools.partial(own_kernel, layers, table),

time: 32.6 us -> 31.8 us (0.975)
  the two profiles are of different devices: /device:TPU:35 before, /device:TPU:57 now
where the time goes in v4:
time: 31.8 us; the launch traced here: 31.3 us
  starting transfers between devices  23.1 us (73%)
  Pallas kernels  4.11 us (13%)
  waiting for transfers between devices  3.36 us (11%)
  between operations  0.72 us (2%)
    ppermute x5, starting transfers between devices, swap(): return lax.ppermute(block, axis, route)  23.1 us
    pallas_call x5, Pallas kernels, call(): pl.pallas_call(kernel, out_shape=[jax.ShapeDtypeStruct(s, F32) for s in s...  4.11 us
    ppermute x5, waiting for transfers between devices, swap(): return lax.ppermute(block, axis, route)  3.36 us
  transfers between devices with their start and end apart: 5, of which 3 were waited for; matrix products, arithmetic and copies ran while one was open for 0% of the time, Pallas kernels for 1%

profile of v4, /device:TPU:57, one launch (start us, length us, event | category | flops | bytes accessed | tf_op | source)
XLA Modules:
  0.0 31.3 jit_solution(3472707250771720767)
XLA Ops:
  0.7 0.0 copy-start
  0.7 1.1 %shard_map.55 = (f32[104,128]{1,0:T(8,128)S(1)}, f32[2,64,320]{2,1,0:T(8,128)S(1)}, f32[64,320]{1,0:T(8,128)S(1)}) custom-call(f32[2,64,320]{2,1,0:T(8,128)} %field_hbm.1, f32[64,320]{1,0:T(8,128)} %coef_hbm.1, s32[320]{0:T(512)} %owner_hbm.1, s32[1]{0:T(128)S(6)} %copy.6.counts_ref), custom_call_target="tpu_custom_call" | custom-call | bytes 247044 | tf_op jit(solution)/shard_map/pallas_call | solution.py:523
  1.8 2.6 %collective-permute-start = (f32[104,128]{1,0:T(8,128)S(1)}, f32[104,128]{1,0:T(8,128)S(1)}, u32[]{:S(2)}, u32[]{:S(2)}) collective-permute-start(f32[104,128]{1,0:T(8,128)S(1)} %get-tuple-element.19.kept_ref), channel_id=1, source_target_pairs={{0,4},{4,0},{8,12},{12,8},{16,20},{20,16},{24,28},{28,24},{32,36},... | collective-permute-start | bytes 159752 | tf_op jit(solution)/shard_map/ppermute | solution.py:516
  4.4 0.9 %collective-permute-done.near_ref = f32[104,128]{1,0:T(8,128)S(1)} collective-permute-done((f32[104,128]{1,0:T(8,128)S(1)}, f32[104,128]{1,0:T(8,128)S(1)}, u32[]{:S(2)}, u32[]{:S(2)}) %collective-permute-start) | collective-permute-done | bytes 53280 | tf_op jit(solution)/shard_map/ppermute | solution.py:516
  5.3 0.0 copy-done
  5.3 0.7 %shard_map.56 = (f32[144,128]{1,0:T(8,128)S(1)}, f32[384,128]{1,0:T(8,128)S(1)}, f32[192,128]{1,0:T(8,128)S(1)}) custom-call(f32[2,64,320]{2,1,0:T(8,128)S(1)} %get-tuple-element.17.field_ref, f32[64,320]{1,0:T(8,128)S(1)} %get-tuple-element.18.coef_ref, s32[6,256]{1,0:T(8,128)S(1)} %copy-done, f32[104,128]{1,0:T(8,128)S(1)} %get-tuple-element.19.kept_ref, ...), custom_call_target="tpu_custom_call" | custom-call | bytes 358400 | tf_op jit(solution)/shard_map/pallas_call | solution.py:523
  5.9 4.2 %collective-permute-start.1 = (f32[144,128]{1,0:T(8,128)S(1)}, f32[144,128]{1,0:T(8,128)S(1)}, u32[]{:S(2)}, u32[]{:S(2)}) collective-permute-start(f32[144,128]{1,0:T(8,128)S(1)} %get-tuple-element.20.kept_ref), channel_id=1, source_target_pairs={{4,8},{8,4},{12,16},{16,12},{20,24},{24,20},{28,32},{32,28},{36,40... | collective-permute-start | bytes 221192 | tf_op jit(solution)/shard_map/ppermute | solution.py:516
  10.2 2.0 %collective-permute-done.1.far_ref = f32[144,128]{1,0:T(8,128)S(1)} collective-permute-done((f32[144,128]{1,0:T(8,128)S(1)}, f32[144,128]{1,0:T(8,128)S(1)}, u32[]{:S(2)}, u32[]{:S(2)}) %collective-permute-start.1) | collective-permute-done | bytes 73760 | tf_op jit(solution)/shard_map/ppermute | solution.py:516
  12.2 0.6 %shard_map.57 = (f32[288,128]{1,0:T(8,128)S(1)}, f32[288,128]{1,0:T(8,128)S(1)}, f32[128,128]{1,0:T(8,128)S(1)}, f32[192,128]{1,0:T(8,128)S(1)}, f32[32,128]{1,0:T(8,128)S(1)}, /*index=5*/f32[128,128]{1,0:T(8,128)S(1)}) custom-call(s32[6,256]{1,0:T(8,128)S(1)} %copy-done, f32[144,128]{1,0:T(8,128)S(1)} %get-tuple-element.20.kept_ref, ...), custom_call_target="tpu_custom_call" | custom-call | bytes 448512 | tf_op jit(solution)/shard_map/pallas_call | solution.py:523
  12.8 0.7 %collective-permute-start.2 = (f32[288,128]{1,0:T(8,128)S(1)}, f32[288,128]{1,0:T(8,128)S(1)}, u32[]{:S(2)}, u32[]{:S(2)}) collective-permute-start(f32[288,128]{1,0:T(8,128)S(1)} %get-tuple-element.26), channel_id=1, source_target_pairs={{1,2},{2,1},{5,6},{6,5},{9,10},{10,9},{13,14},{14,13},{17,18},{18,... | collective-permute-start | bytes 442376 | tf_op jit(solution)/shard_map/ppermute | solution.py:516
  13.4 5.6 %collective-permute-start.3 = (f32[288,128]{1,0:T(8,128)S(1)}, f32[288,128]{1,0:T(8,128)S(1)}, u32[]{:S(2)}, u32[]{:S(2)}) collective-permute-start(f32[288,128]{1,0:T(8,128)S(1)} %get-tuple-element.23.pack_ref), channel_id=1, source_target_pairs={{0,1},{1,0},{2,3},{3,2},{4,5},{5,4},{6,7},{7,6},{8,9},{9,8},{10,11... | collective-permute-start | bytes 442376 | tf_op jit(solution)/shard_map/ppermute | solution.py:516
  19.0 10.1 %collective-permute-start.4 = (f32[32,128]{1,0:T(8,128)S(1)}, f32[32,128]{1,0:T(8,128)S(1)}, u32[]{:S(2)}, u32[]{:S(2)}) collective-permute-start(f32[32,128]{1,0:T(8,128)S(1)} %get-tuple-element.28), channel_id=1, source_target_pairs={{0,4},{4,0},{8,12},{12,8},{16,20},{20,16},{24,28},{28,24},{32,36},... | collective-permute-start | bytes 49160 | tf_op jit(solution)/shard_map/ppermute | solution.py:516
  29.1 0.3 %shard_map.58.half_ref = f32[256,128]{1,0:T(8,128)S(1)} custom-call(s32[6,256]{1,0:T(8,128)S(1)} %copy-done, f32[288,128]{1,0:T(8,128)S(1)} %get-tuple-element.23.pack_ref, f32[128,128]{1,0:T(8,128)S(1)} %get-tuple-element.24.coef_ref, f32[192,128]{1,0:T(8,128)S(1)} %get-tuple-element.25.band_ref), custom_call_target="tpu_custom_call" | custom-call | bytes 317440 | tf_op jit(solution)/shard_map/pallas_call | solution.py:523
  29.4 0.5 %collective-permute-done.4.sum_near = f32[32,128]{1,0:T(8,128)S(1)} collective-permute-done((f32[32,128]{1,0:T(8,128)S(1)}, f32[32,128]{1,0:T(8,128)S(1)}, u32[]{:S(2)}, u32[]{:S(2)}) %collective-permute-start.4) | collective-permute-done | bytes 16416 | tf_op jit(solution)/shard_map/ppermute | solution.py:516
  29.9 0.0 collective-permute-done.2.side_far
  29.9 0.0 collective-permute-done.3.side_near
  29.9 1.4 %shard_map.59 = f32[2,64,256]{2,1,0:T(8,128)} custom-call(s32[6,256]{1,0:T(8,128)S(1)} %copy-done, f32[288,128]{1,0:T(8,128)S(1)} %get-tuple-element.23.pack_ref, f32[128,128]{1,0:T(8,128)S(1)} %get-tuple-element.24.coef_ref, f32[192,128]{1,0:T(8,128)S(1)} %get-tuple-element.25.band_ref, f32[256,128]{1,0:T(8,128)S(1)} %shard_map.58.half_ref, ...), custom_call_target="tpu_custom_call" | custom-call | bytes 825344 | tf_op jit(solution)/shard_map/pallas_call | solution.py:523
Async XLA Ops:
  0.7 4.6 %copy-start = (s32[6,256]{1,0:T(8,128)S(1)}, s32[6,256]{1,0:T(8,128)}, u32[]{:S(2)}) copy-start(s32[6,256]{1,0:T(8,128)} %pattern_ref.7) | copy-start | bytes 18436
  1.8 3.5 %collective-permute-start = (f32[104,128]{1,0:T(8,128)S(1)}, f32[104,128]{1,0:T(8,128)S(1)}, u32[]{:S(2)}, u32[]{:S(2)}) collective-permute-start(f32[104,128]{1,0:T(8,128)S(1)} %get-tuple-element.19.kept_ref), channel_id=1, source_target_pairs={{0,4},{4,0},{8,12},{12,8},{16,20},{20,16},{24,28},{28,24},{32,36},... | collective-permute-start | bytes 159752 | tf_op jit(solution)/shard_map/ppermute | solution.py:516
  5.9 6.3 %collective-permute-start.1 = (f32[144,128]{1,0:T(8,128)S(1)}, f32[144,128]{1,0:T(8,128)S(1)}, u32[]{:S(2)}, u32[]{:S(2)}) collective-permute-start(f32[144,128]{1,0:T(8,128)S(1)} %get-tuple-element.20.kept_ref), channel_id=1, source_target_pairs={{4,8},{8,4},{12,16},{16,12},{20,24},{24,20},{28,32},{32,28},{36,40... | collective-permute-start | bytes 221192 | tf_op jit(solution)/shard_map/ppermute | solution.py:516
  12.8 17.2 %collective-permute-start.2 = (f32[288,128]{1,0:T(8,128)S(1)}, f32[288,128]{1,0:T(8,128)S(1)}, u32[]{:S(2)}, u32[]{:S(2)}) collective-permute-start(f32[288,128]{1,0:T(8,128)S(1)} %get-tuple-element.26), channel_id=1, source_target_pairs={{1,2},{2,1},{5,6},{6,5},{9,10},{10,9},{13,14},{14,13},{17,18},{18,... | collective-permute-start | bytes 442376 | tf_op jit(solution)/shard_map/ppermute | solution.py:516
  13.4 16.5 %collective-permute-start.3 = (f32[288,128]{1,0:T(8,128)S(1)}, f32[288,128]{1,0:T(8,128)S(1)}, u32[]{:S(2)}, u32[]{:S(2)}) collective-permute-start(f32[288,128]{1,0:T(8,128)S(1)} %get-tuple-element.23.pack_ref), channel_id=1, source_target_pairs={{0,1},{1,0},{2,3},{3,2},{4,5},{5,4},{6,7},{7,6},{8,9},{9,8},{10,11... | collective-permute-start | bytes 442376 | tf_op jit(solution)/shard_map/ppermute | solution.py:516
  19.0 10.9 %collective-permute-start.4 = (f32[32,128]{1,0:T(8,128)S(1)}, f32[32,128]{1,0:T(8,128)S(1)}, u32[]{:S(2)}, u32[]{:S(2)}) collective-permute-start(f32[32,128]{1,0:T(8,128)S(1)} %get-tuple-element.28), channel_id=1, source_target_pairs={{0,4},{4,0},{8,12},{12,8},{16,20},{20,16},{24,28},{28,24},{32,36},... | collective-permute-start | bytes 49160 | tf_op jit(solution)/shard_map/ppermute | solution.py:516

commit v5 on v4

--- a/solution.py
+++ b/solution.py
@@ -225,7 +225,25 @@
     )
 
 
-def far_kernel(field_ref, coef_ref, pattern_ref, kept_ref, near_ref, far_ref, own_ref, band_ref):
+def ready_kernel(field_ref, coef_ref, kept_ref, ends_ref, gone_ref):
+    lane = lanes()
+    even = is_even("leaf")
+    live, to_prev, to_next = (kept_ref[96 + i, 0].astype(jnp.int32) for i in (1, 2, 3))
+    for a in range(3):
+        ref, lead = (field_ref, a) if a < 2 else (coef_ref, None)
+        for r in range(4):
+            ends_ref[pl.ds(32 * a + 8 * r, 8), :] = ends(ref, lead, r, live, jnp.logical_not(even))
+        for t in range(TILES):
+            x0, x1, x2 = (old_tile(ref, lead, t, c) for c in range(3))
+            last = jnp.where(lane >= live - to_next - LANES, x1, x2)
+            gone_ref[pl.ds(64 * a + 8 * t, 8), :] = jnp.where(
+                lane < SPILL, spin(x0, SPILL - to_prev), spin(last, SPILL + to_next - live)
+            )
+
+
+def far_kernel(
+    field_ref, coef_ref, pattern_ref, kept_ref, ends_ref, gone_ref, near_ref, far_ref, own_ref, band_ref
+):
     lane, sub = lanes(), rows()
     even = is_even("leaf")
     live, to_prev, to_next = (kept_ref[96 + i, 0].astype(jnp.int32) for i in (1, 2, 3))
@@ -249,7 +267,8 @@
     for a in range(3):
         ref, lead = (field_ref, a) if a < 2 else (coef_ref, None)
         for r in range(4):
-            far_ref[pl.ds(32 * a + 8 * r, 8), :] = ends(ref, lead, r, live, jnp.logical_not(even))
+            at = pl.ds(32 * a + 8 * r, 8)
+            far_ref[at, :] = ends_ref[at, :]
         for t in range(TILES):
             h = 64 * (t // 4)
             near = near_ref[pl.ds(32 * a + 8 * (t % 4), 8), :]
@@ -260,8 +279,7 @@
             arrived = spin(near, arrive_by - h)
             own0 = jnp.where(lane < from_prev, jnp.where(even, 0.0, arrived), own0)
             own1 = jnp.where(lane >= tail, jnp.where(even, arrived, 0.0), own1)
-            last = jnp.where(lane >= live - to_next - LANES, x1, x2)
-            gone = jnp.where(lane < SPILL, spin(x0, SPILL - to_prev), spin(last, SPILL + to_next - live))
+            gone = gone_ref[pl.ds(64 * a + 8 * t, 8), :]
             band = jnp.where(spill, gone, jnp.where(near_lanes, spin(near, band_by - h), 0.0))
             own_ref[pl.ds(128 * a + 8 * t, 8), :] = own0
             own_ref[pl.ds(128 * a + 64 + 8 * t, 8), :] = own1
@@ -292,10 +310,9 @@
 
 
 def place_kernel(
-    pattern_ref, kept_ref, own_ref, band_ref, far_ref,
-    pack_near, pack_far, coef_out, band_out, sum_near, sum_far,
+    kept_ref, own_ref, band_ref, far_ref, pack_near, pack_far, coef_out, band_out
 ):
-    lane, sub = lanes(), rows()
+    lane = lanes()
     even = is_even("leaf")
     even_group = is_even("gy")
     _, live, to_prev, to_next, from_prev, from_next = (
@@ -337,6 +354,13 @@
         pack_near[pl.ds(256 + 8 * r, 8), :] = jnp.where(even_group, packed[1], packed[0])
         pack_far[pl.ds(256 + 8 * r, 8), :] = jnp.where(even_group, packed[0], packed[1])
 
+
+def facing_kernel(
+    pattern_ref, kept_ref, far_ref, pack_ref, band_ref, sum_near, sum_far
+):
+    lane = lanes()
+    even = is_even("leaf")
+    to_prev, to_next = (kept_ref[96 + i, 0].astype(jnp.int32) for i in (2, 3))
     near_kinds = face_indices(
         [jnp.where(even, pattern_row(pattern_ref, d, 1), pattern_row(pattern_ref, d, 0)) for d in range(6)]
     )
@@ -356,8 +380,8 @@
 
         def read(c, t):
             if c < 2:
-                return pack_near[pl.ds(128 * a + 64 * c + 8 * t, 8), :]
-            return band_out[pl.ds(64 * a + 8 * t, 8), :]
+                return pack_ref[pl.ds(128 * a + 64 * c + 8 * t, 8), :]
+            return band_ref[pl.ds(64 * a + 8 * t, 8), :]
 
         src = Sources(read)
         here = [jnp.where(even, src.tile[1][t], src.tile[0][t]) for t in range(TILES)]
@@ -422,91 +446,87 @@
                 half_ref[pl.ds(128 * a + 64 * c + 8 * t, 8), :] = (1.0 - OMEGA) * now + gain * push
 
 
-def relax_kernel(
-    layers, table,
-    pattern_ref, pack_ref, coef_ref, band_ref, half_ref, side_far, side_near, sum_far, sum_near,
-    out_ref, next_own, next_band, next_side,
+def side_kernel(
+    layers, table, final,
+    pattern_ref, pack_ref, coef_ref, band_ref, half_ref, side_ref, sum_near, sum_far, *refs,
 ):
+    if final:
+        other_once, other_twice, out_ref, next_own, next_band, next_side = refs
+    else:
+        next_own, twice_ref, next_band, next_side = refs
     lane = lanes()
     group = lax.axis_index("gy")
     even = is_even("leaf")
-    even_group = is_even("gy")
+    upper = is_even("gy") if final else jnp.logical_not(is_even("gy"))
+    a = jnp.where(upper, 1, 0)
     unpack_by = jnp.where(even, SPILL, 0)
     near_lanes = (lane >= unpack_by) & (lane < unpack_by + SPILL)
     kinds = own_kinds(pattern_ref)
     w_lower, w_first, w_second, w_upper = (weights_at(table, group, layers, o) for o in (-1, 0, 1, 2))
-
-    def step(weights, now, total, below, above, coef, phase):
-        spread, gain = gains(weights, coef)
-        push = spread * total + weights[1] * below + weights[2] * above
-        if phase is not None:
-            push = push + bulge(weights, phase)
-        return (1.0 - OMEGA) * now + gain * push
-
-    def beside(upper, at):
-        near, far = side_near[at, :], side_far[at, :]
-        return jnp.where(even_group, near, far) if upper else jnp.where(even_group, far, near)
-
-    def side(upper, a, c, t):
-        return beside(upper, pl.ds(128 * a + 64 * c + 8 * t, 8))
-
-    def side_band(upper, t):
-        tile = beside(upper, pl.ds(256 + 8 * (t % 4), 8))
-        tile = pltpu.roll(tile, 64, 1) if t >= 4 else tile
-        return jnp.where(lane < 64, tile, 0.0)
-
-    for a in range(2):
-        weights = w_second if a else w_first
-        for c in range(2):
-            for t in range(TILES):
-                _, gain = gains(weights, coef_ref[pl.ds(64 * c + 8 * t, 8), :])
-                missing = weights[1 + a] * side(a, 1 - a, c, t)
-                next_own[pl.ds(128 * a + 64 * c + 8 * t, 8), :] = own(half_ref, a, c, t) + gain * missing
+    w_own = [jnp.where(upper, u, v) for u, v in zip(w_second, w_first)]
+    w_side = [jnp.where(upper, u, v) for u, v in zip(w_upper, w_lower)]
+    own_to_side, own_to_other = jnp.where(upper, w_own[2], w_own[1]), jnp.where(upper, w_own[1], w_own[2])
+    side_to_own, side_to_next = jnp.where(upper, w_side[1], w_side[2]), jnp.where(upper, w_side[2], w_side[1])
+    other_link = jnp.where(upper, w_first[2], w_second[1])
+    w_other = [jnp.where(upper, u, v) for u, v in zip(w_first, w_second)]
+
+    def at(base, offset):
+        return pl.ds(pl.multiple_of(base + offset, 8), 8)
+
+    here, there = 128 * a, 128 * (1 - a)
+
+    def side_band(t):
+        tile = side_ref[pl.ds(256 + 8 * (t % 4), 8), :]
+        return jnp.where(lane < 64, pltpu.roll(tile, 64, 1) if t >= 4 else tile, 0.0)
+
+    for c in range(2):
         for t in range(TILES):
-            now = band_ref[pl.ds(64 * a + 8 * t, 8), :]
-            coef = band_ref[pl.ds(128 + 8 * t, 8), :]
-            near = sum_near[pl.ds(16 * a + 8 * (t % 2), 8), :]
-            near = spin(near, unpack_by - 32 * (t // 2))
-            total_t = jnp.where(near_lanes, near, sum_far[pl.ds(64 * a + 8 * t, 8), :])
-            if a == 0:
-                below, above = side_band(0, t), band_ref[pl.ds(64 + 8 * t, 8), :]
-                new = step(w_first, now, total_t, below, above, coef, now)
-            else:
-                below, above = band_ref[pl.ds(8 * t, 8), :], side_band(1, t)
-                new = step(w_second, now, total_t, below, above, coef, None)
-            next_band[pl.ds(64 * a + 8 * t, 8), :] = new
-
-    for upper in range(2):
-        a = 1 - upper
-        src = Sources(lambda c, t: side(upper, a, c, t) if c < 2 else side_band(upper, t))
-        for c in range(2):
-            total = neighbour_sum(src, src.tile[c], src.turned[c], kinds[c])
-            for t in range(TILES):
-                coef = coef_ref[pl.ds(64 * c + 8 * t, 8), :]
-                if upper:
-                    below, above = own(pack_ref, 1, c, t), side(1, 1, c, t)
-                    new = step(w_upper, src.tile[c][t], total[t], below, above, coef, None)
-                else:
-                    below, above = side(0, 0, c, t), own(pack_ref, 0, c, t)
-                    new = step(w_lower, src.tile[c][t], total[t], below, above, coef, None)
-                next_side[pl.ds(128 * upper + 64 * c + 8 * t, 8), :] = new
-
-    for a in range(2):
-        src = Sources(
-            lambda c, t: own(next_own, a, c, t) if c < 2 else next_band[pl.ds(64 * a + 8 * t, 8), :]
-        )
-        for c in range(2):
-            total = neighbour_sum(src, src.tile[c], src.turned[c], kinds[c])
-            for t in range(TILES):
-                coef = coef_ref[pl.ds(64 * c + 8 * t, 8), :]
-                now = src.tile[c][t]
-                if a == 0:
-                    below, above = own(next_side, 0, c, t), own(next_own, 1, c, t)
-                    new = step(w_first, now, total[t], below, above, coef, own(pack_ref, 0, c, t))
-                else:
-                    below, above = own(next_own, 0, c, t), own(next_side, 1, c, t)
-                    new = step(w_second, now, total[t], below, above, coef, None)
-                out_ref[a, pl.ds(8 * t, 8), pl.ds(LANES * c, LANES)] = new
+            k = 64 * c + 8 * t
+            _, gain = gains(w_own, coef_ref[pl.ds(k, 8), :])
+            next_own[pl.ds(k, 8), :] = (
+                half_ref[at(here, k), :] + gain * own_to_side * side_ref[at(there, k), :]
+            )
+    for t in range(TILES):
+        now = band_ref[at(64 * a, 8 * t), :]
+        spread, gain = gains(w_own, band_ref[pl.ds(128 + 8 * t, 8), :])
+        near = spin(sum_near[at(16 * a, 8 * (t % 2)), :], unpack_by - 32 * (t // 2))
+        total = jnp.where(near_lanes, near, sum_far[at(64 * a, 8 * t), :])
+        push = spread * total + own_to_side * side_band(t) + bulge(w_own, now)
+        push = push + own_to_other * band_ref[at(64 * (1 - a), 8 * t), :]
+        next_band[pl.ds(8 * t, 8), :] = (1.0 - OMEGA) * now + gain * push
+
+    src = Sources(lambda c, t: side_ref[at(there, 64 * c + 8 * t), :] if c < 2 else side_band(t))
+    for c in range(2):
+        total = neighbour_sum(src, src.tile[c], src.turned[c], kinds[c])
+        for t in range(TILES):
+            k = 64 * c + 8 * t
+            spread, gain = gains(w_side, coef_ref[pl.ds(k, 8), :])
+            push = spread * total[t] + side_to_own * pack_ref[at(here, k), :]
+            push = push + side_to_next * side_ref[at(here, k), :]
+            next_side[pl.ds(k, 8), :] = (1.0 - OMEGA) * src.tile[c][t] + gain * push
+
+    src = Sources(
+        lambda c, t: next_own[pl.ds(64 * c + 8 * t, 8), :] if c < 2 else next_band[pl.ds(8 * t, 8), :]
+    )
+    for c in range(2):
+        total = neighbour_sum(src, src.tile[c], src.turned[c], kinds[c])
+        for t in range(TILES):
+            k = 64 * c + 8 * t
+            coef = coef_ref[pl.ds(k, 8), :]
+            spread, gain = gains(w_own, coef)
+            once = src.tile[c][t]
+            push = spread * total[t] + own_to_side * next_side[pl.ds(k, 8), :]
+            push = push + bulge(w_own, pack_ref[at(here, k), :])
+            if not final:
+                twice_ref[pl.ds(k, 8), :] = (1.0 - OMEGA) * once + gain * push
+                continue
+            push = push + own_to_other * other_once[pl.ds(k, 8), :]
+            _, other_gain = gains(w_other, coef)
+            lanes_at = pl.ds(LANES * c, LANES)
+            out_ref[a, pl.ds(8 * t, 8), lanes_at] = (1.0 - OMEGA) * once + gain * push
+            out_ref[1 - a, pl.ds(8 * t, 8), lanes_at] = (
+                other_twice[pl.ds(k, 8), :] + other_gain * other_link * once
+            )
 
 
 def swap(block, axis, first):
@@ -542,21 +562,27 @@
         scratch=[pltpu.SMEM((OLD_SLOTS,), jnp.int32), pltpu.SemaphoreType.DMA((3,))],
     )
     from_near = swap(to_near, "leaf", 0)
+    ends_far, gone = call(
+        ready_kernel, [(96, LANES), (192, LANES)], "vvv", field, coef, to_near
+    )
     to_far, own_part, band_part = call(
         far_kernel,
         [(144, LANES), (384, LANES), (192, LANES)],
-        "vvvvv",
-        field, coef, pattern, to_near, from_near,
+        "vvvvvvv",
+        field, coef, pattern, to_near, ends_far, gone, from_near,
     )
     from_far = swap(to_far, "leaf", 1)
-    pack, pack_far, coef, band, sum_near, sum_far = call(
+    pack, pack_far, coef, band = call(
         place_kernel,
-        [(288, LANES), (288, LANES), (128, LANES), (192, LANES), (32, LANES), (128, LANES)],
-        "vvvvv",
-        pattern, to_far, own_part, band_part, from_far,
+        [(288, LANES), (288, LANES), (128, LANES), (192, LANES)],
+        "vvvv",
+        to_far, own_part, band_part, from_far,
     )
     side_near = swap(pack, "gy", 0)
     side_far = swap(pack_far, "gy", 1)
+    sum_near, sum_far = call(
+        facing_kernel, [(32, LANES), (128, LANES)], "vvvvv", pattern, to_far, from_far, pack, band
+    )
     sum_near = swap(sum_near, "leaf", 0)
     (half,) = call(
         functools.partial(own_kernel, layers, table),
@@ -564,12 +590,19 @@
         "vvvv",
         pattern, pack, coef, band,
     )
+    once, twice = call(
+        functools.partial(side_kernel, layers, table, False),
+        [(128, LANES), (128, LANES)],
+        "vvvvvvvv",
+        pattern, pack, coef, band, half, side_far, sum_near, sum_far,
+        scratch=[pltpu.VMEM((64, LANES), F32), pltpu.VMEM((128, LANES), F32)],
+    )
     (out,) = call(
-        functools.partial(relax_kernel, layers, table),
+        functools.partial(side_kernel, layers, table, True),
         [(layers, 64, BRICKS_DEV)],
-        "vvvvvvvvv",
-        pattern, pack, coef, band, half, side_far, side_near, sum_far, sum_near,
-        scratch=[pltpu.VMEM((rows, LANES), F32) for rows in (256, 128, 256)],
+        "vvvvvvvvvv",
+        pattern, pack, coef, band, half, side_near, sum_near, sum_far, once, twice,
+        scratch=[pltpu.VMEM((rows, LANES), F32) for rows in (128, 64, 128)],
     )
     return out
 

time: 31.8 us -> 31.7 us (level)
    pallas_call x5 -> x8, Pallas kernels: 4.11 us -> 4.36 us  [call(): pl.pallas_call(kernel, out_shape=[jax.ShapeDtypeStruct(s, F32) for s in s...]
  transfers between devices with their start and end apart: 5 -> 5, of which waited for: 3 -> 3; matrix products, arithmetic and copies ran while one was open for 0% -> 0% of each run, Pallas kernels for 1% -> 4%
where the time goes in v5:
time: 31.7 us; the launch traced here: 31.4 us
  starting transfers between devices  23.1 us (73%)
  Pallas kernels  4.36 us (14%)
  waiting for transfers between devices  3.16 us (10%)
  between operations  0.75 us (2%)
    ppermute x5, starting transfers between devices, swap(): return lax.ppermute(block, axis, route)  23.1 us
    pallas_call x8, Pallas kernels, call(): pl.pallas_call(kernel, out_shape=[jax.ShapeDtypeStruct(s, F32) for s in s...  4.36 us
    ppermute x5, waiting for transfers between devices, swap(): return lax.ppermute(block, axis, route)  3.16 us
  transfers between devices with their start and end apart: 5, of which 3 were waited for; matrix products, arithmetic and copies ran while one was open for 0% of the time, Pallas kernels for 4%

profile of v5, /device:TPU:57, one launch (start us, length us, event | category | flops | bytes accessed | tf_op | source)
XLA Modules:
  0.0 31.4 jit_solution(14072525007127680685)
XLA Ops:
  0.7 1.1 %shard_map.55 = (f32[104,128]{1,0:T(8,128)S(1)}, f32[2,64,320]{2,1,0:T(8,128)S(1)}, f32[64,320]{1,0:T(8,128)S(1)}) custom-call(f32[2,64,320]{2,1,0:T(8,128)} %field_hbm.1, f32[64,320]{1,0:T(8,128)} %coef_hbm.1, s32[320]{0:T(512)} %owner_hbm.1, s32[1]{0:T(128)S(6)} %copy.6.counts_ref), custom_call_target="tpu_custom_call" | custom-call | bytes 247044 | tf_op jit(solution)/shard_map/pallas_call | solution.py:543
  1.8 2.6 %collective-permute-start = (f32[104,128]{1,0:T(8,128)S(1)}, f32[104,128]{1,0:T(8,128)S(1)}, u32[]{:S(2)}, u32[]{:S(2)}) collective-permute-start(f32[104,128]{1,0:T(8,128)S(1)} %get-tuple-element.23.kept_ref), channel_id=1, source_target_pairs={{0,4},{4,0},{8,12},{12,8},{16,20},{20,16},{24,28},{28,24},{32,36},... | collective-permute-start | bytes 159752 | tf_op jit(solution)/shard_map/ppermute | solution.py:536
  4.4 0.0 copy-start
  4.4 0.2 shard_map.56
  4.6 0.7 %collective-permute-done.near_ref = f32[104,128]{1,0:T(8,128)S(1)} collective-permute-done((f32[104,128]{1,0:T(8,128)S(1)}, f32[104,128]{1,0:T(8,128)S(1)}, u32[]{:S(2)}, u32[]{:S(2)}) %collective-permute-start) | collective-permute-done | bytes 53280 | tf_op jit(solution)/shard_map/ppermute | solution.py:536
  5.2 0.0 copy-done
  5.2 0.6 %shard_map.57 = (f32[144,128]{1,0:T(8,128)S(1)}, f32[384,128]{1,0:T(8,128)S(1)}, f32[192,128]{1,0:T(8,128)S(1)}) custom-call(f32[2,64,320]{2,1,0:T(8,128)S(1)} %get-tuple-element.21.field_ref, f32[64,320]{1,0:T(8,128)S(1)} %get-tuple-element.22.coef_ref, s32[6,256]{1,0:T(8,128)S(1)} %copy-done, f32[104,128]{1,0:T(8,128)S(1)} %get-tuple-element.23.kept_ref, ...), custom_call_target="tpu_custom_call" | custom-call | bytes 505856 | tf_op jit(solution)/shard_map/pallas_call | solution.py:543
  5.8 4.2 %collective-permute-start.1 = (f32[144,128]{1,0:T(8,128)S(1)}, f32[144,128]{1,0:T(8,128)S(1)}, u32[]{:S(2)}, u32[]{:S(2)}) collective-permute-start(f32[144,128]{1,0:T(8,128)S(1)} %get-tuple-element.26.kept_ref), channel_id=1, source_target_pairs={{4,8},{8,4},{12,16},{16,12},{20,24},{24,20},{28,32},{32,28},{36,40... | collective-permute-start | bytes 221192 | tf_op jit(solution)/shard_map/ppermute | solution.py:536
  10.1 2.0 %collective-permute-done.1.far_ref = f32[144,128]{1,0:T(8,128)S(1)} collective-permute-done((f32[144,128]{1,0:T(8,128)S(1)}, f32[144,128]{1,0:T(8,128)S(1)}, u32[]{:S(2)}, u32[]{:S(2)}) %collective-permute-start.1) | collective-permute-done | bytes 73760 | tf_op jit(solution)/shard_map/ppermute | solution.py:536
  12.1 0.2 shard_map.58
  12.3 0.7 %collective-permute-start.4 = (f32[288,128]{1,0:T(8,128)S(1)}, f32[288,128]{1,0:T(8,128)S(1)}, u32[]{:S(2)}, u32[]{:S(2)}) collective-permute-start(f32[288,128]{1,0:T(8,128)S(1)} %get-tuple-element.34), channel_id=1, source_target_pairs={{1,2},{2,1},{5,6},{6,5},{9,10},{10,9},{13,14},{14,13},{17,18},{18,... | collective-permute-start | bytes 442376 | tf_op jit(solution)/shard_map/ppermute | solution.py:536
  13.0 5.6 %collective-permute-start.2 = (f32[288,128]{1,0:T(8,128)S(1)}, f32[288,128]{1,0:T(8,128)S(1)}, u32[]{:S(2)}, u32[]{:S(2)}) collective-permute-start(f32[288,128]{1,0:T(8,128)S(1)} %get-tuple-element.29.pack_ref), channel_id=1, source_target_pairs={{0,1},{1,0},{2,3},{3,2},{4,5},{5,4},{6,7},{7,6},{8,9},{9,8},{10,11... | collective-permute-start | bytes 442376 | tf_op jit(solution)/shard_map/ppermute | solution.py:536
  18.6 0.5 %shard_map.60 = (f32[32,128]{1,0:T(8,128)S(1)}, f32[128,128]{1,0:T(8,128)S(1)}) custom-call(s32[6,256]{1,0:T(8,128)S(1)} %copy-done, f32[144,128]{1,0:T(8,128)S(1)} %get-tuple-element.26.kept_ref, f32[144,128]{1,0:T(8,128)S(1)} %collective-permute-done.1.far_ref, f32[288,128]{1,0:T(8,128)S(1)} %get-tuple-element.29.pack_ref, ...), custom_call_target="tpu_custom_call" | custom-call | bytes 399360 | tf_op jit(solution)/shard_map/pallas_call | solution.py:543
  19.0 10.1 %collective-permute-start.3 = (f32[32,128]{1,0:T(8,128)S(1)}, f32[32,128]{1,0:T(8,128)S(1)}, u32[]{:S(2)}, u32[]{:S(2)}) collective-permute-start(f32[32,128]{1,0:T(8,128)S(1)} %get-tuple-element.32), channel_id=1, source_target_pairs={{0,4},{4,0},{8,12},{12,8},{16,20},{20,16},{24,28},{28,24},{32,36},... | collective-permute-start | bytes 49160 | tf_op jit(solution)/shard_map/ppermute | solution.py:536
  29.1 0.3 %shard_map.59.half_ref = f32[256,128]{1,0:T(8,128)S(1)} custom-call(s32[6,256]{1,0:T(8,128)S(1)} %copy-done, f32[288,128]{1,0:T(8,128)S(1)} %get-tuple-element.29.pack_ref, f32[128,128]{1,0:T(8,128)S(1)} %get-tuple-element.30.coef_ref, f32[192,128]{1,0:T(8,128)S(1)} %get-tuple-element.31.band_ref), custom_call_target="tpu_custom_call" | custom-call | bytes 317440 | tf_op jit(solution)/shard_map/pallas_call | solution.py:543
  29.5 0.5 %collective-permute-done.3.sum_near = f32[32,128]{1,0:T(8,128)S(1)} collective-permute-done((f32[32,128]{1,0:T(8,128)S(1)}, f32[32,128]{1,0:T(8,128)S(1)}, u32[]{:S(2)}, u32[]{:S(2)}) %collective-permute-start.3) | collective-permute-done | bytes 16416 | tf_op jit(solution)/shard_map/ppermute | solution.py:536
  30.0 0.0 collective-permute-done.4.side_ref
  30.0 0.4 %shard_map.61 = (f32[128,128]{1,0:T(8,128)S(1)}, f32[128,128]{1,0:T(8,128)S(1)}) custom-call(s32[6,256]{1,0:T(8,128)S(1)} %copy-done, f32[288,128]{1,0:T(8,128)S(1)} %get-tuple-element.29.pack_ref, f32[128,128]{1,0:T(8,128)S(1)} %get-tuple-element.30.coef_ref, f32[192,128]{1,0:T(8,128)S(1)} %get-tuple-element.31.band_ref, ...), custom_call_target="tpu_custom_call" | custom-call | bytes 677888 | tf_op jit(solution)/shard_map/pallas_call | solution.py:543
  30.3 0.0 collective-permute-done.2.side_ref
  30.4 1.1 %shard_map.62 = f32[2,64,256]{2,1,0:T(8,128)} custom-call(s32[6,256]{1,0:T(8,128)S(1)} %copy-done, f32[288,128]{1,0:T(8,128)S(1)} %get-tuple-element.29.pack_ref, f32[128,128]{1,0:T(8,128)S(1)} %get-tuple-element.30.coef_ref, f32[192,128]{1,0:T(8,128)S(1)} %get-tuple-element.31.band_ref, f32[256,128]{1,0:T(8,128)S(1)} %shard_map.59.half_ref, ...), custom_call_target="tpu_custom_call" | custom-call | bytes 808960 | tf_op jit(solution)/shard_map/pallas_call | solution.py:543
Async XLA Ops:
  1.8 3.5 %collective-permute-start = (f32[104,128]{1,0:T(8,128)S(1)}, f32[104,128]{1,0:T(8,128)S(1)}, u32[]{:S(2)}, u32[]{:S(2)}) collective-permute-start(f32[104,128]{1,0:T(8,128)S(1)} %get-tuple-element.23.kept_ref), channel_id=1, source_target_pairs={{0,4},{4,0},{8,12},{12,8},{16,20},{20,16},{24,28},{28,24},{32,36},... | collective-permute-start | bytes 159752 | tf_op jit(solution)/shard_map/ppermute | solution.py:536
  4.4 0.9 %copy-start = (s32[6,256]{1,0:T(8,128)S(1)}, s32[6,256]{1,0:T(8,128)}, u32[]{:S(2)}) copy-start(s32[6,256]{1,0:T(8,128)} %pattern_ref.9) | copy-start | bytes 18436
  5.8 6.3 %collective-permute-start.1 = (f32[144,128]{1,0:T(8,128)S(1)}, f32[144,128]{1,0:T(8,128)S(1)}, u32[]{:S(2)}, u32[]{:S(2)}) collective-permute-start(f32[144,128]{1,0:T(8,128)S(1)} %get-tuple-element.26.kept_ref), channel_id=1, source_target_pairs={{4,8},{8,4},{12,16},{16,12},{20,24},{24,20},{28,32},{32,28},{36,40... | collective-permute-start | bytes 221192 | tf_op jit(solution)/shard_map/ppermute | solution.py:536
  12.3 17.6 %collective-permute-start.4 = (f32[288,128]{1,0:T(8,128)S(1)}, f32[288,128]{1,0:T(8,128)S(1)}, u32[]{:S(2)}, u32[]{:S(2)}) collective-permute-start(f32[288,128]{1,0:T(8,128)S(1)} %get-tuple-element.34), channel_id=1, source_target_pairs={{1,2},{2,1},{5,6},{6,5},{9,10},{10,9},{13,14},{14,13},{17,18},{18,... | collective-permute-start | bytes 442376 | tf_op jit(solution)/shard_map/ppermute | solution.py:536
  13.0 17.4 %collective-permute-start.2 = (f32[288,128]{1,0:T(8,128)S(1)}, f32[288,128]{1,0:T(8,128)S(1)}, u32[]{:S(2)}, u32[]{:S(2)}) collective-permute-start(f32[288,128]{1,0:T(8,128)S(1)} %get-tuple-element.29.pack_ref), channel_id=1, source_target_pairs={{0,1},{1,0},{2,3},{3,2},{4,5},{5,4},{6,7},{7,6},{8,9},{9,8},{10,11... | collective-permute-start | bytes 442376 | tf_op jit(solution)/shard_map/ppermute | solution.py:536
  19.0 10.9 %collective-permute-start.3 = (f32[32,128]{1,0:T(8,128)S(1)}, f32[32,128]{1,0:T(8,128)S(1)}, u32[]{:S(2)}, u32[]{:S(2)}) collective-permute-start(f32[32,128]{1,0:T(8,128)S(1)} %get-tuple-element.32), channel_id=1, source_target_pairs={{0,4},{4,0},{8,12},{12,8},{16,20},{20,16},{24,28},{28,24},{32,36},... | collective-permute-start | bytes 49160 | tf_op jit(solution)/shard_map/ppermute | solution.py:536

commit v6 on v5

--- a/solution.py
+++ b/solution.py
@@ -85,16 +85,17 @@
 
 
 def spill_counts(owner_ref, live_count, device):
-    to_prev = jnp.int32(0)
-    to_next = jnp.int32(0)
-    for step in (32, 16, 8, 4, 2, 1):
-        near = jnp.minimum(to_prev + step, SPILL)
-        hit = (to_prev + step <= SPILL) & (owner_ref[near - 1] < device)
-        to_prev = jnp.where(hit, to_prev + step, to_prev)
-        near = jnp.minimum(to_next + step, SPILL)
-        hit = (to_next + step <= SPILL) & (owner_ref[live_count - near] > device)
-        to_next = jnp.where(hit, to_next + step, to_next)
-    return to_prev, to_next
+    lane, sub = lanes(), rows()
+    hits = jnp.zeros((8, LANES), F32)
+    for c in range(3):
+        width = min(LANES, OLD_SLOTS - LANES * c)
+        row = owner_ref[pl.ds(LANES * c, width)].reshape(1, width)
+        if width < LANES:
+            row = jnp.concatenate([row, jnp.zeros((1, LANES - width), jnp.int32)], axis=1)
+        row = jnp.broadcast_to(row, (8, LANES))
+        wanted = device + jnp.where(sub == 0, -1, 1)
+        hits += jnp.where((row == wanted) & (lane + LANES * c < live_count), 1.0, 0.0)
+    return jnp.sum(hits, axis=1, keepdims=True)
 
 
 def old_tile(ref, lead, t, c):
@@ -199,10 +200,10 @@
     even = is_even("leaf")
     live = counts_ref[0]
     copies[0].wait()
-    to_prev, to_next = spill_counts(owner_ref, live, lax.axis_index("leaf"))
-    handed = jnp.where(even, to_next, to_prev)
-    kept = jnp.where(sub == 1, live, jnp.where(sub == 2, to_prev, to_next))
-    near_ref[pl.ds(96, 8), :] = jnp.where(sub == 0, handed, kept).astype(F32)
+    spills = spill_counts(owner_ref, live, lax.axis_index("leaf"))
+    to_prev, to_next = (jnp.broadcast_to(spills[i : i + 1], (8, LANES)) for i in range(2))
+    kept = jnp.where(sub == 1, live.astype(F32), jnp.where(sub == 2, to_prev, to_next))
+    near_ref[pl.ds(96, 8), :] = jnp.where(sub == 0, jnp.where(even, to_next, to_prev), kept)
     for a in range(3):
         ref, lead = (field_ref, a) if a < 2 else (coef_ref, None)
         if a != 1:
@@ -241,34 +242,18 @@
             )
 
 
-def far_kernel(
-    field_ref, coef_ref, pattern_ref, kept_ref, ends_ref, gone_ref, near_ref, far_ref, own_ref, band_ref
-):
-    lane, sub = lanes(), rows()
-    even = is_even("leaf")
-    live, to_prev, to_next = (kept_ref[96 + i, 0].astype(jnp.int32) for i in (1, 2, 3))
-    from_near = near_ref[96, 0].astype(jnp.int32)
-    stay = live - to_prev - to_next
-    from_far = BRICKS_DEV - stay - from_near
-    from_prev, from_next = jnp.where(even, from_far, from_near), jnp.where(even, from_near, from_far)
+def place_part(sources, counts, gone_ref, near_ref, own_ref, band_ref):
+    lane = lanes()
+    even = is_even("leaf")
+    live, to_prev, to_next, from_prev, from_next = counts
     drift = to_prev - from_prev
-    tail = from_prev + stay - LANES
-    handed = jnp.where(even, to_prev, to_next)
-    values = (handed, live, to_prev, to_next, from_prev, from_next, 0, 0)
-    counts = jnp.zeros((8, LANES), jnp.int32)
-    for i, value in enumerate(values):
-        counts = jnp.where(sub == i, value, counts)
-    far_ref[pl.ds(96, 8), :] = counts.astype(F32)
+    tail = from_prev + live - to_prev - to_next - LANES
     spill = (lane >= SPILL - to_prev) & (lane < SPILL + to_next)
-    near_low, near_high = jnp.where(even, SPILL, 0), jnp.where(even, 2 * SPILL, SPILL)
-    near_lanes = (lane >= near_low) & (lane < near_high)
+    near_low = jnp.where(even, SPILL, 0)
+    near_lanes = (lane >= near_low) & (lane < near_low + SPILL)
     arrive_by = jnp.where(even, tail, from_prev - 64)
     band_by = jnp.where(even, SPILL + to_next - from_next, from_prev - to_prev - SPILL)
-    for a in range(3):
-        ref, lead = (field_ref, a) if a < 2 else (coef_ref, None)
-        for r in range(4):
-            at = pl.ds(32 * a + 8 * r, 8)
-            far_ref[at, :] = ends_ref[at, :]
+    for out, (a, ref, lead) in enumerate(sources):
         for t in range(TILES):
             h = 64 * (t // 4)
             near = near_ref[pl.ds(32 * a + 8 * (t % 4), 8), :]
@@ -281,9 +266,38 @@
             own1 = jnp.where(lane >= tail, jnp.where(even, arrived, 0.0), own1)
             gone = gone_ref[pl.ds(64 * a + 8 * t, 8), :]
             band = jnp.where(spill, gone, jnp.where(near_lanes, spin(near, band_by - h), 0.0))
-            own_ref[pl.ds(128 * a + 8 * t, 8), :] = own0
-            own_ref[pl.ds(128 * a + 64 + 8 * t, 8), :] = own1
-            band_ref[pl.ds(64 * a + 8 * t, 8), :] = band
+            own_ref[pl.ds(128 * out + 8 * t, 8), :] = own0
+            own_ref[pl.ds(128 * out + 64 + 8 * t, 8), :] = own1
+            band_ref[pl.ds(64 * out + 8 * t, 8), :] = band
+    return near_lanes
+
+
+def coef_kernel(coef_ref, kept_ref, gone_ref, near_ref, own_ref, band_ref):
+    counts = [kept_ref[96 + i, 0].astype(jnp.int32) for i in range(1, 6)]
+    place_part([(2, coef_ref, None)], counts, gone_ref, near_ref, own_ref, band_ref)
+
+
+def far_kernel(
+    field_ref, pattern_ref, kept_ref, ends_ref, gone_ref, near_ref, far_ref, own_ref, band_ref
+):
+    lane, sub = lanes(), rows()
+    even = is_even("leaf")
+    live, to_prev, to_next = (kept_ref[96 + i, 0].astype(jnp.int32) for i in (1, 2, 3))
+    from_near = near_ref[96, 0].astype(jnp.int32)
+    from_far = BRICKS_DEV - (live - to_prev - to_next) - from_near
+    from_prev, from_next = jnp.where(even, from_far, from_near), jnp.where(even, from_near, from_far)
+    handed = jnp.where(even, to_prev, to_next)
+    counts = jnp.zeros((8, LANES), jnp.int32)
+    for i, value in enumerate((handed, live, to_prev, to_next, from_prev, from_next)):
+        counts = jnp.where(sub == i, value, counts)
+    far_ref[pl.ds(96, 8), :] = counts.astype(F32)
+    for r in range(12):
+        far_ref[pl.ds(8 * r, 8), :] = ends_ref[pl.ds(8 * r, 8), :]
+    near_lanes = place_part(
+        [(a, field_ref, a) for a in range(2)],
+        (live, to_prev, to_next, from_prev, from_next),
+        gone_ref, near_ref, own_ref, band_ref,
+    )
     far_rows = [
         jnp.where(even, pattern_row(pattern_ref, d, 0), pattern_row(pattern_ref, d, 1)) for d in range(6)
     ]
@@ -310,7 +324,7 @@
 
 
 def place_kernel(
-    kept_ref, own_ref, band_ref, far_ref, pack_near, pack_far, coef_out, band_out
+    kept_ref, own_ref, band_ref, coef_own, coef_band, far_ref, pack_near, pack_far, coef_out, band_out
 ):
     lane = lanes()
     even = is_even("leaf")
@@ -331,10 +345,11 @@
             h = 64 * (t // 4)
             far = far_ref[pl.ds(32 * a + 8 * (t % 4), 8), :]
             arrived = spin(far, arrive_by - h)
-            own0 = jnp.where(lane < first, arrived, own_ref[pl.ds(128 * a + 8 * t, 8), :])
-            own1 = jnp.where(lane >= final, arrived, own_ref[pl.ds(128 * a + 64 + 8 * t, 8), :])
-            at = pl.ds(64 * a + 8 * t, 8)
-            band_out[at, :] = jnp.where(stays, spin(far, band_by - h), band_ref[at, :])
+            part, side, b = (own_ref, band_ref, a) if a < 2 else (coef_own, coef_band, 0)
+            own0 = jnp.where(lane < first, arrived, part[pl.ds(128 * b + 8 * t, 8), :])
+            own1 = jnp.where(lane >= final, arrived, part[pl.ds(128 * b + 64 + 8 * t, 8), :])
+            band = jnp.where(stays, spin(far, band_by - h), side[pl.ds(64 * b + 8 * t, 8), :])
+            band_out[pl.ds(64 * a + 8 * t, 8), :] = band
             if a < 2:
                 for pack in (pack_near, pack_far):
                     pack[pl.ds(128 * a + 8 * t, 8), :] = own0
@@ -355,50 +370,48 @@
         pack_far[pl.ds(256 + 8 * r, 8), :] = jnp.where(even_group, packed[0], packed[1])
 
 
-def facing_kernel(
-    pattern_ref, kept_ref, far_ref, pack_ref, band_ref, sum_near, sum_far
-):
+def facing_kernel(pattern_ref, pack_ref, band_ref, sum_near):
+    even = is_even("leaf")
+    kinds = face_indices(
+        [jnp.where(even, pattern_row(pattern_ref, d, 1), pattern_row(pattern_ref, d, 0)) for d in range(6)]
+    )
+    for a in range(2):
+        src = Sources(
+            lambda c, t: own(pack_ref, a, c, t) if c < 2 else band_ref[pl.ds(64 * a + 8 * t, 8), :]
+        )
+        here = [jnp.where(even, src.tile[1][t], src.tile[0][t]) for t in range(TILES)]
+        turned = [jnp.where(even, src.turned[1][t], src.turned[0][t]) for t in range(TILES)]
+        total = neighbour_sum(src, here, turned, kinds)
+        for half in range(2):
+            sum_near[pl.ds(16 * a + 8 * half, 8), :] = pack_quarters(total, half, jnp.logical_not(even))
+
+
+def far_sums(kept_ref, far_ref, pack_ref, band_ref, sum_far):
     lane = lanes()
     even = is_even("leaf")
     to_prev, to_next = (kept_ref[96 + i, 0].astype(jnp.int32) for i in (2, 3))
-    near_kinds = face_indices(
-        [jnp.where(even, pattern_row(pattern_ref, d, 1), pattern_row(pattern_ref, d, 0)) for d in range(6)]
-    )
     shift = jnp.where(even, 480, 224)
     window = [
         jnp.broadcast_to(far_ref[pl.ds(104 + d, 1), :], (8, LANES)).astype(jnp.int32) - shift
         for d in range(6)
     ]
     window = [jnp.where((w >= 0) & (w < 2 * SPILL), w, LANES - 1) for w in window]
-    far_kinds = [(w,) for w in face_rows(window)]
-    far_low, far_high = jnp.where(even, 0, SPILL), jnp.where(even, SPILL, 2 * SPILL)
-    far_lanes = (lane >= far_low) & (lane < far_high)
+    kinds = [(w,) for w in face_rows(window)]
+    far_low = jnp.where(even, 0, SPILL)
+    far_lanes = (lane >= far_low) & (lane < far_low + SPILL)
     mine = (lane < 2 * SPILL) & jnp.logical_not(far_lanes)
     given = far_lanes & (lane >= SPILL - to_prev) & (lane < SPILL + to_next)
-    unpack_by = jnp.where(even, 0, 32)
     for a in range(2):
 
-        def read(c, t):
-            if c < 2:
-                return pack_ref[pl.ds(128 * a + 64 * c + 8 * t, 8), :]
-            return band_ref[pl.ds(64 * a + 8 * t, 8), :]
-
-        src = Sources(read)
-        here = [jnp.where(even, src.tile[1][t], src.tile[0][t]) for t in range(TILES)]
-        turned = [jnp.where(even, src.turned[1][t], src.turned[0][t]) for t in range(TILES)]
-        total = neighbour_sum(src, here, turned, near_kinds)
-        for half in range(2):
-            sum_near[pl.ds(16 * a + 8 * half, 8), :] = pack_quarters(total, half, jnp.logical_not(even))
-
         def meet(_, t):
-            facing = spin(jnp.where(even, src.tile[0][t], src.tile[1][t]), 32)
-            return jnp.where(given, src.tile[2][t], jnp.where(mine, facing, 0.0))
+            facing = spin(jnp.where(even, own(pack_ref, a, 0, t), own(pack_ref, a, 1, t)), 32)
+            return jnp.where(given, band_ref[pl.ds(64 * a + 8 * t, 8), :], jnp.where(mine, facing, 0.0))
 
         joint = Sources(meet, 1)
-        total = neighbour_sum(joint, joint.tile[0], joint.turned[0], far_kinds)
+        total = neighbour_sum(joint, joint.tile[0], joint.turned[0], kinds)
         for t in range(TILES):
             part = far_ref[pl.ds(112 + 16 * a + 8 * (t % 2), 8), :]
-            part = spin(part, unpack_by - 32 * (t // 2))
+            part = spin(part, far_low - 32 * (t // 2))
             sum_far[pl.ds(64 * a + 8 * t, 8), :] = jnp.where(far_lanes, total[t] + part, 0.0)
 
 
@@ -427,7 +440,10 @@
     return weights[3] * (2.0 * phase - phase * phase * phase)
 
 
-def own_kernel(layers, table, pattern_ref, pack_ref, coef_ref, band_ref, half_ref):
+def own_kernel(
+    layers, table, pattern_ref, pack_ref, coef_ref, band_ref, kept_ref, far_ref, half_ref, sum_far
+):
+    far_sums(kept_ref, far_ref, pack_ref, band_ref, sum_far)
     group = lax.axis_index("gy")
     kinds = own_kinds(pattern_ref)
     weights = [weights_at(table, group, layers, a) for a in range(2)]
@@ -559,7 +575,7 @@
         [(104, LANES), field_old.shape, coef_old.shape],
         "hhhs",
         *stored, counts,
-        scratch=[pltpu.SMEM((OLD_SLOTS,), jnp.int32), pltpu.SemaphoreType.DMA((3,))],
+        scratch=[pltpu.VMEM((OLD_SLOTS,), jnp.int32), pltpu.SemaphoreType.DMA((3,))],
     )
     from_near = swap(to_near, "leaf", 0)
     ends_far, gone = call(
@@ -567,28 +583,29 @@
     )
     to_far, own_part, band_part = call(
         far_kernel,
-        [(144, LANES), (384, LANES), (192, LANES)],
-        "vvvvvvv",
-        field, coef, pattern, to_near, ends_far, gone, from_near,
+        [(144, LANES), (256, LANES), (128, LANES)],
+        "vvvvvv",
+        field, pattern, to_near, ends_far, gone, from_near,
     )
     from_far = swap(to_far, "leaf", 1)
+    coef_part, coef_side = call(
+        coef_kernel, [(128, LANES), (64, LANES)], "vvvv", coef, to_far, gone, from_near
+    )
     pack, pack_far, coef, band = call(
         place_kernel,
         [(288, LANES), (288, LANES), (128, LANES), (192, LANES)],
-        "vvvv",
-        to_far, own_part, band_part, from_far,
+        "vvvvvv",
+        to_far, own_part, band_part, coef_part, coef_side, from_far,
     )
     side_near = swap(pack, "gy", 0)
     side_far = swap(pack_far, "gy", 1)
-    sum_near, sum_far = call(
-        facing_kernel, [(32, LANES), (128, LANES)], "vvvvv", pattern, to_far, from_far, pack, band
-    )
+    (sum_near,) = call(facing_kernel, [(32, LANES)], "vvv", pattern, pack, band)
     sum_near = swap(sum_near, "leaf", 0)
-    (half,) = call(
+    half, sum_far = call(
         functools.partial(own_kernel, layers, table),
-        [(256, LANES)],
-        "vvvv",
-        pattern, pack, coef, band,
+        [(256, LANES), (128, LANES)],
+        "vvvvvv",
+        pattern, pack, coef, band, to_far, from_far,
     )
     once, twice = call(
         functools.partial(side_kernel, layers, table, False),

time: 31.7 us -> 31.4 us (level)
    pallas_call x8 -> x9, Pallas kernels: 4.36 us -> 4.43 us  [call(): pl.pallas_call(kernel, out_shape=[jax.ShapeDtypeStruct(s, F32) for s in s...]
  transfers between devices with their start and end apart: 5 -> 5, of which waited for: 3 -> 3; matrix products, arithmetic and copies ran while one was open for 0% -> 0% of each run, Pallas kernels for 4% -> 5%
where the time goes in v6:
time: 31.4 us; the launch traced here: 31.2 us
  starting transfers between devices  23.1 us (74%)
  Pallas kernels  4.43 us (14%)
  waiting for transfers between devices  2.86 us (9%)
  between operations  0.75 us (2%)
    ppermute x5, starting transfers between devices, swap(): return lax.ppermute(block, axis, route)  23.1 us
    pallas_call x9, Pallas kernels, call(): pl.pallas_call(kernel, out_shape=[jax.ShapeDtypeStruct(s, F32) for s in s...  4.43 us
    ppermute x5, waiting for transfers between devices, swap(): return lax.ppermute(block, axis, route)  2.86 us
  transfers between devices with their start and end apart: 5, of which 3 were waited for; matrix products, arithmetic and copies ran while one was open for 0% of the time, Pallas kernels for 5%

profile of v6, /device:TPU:57, one launch (start us, length us, event | category | flops | bytes accessed | tf_op | source)
XLA Modules:
  0.0 31.2 jit_solution(12023445881009450742)
XLA Ops:
  0.7 1.1 %shard_map.55 = (f32[104,128]{1,0:T(8,128)S(1)}, f32[2,64,320]{2,1,0:T(8,128)S(1)}, f32[64,320]{1,0:T(8,128)S(1)}) custom-call(f32[2,64,320]{2,1,0:T(8,128)} %field_hbm.1, f32[64,320]{1,0:T(8,128)} %coef_hbm.1, s32[320]{0:T(512)} %owner_hbm.1, s32[1]{0:T(128)S(6)} %copy.6.counts_ref), custom_call_target="tpu_custom_call" | custom-call | bytes 247044 | tf_op jit(solution)/shard_map/pallas_call | solution.py:559
  1.8 2.6 %collective-permute-start = (f32[104,128]{1,0:T(8,128)S(1)}, f32[104,128]{1,0:T(8,128)S(1)}, u32[]{:S(2)}, u32[]{:S(2)}) collective-permute-start(f32[104,128]{1,0:T(8,128)S(1)} %get-tuple-element.24.kept_ref), channel_id=1, source_target_pairs={{0,4},{4,0},{8,12},{12,8},{16,20},{20,16},{24,28},{28,24},{32,36},... | collective-permute-start | bytes 159752 | tf_op jit(solution)/shard_map/ppermute | solution.py:552
  4.4 0.0 copy-start
  4.4 0.2 shard_map.56
  4.6 0.7 %collective-permute-done.near_ref = f32[104,128]{1,0:T(8,128)S(1)} collective-permute-done((f32[104,128]{1,0:T(8,128)S(1)}, f32[104,128]{1,0:T(8,128)S(1)}, u32[]{:S(2)}, u32[]{:S(2)}) %collective-permute-start) | collective-permute-done | bytes 53280 | tf_op jit(solution)/shard_map/ppermute | solution.py:552
  5.3 0.0 copy-done
  5.3 0.5 %shard_map.57 = (f32[144,128]{1,0:T(8,128)S(1)}, f32[256,128]{1,0:T(8,128)S(1)}, f32[128,128]{1,0:T(8,128)S(1)}) custom-call(f32[2,64,320]{2,1,0:T(8,128)S(1)} %get-tuple-element.23.field_ref, s32[6,256]{1,0:T(8,128)S(1)} %copy-done, f32[104,128]{1,0:T(8,128)S(1)} %get-tuple-element.24.kept_ref, f32[96,128]{1,0:T(8,128)S(1)} %get-tuple-element.26.ends_ref, ...), custom_call_target="tpu_custom_call" | custom-call | bytes 423936 | tf_op jit(solution)/shard_map/pallas_call | solution.py:559
  5.8 4.2 %collective-permute-start.1 = (f32[144,128]{1,0:T(8,128)S(1)}, f32[144,128]{1,0:T(8,128)S(1)}, u32[]{:S(2)}, u32[]{:S(2)}) collective-permute-start(f32[144,128]{1,0:T(8,128)S(1)} %get-tuple-element.28.kept_ref), channel_id=1, source_target_pairs={{4,8},{8,4},{12,16},{16,12},{20,24},{24,20},{28,32},{32,28},{36,40... | collective-permute-start | bytes 221192 | tf_op jit(solution)/shard_map/ppermute | solution.py:552
  10.0 0.1 shard_map.58
  10.2 1.9 %collective-permute-done.1.far_ref = f32[144,128]{1,0:T(8,128)S(1)} collective-permute-done((f32[144,128]{1,0:T(8,128)S(1)}, f32[144,128]{1,0:T(8,128)S(1)}, u32[]{:S(2)}, u32[]{:S(2)}) %collective-permute-start.1) | collective-permute-done | bytes 73760 | tf_op jit(solution)/shard_map/ppermute | solution.py:552
  12.0 0.2 shard_map.59
  12.2 0.7 %collective-permute-start.4 = (f32[288,128]{1,0:T(8,128)S(1)}, f32[288,128]{1,0:T(8,128)S(1)}, u32[]{:S(2)}, u32[]{:S(2)}) collective-permute-start(f32[288,128]{1,0:T(8,128)S(1)} %get-tuple-element.38), channel_id=1, source_target_pairs={{1,2},{2,1},{5,6},{6,5},{9,10},{10,9},{13,14},{14,13},{17,18},{18,... | collective-permute-start | bytes 442376 | tf_op jit(solution)/shard_map/ppermute | solution.py:552
  12.9 5.6 %collective-permute-start.2 = (f32[288,128]{1,0:T(8,128)S(1)}, f32[288,128]{1,0:T(8,128)S(1)}, u32[]{:S(2)}, u32[]{:S(2)}) collective-permute-start(f32[288,128]{1,0:T(8,128)S(1)} %get-tuple-element.33.pack_ref), channel_id=1, source_target_pairs={{0,1},{1,0},{2,3},{3,2},{4,5},{5,4},{6,7},{7,6},{8,9},{9,8},{10,11... | collective-permute-start | bytes 442376 | tf_op jit(solution)/shard_map/ppermute | solution.py:552
  18.5 0.3 %shard_map.61 = f32[32,128]{1,0:T(8,128)S(1)} custom-call(s32[6,256]{1,0:T(8,128)S(1)} %copy-done, f32[288,128]{1,0:T(8,128)S(1)} %get-tuple-element.33.pack_ref, f32[192,128]{1,0:T(8,128)S(1)} %get-tuple-element.35.band_ref), custom_call_target="tpu_custom_call" | custom-call | bytes 251904 | tf_op jit(solution)/shard_map/pallas_call | solution.py:559
  18.8 10.1 %collective-permute-start.3 = (f32[32,128]{1,0:T(8,128)S(1)}, f32[32,128]{1,0:T(8,128)S(1)}, u32[]{:S(2)}, u32[]{:S(2)}) collective-permute-start(f32[32,128]{1,0:T(8,128)S(1)} %shard_map.61), channel_id=1, source_target_pairs={{0,4},{4,0},{8,12},{12,8},{16,20},{20,16},{24,28},{28,24},{32,36},... | collective-permute-start | bytes 49160 | tf_op jit(solution)/shard_map/ppermute | solution.py:552
  28.9 0.5 %shard_map.60 = (f32[256,128]{1,0:T(8,128)S(1)}, f32[128,128]{1,0:T(8,128)S(1)}) custom-call(s32[6,256]{1,0:T(8,128)S(1)} %copy-done, f32[288,128]{1,0:T(8,128)S(1)} %get-tuple-element.33.pack_ref, f32[128,128]{1,0:T(8,128)S(1)} %get-tuple-element.34.coef_ref, f32[192,128]{1,0:T(8,128)S(1)} %get-tuple-element.35.band_ref, ...), custom_call_target="tpu_custom_call" | custom-call | bytes 464896 | tf_op jit(solution)/shard_map/pallas_call | solution.py:559
  29.4 0.3 %collective-permute-done.3.sum_near = f32[32,128]{1,0:T(8,128)S(1)} collective-permute-done((f32[32,128]{1,0:T(8,128)S(1)}, f32[32,128]{1,0:T(8,128)S(1)}, u32[]{:S(2)}, u32[]{:S(2)}) %collective-permute-start.3) | collective-permute-done | bytes 16416 | tf_op jit(solution)/shard_map/ppermute | solution.py:552
  29.7 0.0 collective-permute-done.4.side_ref
  29.7 0.4 %shard_map.62 = (f32[128,128]{1,0:T(8,128)S(1)}, f32[128,128]{1,0:T(8,128)S(1)}) custom-call(s32[6,256]{1,0:T(8,128)S(1)} %copy-done, f32[288,128]{1,0:T(8,128)S(1)} %get-tuple-element.33.pack_ref, f32[128,128]{1,0:T(8,128)S(1)} %get-tuple-element.34.coef_ref, f32[192,128]{1,0:T(8,128)S(1)} %get-tuple-element.35.band_ref, ...), custom_call_target="tpu_custom_call" | custom-call | bytes 677888 | tf_op jit(solution)/shard_map/pallas_call | solution.py:559
  30.1 0.0 collective-permute-done.2.side_ref
  30.1 1.1 %shard_map.63 = f32[2,64,256]{2,1,0:T(8,128)} custom-call(s32[6,256]{1,0:T(8,128)S(1)} %copy-done, f32[288,128]{1,0:T(8,128)S(1)} %get-tuple-element.33.pack_ref, f32[128,128]{1,0:T(8,128)S(1)} %get-tuple-element.34.coef_ref, f32[192,128]{1,0:T(8,128)S(1)} %get-tuple-element.35.band_ref, f32[256,128]{1,0:T(8,128)S(1)} %get-tuple-element.36.half_ref, ...), custom_call_target="tpu_custom_call" | custom-call | bytes 808960 | tf_op jit(solution)/shard_map/pallas_call | solution.py:559
Async XLA Ops:
  1.8 3.5 %collective-permute-start = (f32[104,128]{1,0:T(8,128)S(1)}, f32[104,128]{1,0:T(8,128)S(1)}, u32[]{:S(2)}, u32[]{:S(2)}) collective-permute-start(f32[104,128]{1,0:T(8,128)S(1)} %get-tuple-element.24.kept_ref), channel_id=1, source_target_pairs={{0,4},{4,0},{8,12},{12,8},{16,20},{20,16},{24,28},{28,24},{32,36},... | collective-permute-start | bytes 159752 | tf_op jit(solution)/shard_map/ppermute | solution.py:552
  4.4 0.9 %copy-start = (s32[6,256]{1,0:T(8,128)S(1)}, s32[6,256]{1,0:T(8,128)}, u32[]{:S(2)}) copy-start(s32[6,256]{1,0:T(8,128)} %pattern_ref.9) | copy-start | bytes 18436
  5.8 6.3 %collective-permute-start.1 = (f32[144,128]{1,0:T(8,128)S(1)}, f32[144,128]{1,0:T(8,128)S(1)}, u32[]{:S(2)}, u32[]{:S(2)}) collective-permute-start(f32[144,128]{1,0:T(8,128)S(1)} %get-tuple-element.28.kept_ref), channel_id=1, source_target_pairs={{4,8},{8,4},{12,16},{16,12},{20,24},{24,20},{28,32},{32,28},{36,40... | collective-permute-start | bytes 221192 | tf_op jit(solution)/shard_map/ppermute | solution.py:552
  12.2 17.5 %collective-permute-start.4 = (f32[288,128]{1,0:T(8,128)S(1)}, f32[288,128]{1,0:T(8,128)S(1)}, u32[]{:S(2)}, u32[]{:S(2)}) collective-permute-start(f32[288,128]{1,0:T(8,128)S(1)} %get-tuple-element.38), channel_id=1, source_target_pairs={{1,2},{2,1},{5,6},{6,5},{9,10},{10,9},{13,14},{14,13},{17,18},{18,... | collective-permute-start | bytes 442376 | tf_op jit(solution)/shard_map/ppermute | solution.py:552
  12.9 17.2 %collective-permute-start.2 = (f32[288,128]{1,0:T(8,128)S(1)}, f32[288,128]{1,0:T(8,128)S(1)}, u32[]{:S(2)}, u32[]{:S(2)}) collective-permute-start(f32[288,128]{1,0:T(8,128)S(1)} %get-tuple-element.33.pack_ref), channel_id=1, source_target_pairs={{0,1},{1,0},{2,3},{3,2},{4,5},{5,4},{6,7},{7,6},{8,9},{9,8},{10,11... | collective-permute-start | bytes 442376 | tf_op jit(solution)/shard_map/ppermute | solution.py:552
  18.8 10.9 %collective-permute-start.3 = (f32[32,128]{1,0:T(8,128)S(1)}, f32[32,128]{1,0:T(8,128)S(1)}, u32[]{:S(2)}, u32[]{:S(2)}) collective-permute-start(f32[32,128]{1,0:T(8,128)S(1)} %shard_map.61), channel_id=1, source_target_pairs={{0,4},{4,0},{8,12},{12,8},{16,20},{20,16},{24,28},{28,24},{32,36},... | collective-permute-start | bytes 49160 | tf_op jit(solution)/shard_map/ppermute | solution.py:552

commit v7 on v6

--- a/solution.py
+++ b/solution.py
@@ -462,33 +462,33 @@
                 half_ref[pl.ds(128 * a + 64 * c + 8 * t, 8), :] = (1.0 - OMEGA) * now + gain * push
 
 
+def at(base, offset):
+    return pl.ds(pl.multiple_of(base + offset, 8), 8)
+
+
+def side_weights(layers, table, upper):
+    group = lax.axis_index("gy")
+    lower, first, second, over = (weights_at(table, group, layers, o) for o in (-1, 0, 1, 2))
+    own_w = [jnp.where(upper, u, v) for u, v in zip(second, first)]
+    side_w = [jnp.where(upper, u, v) for u, v in zip(over, lower)]
+
+    def link(weights, outward):
+        return jnp.where(upper == outward, weights[2], weights[1])
+
+    return own_w, side_w, link(own_w, True), link(own_w, False), link(side_w, False), link(side_w, True)
+
+
 def side_kernel(
-    layers, table, final,
-    pattern_ref, pack_ref, coef_ref, band_ref, half_ref, side_ref, sum_near, sum_far, *refs,
+    layers, table, near_side,
+    pattern_ref, pack_ref, coef_ref, band_ref, half_ref, side_ref, once_ref, next_ref, edge_ref,
 ):
-    if final:
-        other_once, other_twice, out_ref, next_own, next_band, next_side = refs
-    else:
-        next_own, twice_ref, next_band, next_side = refs
-    lane = lanes()
-    group = lax.axis_index("gy")
-    even = is_even("leaf")
-    upper = is_even("gy") if final else jnp.logical_not(is_even("gy"))
+    lane = lanes()
+    upper = is_even("gy") if near_side else jnp.logical_not(is_even("gy"))
     a = jnp.where(upper, 1, 0)
-    unpack_by = jnp.where(even, SPILL, 0)
-    near_lanes = (lane >= unpack_by) & (lane < unpack_by + SPILL)
     kinds = own_kinds(pattern_ref)
-    w_lower, w_first, w_second, w_upper = (weights_at(table, group, layers, o) for o in (-1, 0, 1, 2))
-    w_own = [jnp.where(upper, u, v) for u, v in zip(w_second, w_first)]
-    w_side = [jnp.where(upper, u, v) for u, v in zip(w_upper, w_lower)]
-    own_to_side, own_to_other = jnp.where(upper, w_own[2], w_own[1]), jnp.where(upper, w_own[1], w_own[2])
-    side_to_own, side_to_next = jnp.where(upper, w_side[1], w_side[2]), jnp.where(upper, w_side[2], w_side[1])
-    other_link = jnp.where(upper, w_first[2], w_second[1])
-    w_other = [jnp.where(upper, u, v) for u, v in zip(w_first, w_second)]
-
-    def at(base, offset):
-        return pl.ds(pl.multiple_of(base + offset, 8), 8)
-
+    w_own, w_side, own_to_side, own_to_other, side_to_own, side_to_next = side_weights(
+        layers, table, upper
+    )
     here, there = 128 * a, 128 * (1 - a)
 
     def side_band(t):
@@ -499,17 +499,15 @@
         for t in range(TILES):
             k = 64 * c + 8 * t
             _, gain = gains(w_own, coef_ref[pl.ds(k, 8), :])
-            next_own[pl.ds(k, 8), :] = (
+            once_ref[pl.ds(k, 8), :] = (
                 half_ref[at(here, k), :] + gain * own_to_side * side_ref[at(there, k), :]
             )
     for t in range(TILES):
         now = band_ref[at(64 * a, 8 * t), :]
-        spread, gain = gains(w_own, band_ref[pl.ds(128 + 8 * t, 8), :])
-        near = spin(sum_near[at(16 * a, 8 * (t % 2)), :], unpack_by - 32 * (t // 2))
-        total = jnp.where(near_lanes, near, sum_far[at(64 * a, 8 * t), :])
-        push = spread * total + own_to_side * side_band(t) + bulge(w_own, now)
+        _, gain = gains(w_own, band_ref[pl.ds(128 + 8 * t, 8), :])
+        push = own_to_side * side_band(t) + bulge(w_own, now)
         push = push + own_to_other * band_ref[at(64 * (1 - a), 8 * t), :]
-        next_band[pl.ds(8 * t, 8), :] = (1.0 - OMEGA) * now + gain * push
+        edge_ref[pl.ds(8 * t, 8), :] = (1.0 - OMEGA) * now + gain * push
 
     src = Sources(lambda c, t: side_ref[at(there, 64 * c + 8 * t), :] if c < 2 else side_band(t))
     for c in range(2):
@@ -519,30 +517,56 @@
             spread, gain = gains(w_side, coef_ref[pl.ds(k, 8), :])
             push = spread * total[t] + side_to_own * pack_ref[at(here, k), :]
             push = push + side_to_next * side_ref[at(here, k), :]
-            next_side[pl.ds(k, 8), :] = (1.0 - OMEGA) * src.tile[c][t] + gain * push
-
-    src = Sources(
-        lambda c, t: next_own[pl.ds(64 * c + 8 * t, 8), :] if c < 2 else next_band[pl.ds(8 * t, 8), :]
-    )
-    for c in range(2):
-        total = neighbour_sum(src, src.tile[c], src.turned[c], kinds[c])
+            next_ref[pl.ds(k, 8), :] = (1.0 - OMEGA) * src.tile[c][t] + gain * push
+
+
+def final_kernel(
+    layers, table,
+    pattern_ref, pack_ref, coef_ref, band_ref, sum_near, sum_far,
+    far_once, far_next, far_edge, near_once, near_next, near_edge,
+    out_hbm, edge_ref, left_ref, right_ref, sems,
+):
+    even = is_even("leaf")
+    unpack_by = jnp.where(even, SPILL, 0)
+    lane = lanes()
+    near_lanes = (lane >= unpack_by) & (lane < unpack_by + SPILL)
+    kinds = own_kinds(pattern_ref)
+    sides = []
+    for side, (once, next, edge) in enumerate(
+        ((near_once, near_next, near_edge), (far_once, far_next, far_edge))
+    ):
+        upper = jnp.logical_not(is_even("gy")) if side else is_even("gy")
+        a = jnp.where(upper, 1, 0)
+        w_own, _, own_to_side, own_to_other, _, _ = side_weights(layers, table, upper)
         for t in range(TILES):
-            k = 64 * c + 8 * t
-            coef = coef_ref[pl.ds(k, 8), :]
-            spread, gain = gains(w_own, coef)
-            once = src.tile[c][t]
-            push = spread * total[t] + own_to_side * next_side[pl.ds(k, 8), :]
-            push = push + bulge(w_own, pack_ref[at(here, k), :])
-            if not final:
-                twice_ref[pl.ds(k, 8), :] = (1.0 - OMEGA) * once + gain * push
-                continue
-            push = push + own_to_other * other_once[pl.ds(k, 8), :]
-            _, other_gain = gains(w_other, coef)
-            lanes_at = pl.ds(LANES * c, LANES)
-            out_ref[a, pl.ds(8 * t, 8), lanes_at] = (1.0 - OMEGA) * once + gain * push
-            out_ref[1 - a, pl.ds(8 * t, 8), lanes_at] = (
-                other_twice[pl.ds(k, 8), :] + other_gain * other_link * once
-            )
+            spread, gain = gains(w_own, band_ref[pl.ds(128 + 8 * t, 8), :])
+            near = spin(sum_near[at(16 * a, 8 * (t % 2)), :], unpack_by - 32 * (t // 2))
+            total = jnp.where(near_lanes, near, sum_far[at(64 * a, 8 * t), :])
+            k = 64 * side + 8 * t
+            edge_ref[pl.ds(k, 8), :] = edge[pl.ds(8 * t, 8), :] + gain * (spread * total)
+
+        def read(c, t):
+            return once[pl.ds(64 * c + 8 * t, 8), :] if c < 2 else edge_ref[pl.ds(64 * side + 8 * t, 8), :]
+
+        sides.append((a, w_own, own_to_side, own_to_other, Sources(read), next))
+    copies = []
+    for c, buffer in enumerate((left_ref, right_ref)):
+        for side, (a, w_own, own_to_side, own_to_other, src, next) in enumerate(sides):
+            other = sides[1 - side][4]
+            total = neighbour_sum(src, src.tile[c], src.turned[c], kinds[c])
+            for t in range(TILES):
+                k = 64 * c + 8 * t
+                spread, gain = gains(w_own, coef_ref[pl.ds(k, 8), :])
+                push = spread * total[t] + own_to_side * next[pl.ds(k, 8), :]
+                push = push + own_to_other * other.tile[c][t]
+                push = push + bulge(w_own, pack_ref[at(128 * a, k), :])
+                buffer[a, pl.ds(8 * t, 8), :] = (1.0 - OMEGA) * src.tile[c][t] + gain * push
+        copies.append(
+            pltpu.make_async_copy(buffer, out_hbm.at[:, :, pl.ds(LANES * c, LANES)], sems.at[c])
+        )
+        copies[-1].start()
+    for copy in copies:
+        copy.wait()
 
 
 def swap(block, axis, first):
@@ -552,7 +576,7 @@
     return lax.ppermute(block, axis, route)
 
 
-def call(kernel, shapes, spaces, *operands, scratch=(), flops=0):
+def call(kernel, shapes, spaces, *operands, scratch=(), out_space=pltpu.VMEM):
     vmem = pltpu.VMEM
     space = {"h": pltpu.HBM, "v": vmem, "s": pltpu.SMEM}
     moved = sum(4 * int(np.prod(o.shape)) for o in operands)
@@ -560,10 +584,10 @@
         kernel,
         out_shape=[jax.ShapeDtypeStruct(s, F32) for s in shapes],
         in_specs=[pl.BlockSpec(memory_space=space[s]) for s in spaces],
-        out_specs=[pl.BlockSpec(memory_space=vmem) for _ in shapes],
+        out_specs=[pl.BlockSpec(memory_space=out_space) for _ in shapes],
         scratch_shapes=list(scratch),
         compiler_params=pltpu.CompilerParams(vmem_limit_bytes=16 * 2**20),
-        cost_estimate=pl.CostEstimate(flops=flops, bytes_accessed=moved, transcendentals=0),
+        cost_estimate=pl.CostEstimate(flops=0, bytes_accessed=moved, transcendentals=0),
     )(*operands)
 
 
@@ -607,19 +631,23 @@
         "vvvvvv",
         pattern, pack, coef, band, to_far, from_far,
     )
-    once, twice = call(
-        functools.partial(side_kernel, layers, table, False),
-        [(128, LANES), (128, LANES)],
-        "vvvvvvvv",
-        pattern, pack, coef, band, half, side_far, sum_near, sum_far,
-        scratch=[pltpu.VMEM((64, LANES), F32), pltpu.VMEM((128, LANES), F32)],
-    )
+    sides = []
+    for near_side, side in ((True, side_near), (False, side_far)):
+        sides += call(
+            functools.partial(side_kernel, layers, table, near_side),
+            [(128, LANES), (128, LANES), (64, LANES)],
+            "vvvvvv",
+            pattern, pack, coef, band, half, side,
+        )
     (out,) = call(
-        functools.partial(side_kernel, layers, table, True),
+        functools.partial(final_kernel, layers, table),
         [(layers, 64, BRICKS_DEV)],
-        "vvvvvvvvvv",
-        pattern, pack, coef, band, half, side_near, sum_near, sum_far, once, twice,
-        scratch=[pltpu.VMEM((rows, LANES), F32) for rows in (128, 64, 128)],
+        "v" * 12,
+        pattern, pack, coef, band, sum_near, sum_far, *sides[3:], *sides[:3],
+        out_space=pltpu.HBM,
+        scratch=[pltpu.VMEM((128, LANES), F32)]
+        + [pltpu.VMEM((layers, 64, LANES), F32)] * 2
+        + [pltpu.SemaphoreType.DMA((2,))],
     )
     return out
 

time: 31.4 us -> 30.9 us (0.984)
  the two profiles are of different devices: /device:TPU:57 before, /device:TPU:51 now
where the time goes in v7:
time: 30.9 us; the launch traced here: 30.6 us
  starting transfers between devices  22.8 us (74%)
  Pallas kernels  4.48 us (14%)
  waiting for transfers between devices  2.53 us (8%)
  between operations  0.77 us (2%)
    ppermute x5, starting transfers between devices, swap(): return lax.ppermute(block, axis, route)  22.8 us
    pallas_call x10, Pallas kernels, call(): pl.pallas_call(kernel, out_shape=[jax.ShapeDtypeStruct(s, F32) for s in s...  4.48 us
    ppermute x5, waiting for transfers between devices, swap(): return lax.ppermute(block, axis, route)  2.53 us
  transfers between devices with their start and end apart: 5, of which 2 were waited for; matrix products, arithmetic and copies ran while one was open for 0% of the time, Pallas kernels for 5%

profile of v7, /device:TPU:51, one launch (start us, length us, event | category | flops | bytes accessed | tf_op | source)
XLA Modules:
  0.0 30.6 jit_solution(15126361933387619733)
XLA Ops:
  0.7 1.1 %shard_map.55 = (f32[104,128]{1,0:T(8,128)S(1)}, f32[2,64,320]{2,1,0:T(8,128)S(1)}, f32[64,320]{1,0:T(8,128)S(1)}) custom-call(f32[2,64,320]{2,1,0:T(8,128)} %field_hbm.1, f32[64,320]{1,0:T(8,128)} %coef_hbm.1, s32[320]{0:T(512)} %owner_hbm.1, s32[1]{0:T(128)S(6)} %copy.6.counts_ref), custom_call_target="tpu_custom_call" | custom-call | bytes 247044 | tf_op jit(solution)/shard_map/pallas_call | solution.py:583
  1.8 2.6 %collective-permute-start = (f32[104,128]{1,0:T(8,128)S(1)}, f32[104,128]{1,0:T(8,128)S(1)}, u32[]{:S(2)}, u32[]{:S(2)}) collective-permute-start(f32[104,128]{1,0:T(8,128)S(1)} %get-tuple-element.28.kept_ref), channel_id=1, source_target_pairs={{0,4},{4,0},{8,12},{12,8},{16,20},{20,16},{24,28},{28,24},{32,36},... | collective-permute-start | bytes 159752 | tf_op jit(solution)/shard_map/ppermute | solution.py:576
  4.4 0.0 copy-start
  4.4 0.2 shard_map.56
  4.6 0.7 %collective-permute-done.near_ref = f32[104,128]{1,0:T(8,128)S(1)} collective-permute-done((f32[104,128]{1,0:T(8,128)S(1)}, f32[104,128]{1,0:T(8,128)S(1)}, u32[]{:S(2)}, u32[]{:S(2)}) %collective-permute-start) | collective-permute-done | bytes 53280 | tf_op jit(solution)/shard_map/ppermute | solution.py:576
  5.3 0.0 copy-done
  5.3 0.5 %shard_map.57 = (f32[144,128]{1,0:T(8,128)S(1)}, f32[256,128]{1,0:T(8,128)S(1)}, f32[128,128]{1,0:T(8,128)S(1)}) custom-call(f32[2,64,320]{2,1,0:T(8,128)S(1)} %get-tuple-element.27.field_ref, s32[6,256]{1,0:T(8,128)S(1)} %copy-done, f32[104,128]{1,0:T(8,128)S(1)} %get-tuple-element.28.kept_ref, f32[96,128]{1,0:T(8,128)S(1)} %get-tuple-element.30.ends_ref, ...), custom_call_target="tpu_custom_call" | custom-call | bytes 423936 | tf_op jit(solution)/shard_map/pallas_call | solution.py:583
  5.8 4.2 %collective-permute-start.1 = (f32[144,128]{1,0:T(8,128)S(1)}, f32[144,128]{1,0:T(8,128)S(1)}, u32[]{:S(2)}, u32[]{:S(2)}) collective-permute-start(f32[144,128]{1,0:T(8,128)S(1)} %get-tuple-element.32.kept_ref), channel_id=1, source_target_pairs={{4,8},{8,4},{12,16},{16,12},{20,24},{24,20},{28,32},{32,28},{36,40... | collective-permute-start | bytes 221192 | tf_op jit(solution)/shard_map/ppermute | solution.py:576
  10.0 0.1 shard_map.58
  10.2 1.9 %collective-permute-done.1.far_ref = f32[144,128]{1,0:T(8,128)S(1)} collective-permute-done((f32[144,128]{1,0:T(8,128)S(1)}, f32[144,128]{1,0:T(8,128)S(1)}, u32[]{:S(2)}, u32[]{:S(2)}) %collective-permute-start.1) | collective-permute-done | bytes 73760 | tf_op jit(solution)/shard_map/ppermute | solution.py:576
  12.0 0.2 shard_map.59
  12.2 2.2 %collective-permute-start.4 = (f32[288,128]{1,0:T(8,128)S(1)}, f32[288,128]{1,0:T(8,128)S(1)}, u32[]{:S(2)}, u32[]{:S(2)}) collective-permute-start(f32[288,128]{1,0:T(8,128)S(1)} %get-tuple-element.37.pack_ref), channel_id=1, source_target_pairs={{0,1},{1,0},{2,3},{3,2},{4,5},{5,4},{6,7},{7,6},{8,9},{9,8},{10,11... | collective-permute-start | bytes 442376 | tf_op jit(solution)/shard_map/ppermute | solution.py:576
  14.4 3.8 %collective-permute-start.3 = (f32[288,128]{1,0:T(8,128)S(1)}, f32[288,128]{1,0:T(8,128)S(1)}, u32[]{:S(2)}, u32[]{:S(2)}) collective-permute-start(f32[288,128]{1,0:T(8,128)S(1)} %get-tuple-element.42), channel_id=1, source_target_pairs={{1,2},{2,1},{5,6},{6,5},{9,10},{10,9},{13,14},{14,13},{17,18},{18,... | collective-permute-start | bytes 442376 | tf_op jit(solution)/shard_map/ppermute | solution.py:576
  18.2 0.3 %shard_map.60 = f32[32,128]{1,0:T(8,128)S(1)} custom-call(s32[6,256]{1,0:T(8,128)S(1)} %copy-done, f32[288,128]{1,0:T(8,128)S(1)} %get-tuple-element.37.pack_ref, f32[192,128]{1,0:T(8,128)S(1)} %get-tuple-element.39.band_ref), custom_call_target="tpu_custom_call" | custom-call | bytes 251904 | tf_op jit(solution)/shard_map/pallas_call | solution.py:583
  18.5 10.1 %collective-permute-start.2 = (f32[32,128]{1,0:T(8,128)S(1)}, f32[32,128]{1,0:T(8,128)S(1)}, u32[]{:S(2)}, u32[]{:S(2)}) collective-permute-start(f32[32,128]{1,0:T(8,128)S(1)} %shard_map.60), channel_id=1, source_target_pairs={{0,4},{4,0},{8,12},{12,8},{16,20},{20,16},{24,28},{28,24},{32,36},... | collective-permute-start | bytes 49160 | tf_op jit(solution)/shard_map/ppermute | solution.py:576
  28.6 0.5 %shard_map.61 = (f32[256,128]{1,0:T(8,128)S(1)}, f32[128,128]{1,0:T(8,128)S(1)}) custom-call(s32[6,256]{1,0:T(8,128)S(1)} %copy-done, f32[288,128]{1,0:T(8,128)S(1)} %get-tuple-element.37.pack_ref, f32[128,128]{1,0:T(8,128)S(1)} %get-tuple-element.38.coef_ref, f32[192,128]{1,0:T(8,128)S(1)} %get-tuple-element.39.band_ref, ...), custom_call_target="tpu_custom_call" | custom-call | bytes 464896 | tf_op jit(solution)/shard_map/pallas_call | solution.py:583
  29.1 0.0 collective-permute-done.4.side_ref
  29.1 0.2 shard_map.63
  29.3 0.0 collective-permute-done.3.side_ref
  29.3 0.2 shard_map.62
  29.6 0.0 collective-permute-done.2.sum_near
  29.6 1.0 %shard_map.64 = f32[2,64,256]{2,1,0:T(8,128)} custom-call(s32[6,256]{1,0:T(8,128)S(1)} %copy-done, f32[288,128]{1,0:T(8,128)S(1)} %get-tuple-element.37.pack_ref, f32[128,128]{1,0:T(8,128)S(1)} %get-tuple-element.38.coef_ref, f32[192,128]{1,0:T(8,128)S(1)} %get-tuple-element.39.band_ref, f32[32,128]{1,0:T(8,128)S(1)} %collective-permute-done.2.sum_near, ...), custom_call_target="tpu_custom_call" | custom-call | bytes 727040 | tf_op jit(solution)/shard_map/pallas_call | solution.py:583
Async XLA Ops:
  1.8 3.5 %collective-permute-start = (f32[104,128]{1,0:T(8,128)S(1)}, f32[104,128]{1,0:T(8,128)S(1)}, u32[]{:S(2)}, u32[]{:S(2)}) collective-permute-start(f32[104,128]{1,0:T(8,128)S(1)} %get-tuple-element.28.kept_ref), channel_id=1, source_target_pairs={{0,4},{4,0},{8,12},{12,8},{16,20},{20,16},{24,28},{28,24},{32,36},... | collective-permute-start | bytes 159752 | tf_op jit(solution)/shard_map/ppermute | solution.py:576
  4.4 0.9 %copy-start = (s32[6,256]{1,0:T(8,128)S(1)}, s32[6,256]{1,0:T(8,128)}, u32[]{:S(2)}) copy-start(s32[6,256]{1,0:T(8,128)} %pattern_ref.11) | copy-start | bytes 18436
  5.8 6.3 %collective-permute-start.1 = (f32[144,128]{1,0:T(8,128)S(1)}, f32[144,128]{1,0:T(8,128)S(1)}, u32[]{:S(2)}, u32[]{:S(2)}) collective-permute-start(f32[144,128]{1,0:T(8,128)S(1)} %get-tuple-element.32.kept_ref), channel_id=1, source_target_pairs={{4,8},{8,4},{12,16},{16,12},{20,24},{24,20},{28,32},{32,28},{36,40... | collective-permute-start | bytes 221192 | tf_op jit(solution)/shard_map/ppermute | solution.py:576
  12.2 16.9 %collective-permute-start.4 = (f32[288,128]{1,0:T(8,128)S(1)}, f32[288,128]{1,0:T(8,128)S(1)}, u32[]{:S(2)}, u32[]{:S(2)}) collective-permute-start(f32[288,128]{1,0:T(8,128)S(1)} %get-tuple-element.37.pack_ref), channel_id=1, source_target_pairs={{0,1},{1,0},{2,3},{3,2},{4,5},{5,4},{6,7},{7,6},{8,9},{9,8},{10,11... | collective-permute-start | bytes 442376 | tf_op jit(solution)/shard_map/ppermute | solution.py:576
  14.4 14.9 %collective-permute-start.3 = (f32[288,128]{1,0:T(8,128)S(1)}, f32[288,128]{1,0:T(8,128)S(1)}, u32[]{:S(2)}, u32[]{:S(2)}) collective-permute-start(f32[288,128]{1,0:T(8,128)S(1)} %get-tuple-element.42), channel_id=1, source_target_pairs={{1,2},{2,1},{5,6},{6,5},{9,10},{10,9},{13,14},{14,13},{17,18},{18,... | collective-permute-start | bytes 442376 | tf_op jit(solution)/shard_map/ppermute | solution.py:576
  18.5 11.1 %collective-permute-start.2 = (f32[32,128]{1,0:T(8,128)S(1)}, f32[32,128]{1,0:T(8,128)S(1)}, u32[]{:S(2)}, u32[]{:S(2)}) collective-permute-start(f32[32,128]{1,0:T(8,128)S(1)} %shard_map.60), channel_id=1, source_target_pairs={{0,4},{4,0},{8,12},{12,8},{16,20},{20,16},{24,28},{28,24},{32,36},... | collective-permute-start | bytes 49160 | tf_op jit(solution)/shard_map/ppermute | solution.py:576

commit v8 on v7

--- a/solution.py
+++ b/solution.py
@@ -522,10 +522,14 @@
 
 def final_kernel(
     layers, table,
-    pattern_ref, pack_ref, coef_ref, band_ref, sum_near, sum_far,
-    far_once, far_next, far_edge, near_once, near_next, near_edge,
-    out_hbm, edge_ref, left_ref, right_ref, sems,
+    pattern_ref, pack_ref, coef_ref, band_ref, half_ref, side_ref, sum_near, sum_far,
+    near_once, near_next, near_edge,
+    out_hbm, far_once, far_next, far_edge, edge_ref, left_ref, right_ref, sems,
 ):
+    side_kernel(
+        layers, table, False,
+        pattern_ref, pack_ref, coef_ref, band_ref, half_ref, side_ref, far_once, far_next, far_edge,
+    )
     even = is_even("leaf")
     unpack_by = jnp.where(even, SPILL, 0)
     lane = lanes()
@@ -560,11 +564,10 @@
                 push = spread * total[t] + own_to_side * next[pl.ds(k, 8), :]
                 push = push + own_to_other * other.tile[c][t]
                 push = push + bulge(w_own, pack_ref[at(128 * a, k), :])
-                buffer[a, pl.ds(8 * t, 8), :] = (1.0 - OMEGA) * src.tile[c][t] + gain * push
-        copies.append(
-            pltpu.make_async_copy(buffer, out_hbm.at[:, :, pl.ds(LANES * c, LANES)], sems.at[c])
-        )
-        copies[-1].start()
+                buffer[side, pl.ds(8 * t, 8), :] = (1.0 - OMEGA) * src.tile[c][t] + gain * push
+            target = out_hbm.at[a, :, pl.ds(LANES * c, LANES)]
+            copies.append(pltpu.make_async_copy(buffer.at[side], target, sems.at[2 * c + side]))
+            copies[-1].start()
     for copy in copies:
         copy.wait()
 
@@ -631,23 +634,21 @@
         "vvvvvv",
         pattern, pack, coef, band, to_far, from_far,
     )
-    sides = []
-    for near_side, side in ((True, side_near), (False, side_far)):
-        sides += call(
-            functools.partial(side_kernel, layers, table, near_side),
-            [(128, LANES), (128, LANES), (64, LANES)],
-            "vvvvvv",
-            pattern, pack, coef, band, half, side,
-        )
+    facing = call(
+        functools.partial(side_kernel, layers, table, True),
+        [(128, LANES), (128, LANES), (64, LANES)],
+        "vvvvvv",
+        pattern, pack, coef, band, half, side_near,
+    )
     (out,) = call(
         functools.partial(final_kernel, layers, table),
         [(layers, 64, BRICKS_DEV)],
-        "v" * 12,
-        pattern, pack, coef, band, sum_near, sum_far, *sides[3:], *sides[:3],
+        "v" * 11,
+        pattern, pack, coef, band, half, side_far, sum_near, sum_far, *facing,
         out_space=pltpu.HBM,
-        scratch=[pltpu.VMEM((128, LANES), F32)]
+        scratch=[pltpu.VMEM((rows, LANES), F32) for rows in (128, 128, 64, 128)]
         + [pltpu.VMEM((layers, 64, LANES), F32)] * 2
-        + [pltpu.SemaphoreType.DMA((2,))],
+        + [pltpu.SemaphoreType.DMA((4,))],
     )
     return out
 

time: 30.9 us -> 30.9 us (level)
    pallas_call x10 -> x9, Pallas kernels: 4.48 us -> 4.44 us  [call(): pl.pallas_call(kernel, out_shape=[jax.ShapeDtypeStruct(s, F32) for s in s...]
  transfers between devices with their start and end apart: 5 -> 5, of which waited for: 2 -> 3; matrix products, arithmetic and copies ran while one was open for 0% -> 0% of each run, Pallas kernels for 5% -> 4%
where the time goes in v8:
time: 30.9 us; the launch traced here: 30.7 us
  starting transfers between devices  22.8 us (74%)
  Pallas kernels  4.44 us (14%)
  waiting for transfers between devices  2.61 us (8%)
  between operations  0.75 us (2%)
    ppermute x5, starting transfers between devices, swap(): return lax.ppermute(block, axis, route)  22.8 us
    pallas_call x9, Pallas kernels, call(): pl.pallas_call(kernel, out_shape=[jax.ShapeDtypeStruct(s, F32) for s in s...  4.44 us
    ppermute x5, waiting for transfers between devices, swap(): return lax.ppermute(block, axis, route)  2.61 us
  transfers between devices with their start and end apart: 5, of which 3 were waited for; matrix products, arithmetic and copies ran while one was open for 0% of the time, Pallas kernels for 4%

profile of v8, /device:TPU:51, one launch (start us, length us, event | category | flops | bytes accessed | tf_op | source)
XLA Modules:
  0.0 30.7 jit_solution(16757309992852742709)
XLA Ops:
  0.7 1.1 %shard_map.55 = (f32[104,128]{1,0:T(8,128)S(1)}, f32[2,64,320]{2,1,0:T(8,128)S(1)}, f32[64,320]{1,0:T(8,128)S(1)}) custom-call(f32[2,64,320]{2,1,0:T(8,128)} %field_hbm.1, f32[64,320]{1,0:T(8,128)} %coef_hbm.1, s32[320]{0:T(512)} %owner_hbm.1, s32[1]{0:T(128)S(6)} %copy.6.counts_ref), custom_call_target="tpu_custom_call" | custom-call | bytes 247044 | tf_op jit(solution)/shard_map/pallas_call | solution.py:586
  1.8 2.6 %collective-permute-start = (f32[104,128]{1,0:T(8,128)S(1)}, f32[104,128]{1,0:T(8,128)S(1)}, u32[]{:S(2)}, u32[]{:S(2)}) collective-permute-start(f32[104,128]{1,0:T(8,128)S(1)} %get-tuple-element.25.kept_ref), channel_id=1, source_target_pairs={{0,4},{4,0},{8,12},{12,8},{16,20},{20,16},{24,28},{28,24},{32,36},... | collective-permute-start | bytes 159752 | tf_op jit(solution)/shard_map/ppermute | solution.py:579
  4.4 0.0 copy-start
  4.4 0.2 shard_map.56
  4.6 0.7 %collective-permute-done.near_ref = f32[104,128]{1,0:T(8,128)S(1)} collective-permute-done((f32[104,128]{1,0:T(8,128)S(1)}, f32[104,128]{1,0:T(8,128)S(1)}, u32[]{:S(2)}, u32[]{:S(2)}) %collective-permute-start) | collective-permute-done | bytes 53280 | tf_op jit(solution)/shard_map/ppermute | solution.py:579
  5.3 0.0 copy-done
  5.3 0.5 %shard_map.57 = (f32[144,128]{1,0:T(8,128)S(1)}, f32[256,128]{1,0:T(8,128)S(1)}, f32[128,128]{1,0:T(8,128)S(1)}) custom-call(f32[2,64,320]{2,1,0:T(8,128)S(1)} %get-tuple-element.24.field_ref, s32[6,256]{1,0:T(8,128)S(1)} %copy-done, f32[104,128]{1,0:T(8,128)S(1)} %get-tuple-element.25.kept_ref, f32[96,128]{1,0:T(8,128)S(1)} %get-tuple-element.27.ends_ref, ...), custom_call_target="tpu_custom_call" | custom-call | bytes 423936 | tf_op jit(solution)/shard_map/pallas_call | solution.py:586
  5.8 4.2 %collective-permute-start.1 = (f32[144,128]{1,0:T(8,128)S(1)}, f32[144,128]{1,0:T(8,128)S(1)}, u32[]{:S(2)}, u32[]{:S(2)}) collective-permute-start(f32[144,128]{1,0:T(8,128)S(1)} %get-tuple-element.29.kept_ref), channel_id=1, source_target_pairs={{4,8},{8,4},{12,16},{16,12},{20,24},{24,20},{28,32},{32,28},{36,40... | collective-permute-start | bytes 221192 | tf_op jit(solution)/shard_map/ppermute | solution.py:579
  10.0 0.1 shard_map.58
  10.2 1.9 %collective-permute-done.1.far_ref = f32[144,128]{1,0:T(8,128)S(1)} collective-permute-done((f32[144,128]{1,0:T(8,128)S(1)}, f32[144,128]{1,0:T(8,128)S(1)}, u32[]{:S(2)}, u32[]{:S(2)}) %collective-permute-start.1) | collective-permute-done | bytes 73760 | tf_op jit(solution)/shard_map/ppermute | solution.py:579
  12.0 0.2 shard_map.59
  12.2 2.2 %collective-permute-start.4 = (f32[288,128]{1,0:T(8,128)S(1)}, f32[288,128]{1,0:T(8,128)S(1)}, u32[]{:S(2)}, u32[]{:S(2)}) collective-permute-start(f32[288,128]{1,0:T(8,128)S(1)} %get-tuple-element.34.pack_ref), channel_id=1, source_target_pairs={{0,1},{1,0},{2,3},{3,2},{4,5},{5,4},{6,7},{7,6},{8,9},{9,8},{10,11... | collective-permute-start | bytes 442376 | tf_op jit(solution)/shard_map/ppermute | solution.py:579
  14.4 3.8 %collective-permute-start.2 = (f32[288,128]{1,0:T(8,128)S(1)}, f32[288,128]{1,0:T(8,128)S(1)}, u32[]{:S(2)}, u32[]{:S(2)}) collective-permute-start(f32[288,128]{1,0:T(8,128)S(1)} %get-tuple-element.38), channel_id=1, source_target_pairs={{1,2},{2,1},{5,6},{6,5},{9,10},{10,9},{13,14},{14,13},{17,18},{18,... | collective-permute-start | bytes 442376 | tf_op jit(solution)/shard_map/ppermute | solution.py:579
  18.2 0.3 %shard_map.61 = f32[32,128]{1,0:T(8,128)S(1)} custom-call(s32[6,256]{1,0:T(8,128)S(1)} %copy-done, f32[288,128]{1,0:T(8,128)S(1)} %get-tuple-element.34.pack_ref, f32[192,128]{1,0:T(8,128)S(1)} %get-tuple-element.36.band_ref), custom_call_target="tpu_custom_call" | custom-call | bytes 251904 | tf_op jit(solution)/shard_map/pallas_call | solution.py:586
  18.5 10.1 %collective-permute-start.3 = (f32[32,128]{1,0:T(8,128)S(1)}, f32[32,128]{1,0:T(8,128)S(1)}, u32[]{:S(2)}, u32[]{:S(2)}) collective-permute-start(f32[32,128]{1,0:T(8,128)S(1)} %shard_map.61), channel_id=1, source_target_pairs={{0,4},{4,0},{8,12},{12,8},{16,20},{20,16},{24,28},{28,24},{32,36},... | collective-permute-start | bytes 49160 | tf_op jit(solution)/shard_map/ppermute | solution.py:579
  28.6 0.5 %shard_map.60 = (f32[256,128]{1,0:T(8,128)S(1)}, f32[128,128]{1,0:T(8,128)S(1)}) custom-call(s32[6,256]{1,0:T(8,128)S(1)} %copy-done, f32[288,128]{1,0:T(8,128)S(1)} %get-tuple-element.34.pack_ref, f32[128,128]{1,0:T(8,128)S(1)} %get-tuple-element.35.coef_ref, f32[192,128]{1,0:T(8,128)S(1)} %get-tuple-element.36.band_ref, ...), custom_call_target="tpu_custom_call" | custom-call | bytes 464896 | tf_op jit(solution)/shard_map/pallas_call | solution.py:586
  29.1 0.0 collective-permute-done.4.side_ref
  29.1 0.2 shard_map.62
  29.3 0.1 collective-permute-done.3.sum_near
  29.4 0.0 collective-permute-done.2.side_ref
  29.4 1.2 %shard_map.63 = f32[2,64,256]{2,1,0:T(8,128)} custom-call(s32[6,256]{1,0:T(8,128)S(1)} %copy-done, f32[288,128]{1,0:T(8,128)S(1)} %get-tuple-element.34.pack_ref, f32[128,128]{1,0:T(8,128)S(1)} %get-tuple-element.35.coef_ref, f32[192,128]{1,0:T(8,128)S(1)} %get-tuple-element.36.band_ref, f32[256,128]{1,0:T(8,128)S(1)} %get-tuple-element.37.half_ref, ...), custom_call_target="tpu_custom_call" | custom-call | bytes 841728 | tf_op jit(solution)/shard_map/pallas_call | solution.py:586
Async XLA Ops:
  1.8 3.5 %collective-permute-start = (f32[104,128]{1,0:T(8,128)S(1)}, f32[104,128]{1,0:T(8,128)S(1)}, u32[]{:S(2)}, u32[]{:S(2)}) collective-permute-start(f32[104,128]{1,0:T(8,128)S(1)} %get-tuple-element.25.kept_ref), channel_id=1, source_target_pairs={{0,4},{4,0},{8,12},{12,8},{16,20},{20,16},{24,28},{28,24},{32,36},... | collective-permute-start | bytes 159752 | tf_op jit(solution)/shard_map/ppermute | solution.py:579
  4.4 0.9 %copy-start = (s32[6,256]{1,0:T(8,128)S(1)}, s32[6,256]{1,0:T(8,128)}, u32[]{:S(2)}) copy-start(s32[6,256]{1,0:T(8,128)} %pattern_ref.9) | copy-start | bytes 18436
  5.8 6.3 %collective-permute-start.1 = (f32[144,128]{1,0:T(8,128)S(1)}, f32[144,128]{1,0:T(8,128)S(1)}, u32[]{:S(2)}, u32[]{:S(2)}) collective-permute-start(f32[144,128]{1,0:T(8,128)S(1)} %get-tuple-element.29.kept_ref), channel_id=1, source_target_pairs={{4,8},{8,4},{12,16},{16,12},{20,24},{24,20},{28,32},{32,28},{36,40... | collective-permute-start | bytes 221192 | tf_op jit(solution)/shard_map/ppermute | solution.py:579
  12.2 16.9 %collective-permute-start.4 = (f32[288,128]{1,0:T(8,128)S(1)}, f32[288,128]{1,0:T(8,128)S(1)}, u32[]{:S(2)}, u32[]{:S(2)}) collective-permute-start(f32[288,128]{1,0:T(8,128)S(1)} %get-tuple-element.34.pack_ref), channel_id=1, source_target_pairs={{0,1},{1,0},{2,3},{3,2},{4,5},{5,4},{6,7},{7,6},{8,9},{9,8},{10,11... | collective-permute-start | bytes 442376 | tf_op jit(solution)/shard_map/ppermute | solution.py:579
  14.4 15.0 %collective-permute-start.2 = (f32[288,128]{1,0:T(8,128)S(1)}, f32[288,128]{1,0:T(8,128)S(1)}, u32[]{:S(2)}, u32[]{:S(2)}) collective-permute-start(f32[288,128]{1,0:T(8,128)S(1)} %get-tuple-element.38), channel_id=1, source_target_pairs={{1,2},{2,1},{5,6},{6,5},{9,10},{10,9},{13,14},{14,13},{17,18},{18,... | collective-permute-start | bytes 442376 | tf_op jit(solution)/shard_map/ppermute | solution.py:579
  18.5 10.9 %collective-permute-start.3 = (f32[32,128]{1,0:T(8,128)S(1)}, f32[32,128]{1,0:T(8,128)S(1)}, u32[]{:S(2)}, u32[]{:S(2)}) collective-permute-start(f32[32,128]{1,0:T(8,128)S(1)} %shard_map.61), channel_id=1, source_target_pairs={{0,4},{4,0},{8,12},{12,8},{16,20},{20,16},{24,28},{28,24},{32,36},... | collective-permute-start | bytes 49160 | tf_op jit(solution)/shard_map/ppermute | solution.py:579
